TPU v7x, 32 devices: a whole 2x2x4 slice. The times are simulated.
32 devices in a mesh: ctx: 8 (over y, x, core), tp: 4 (over z).
Axes of the slice: x: 2, y: 2, z: 4, core: 2. Of those that a mesh axis runs over, the one named last changes fastest.
Arguments:
- queries: bfloat16 [2048, 4096], P('ctx', 'tp'), may hold values from -6 to 6
- keys: bfloat16 [2048, 512], P('ctx'), may hold values from -6 to 6
- values: bfloat16 [2048, 512], P('ctx'), may hold values from -6 to 6
- out_weight: bfloat16 [4096, 8192], P('tp'), may hold values from -0.125 to 0.125
- storm_mask: int32 [16, 16], replicated, may hold values from 0 to 1, as said below
Outputs:
- mixed: bfloat16 [2048, 8192], P('ctx', 'tp')
Inputs may be any that keep to these rules, and one draw needn't show every extreme that they name: storm_mask[i, j] is 0 where j > i and 1 where 0 <= i - j < 4.
All inputs are finite; a program needn't handle non-finite values.
Results may differ from a plain program's by a relative error of at most 0.019.
Values may be sent and summed in bfloat16 or wider, within the bound.
No kernel may reach another device: no remote copies, remote signals or barrier semaphores. Data moves between devices by JAX's collectives and lax.ppermute only.
A program may use at most 64 MiB of HBM per device.

v0:
```python
import jax
import jax.numpy as jnp
from jax import lax
from jax.sharding import PartitionSpec as P

HDIM = 128
BLOCK = 128
GQ = 8


def rows_of_mask(index_of_block, storm_mask):
    blocks = storm_mask.shape[0]
    one_hot = (index_of_block[:, None] == jnp.arange(blocks)[None, :]).astype(jnp.float32)
    return jnp.dot(one_hot, storm_mask.astype(jnp.float32))


def update(carry, query, keys_part, values_part, first, row_mask):
    count = keys_part.shape[0]
    blocks = row_mask.shape[1]
    block_of = (first + jnp.arange(count)) // BLOCK
    one_hot = (jnp.arange(blocks)[:, None] == block_of[None, :]).astype(jnp.float32)
    allowed = jnp.dot(row_mask, one_hot) > 0.5

    def compute(state):
        maximum, total, running_total = state
        scores = jnp.einsum(
            "qhd,kd->hqk", query, keys_part, preferred_element_type=jnp.float32
        ) * HDIM ** (-0.5)
        scores = jnp.where(allowed[None], scores, -1e30)
        peak = jnp.maximum(maximum, jnp.max(scores, axis=2))
        weights = jnp.where(allowed[None], jnp.exp(scores - peak[:, :, None]), 0.0)
        factor = jnp.exp(maximum - peak)
        total = total * factor + jnp.sum(weights, axis=2)
        running_total = running_total * factor[:, :, None] + jnp.einsum(
            "hqk,kd->hqd",
            weights.astype(jnp.bfloat16),
            values_part,
            preferred_element_type=jnp.float32,
        )
        return (peak, total, running_total)

    return lax.cond(jnp.any(allowed), compute, lambda state: state, carry)


def body(queries, keys, values, out_weight, storm_mask):
    rows, width = queries.shape
    heads = width // HDIM
    place = lax.axis_index("ctx")
    shared_head = lax.axis_index("tp") * heads // GQ
    local_keys = lax.dynamic_slice_in_dim(keys, shared_head * HDIM, HDIM, 1)
    own_values = lax.dynamic_slice_in_dim(values, shared_head * HDIM, HDIM, 1)
    per_device = rows // BLOCK
    owned = place * per_device + jnp.arange(per_device)
    row_mask = jnp.repeat(rows_of_mask(owned, storm_mask), BLOCK, axis=0)
    query = queries.reshape(rows, heads, HDIM)
    initial = (
        jnp.full((heads, rows), -1e30, jnp.float32),
        jnp.zeros((heads, rows), jnp.float32),
        jnp.zeros((heads, rows, HDIM), jnp.float32),
    )
    carry = initial
    keys_part = lax.all_gather(local_keys, "ctx", axis=0, tiled=True)
    values_part = lax.all_gather(own_values, "ctx", axis=0, tiled=True)
    count = keys_part.shape[0]
    stride = 512

    def inner(state, number):
        first = number * stride
        keys_block = lax.dynamic_slice_in_dim(keys_part, first, stride, 0)
        values_block = lax.dynamic_slice_in_dim(values_part, first, stride, 0)
        return (update(state, query, keys_block, values_block, first, row_mask), None)

    carry, unused = lax.scan(inner, carry, jnp.arange(count // stride))
    maximum, total, running_total = carry
    attended = (
        (running_total / total[:, :, None])
        .astype(jnp.bfloat16)
        .transpose(1, 0, 2)
        .reshape(rows, width)
    )
    shares = lax.psum_scatter(
        lax.dot_general(
            out_weight, attended, (((0,), (1,)), ((), ())), preferred_element_type=jnp.float32
        ).astype(jnp.bfloat16),
        "tp",
        scatter_dimension=0,
        tiled=True,
    ).astype(jnp.float32)
    result = shares.T.astype(jnp.bfloat16)
    return result


def solution(mesh):
    placed = (P("ctx", "tp"), P("ctx", None), P("ctx", None), P("tp", None), P())
    return jax.shard_map(
        body, mesh=mesh, in_specs=placed, out_specs=P("ctx", "tp"), check_vma=False
    )
```

profile of v0, /device:TPU:0, one launch (start us, length us, event | category | flops | bytes accessed | tf_op | source)
XLA Modules:
  0.0 154.1 jit_solution(12067931370008065776)
XLA Ops:
  6.5 0.0 copy-start
  6.5 0.0 reduce-scatter.2.cloned.1.call-start
  6.5 0.9 copy-done
  7.5 0.9 constant_dynamic-slice_fusion
  8.4 11.3 %all_gather.7 = bf16[2048,128]{1,0:T(8,128)(2,1)S(1)} all-gather(bf16[256,128]{1,0:T(8,128)(2,1)S(1)} %constant_dynamic-slice_fusion), channel_id=1, replica_groups=mesh['ctx'=8,'tp'=4] {'ctx'}, dimensions={0}, use_global_device_ids=true | all-gather | bytes 589824 | tf_op jit(solution)/shard_map/all_gather | solution.py:63
  19.6 9.8 %all_gather.6 = bf16[2048,128]{1,0:T(8,128)(2,1)S(1)} all-gather(bf16[256,128]{1,0:T(8,128)(2,1)S(1)} %constant_dynamic-slice_fusion.1), channel_id=1, replica_groups=mesh['ctx'=8,'tp'=4] {'ctx'}, dimensions={0}, use_global_device_ids=true | all-gather | bytes 589824 | tf_op jit(solution)/shard_map/all_gather | solution.py:62
  29.5 1.2 copy.8
  30.7 0.3 copy.9
  31.0 0.9 fusion.28
  31.9 0.1 broadcast_in_dim.50
  32.0 14.9 %while.17 = (s32[]{:T(128)}, f32[8,256]{1,0:T(8,128)S(1)}, f32[8,256]{1,0:T(8,128)S(1)}, f32[8,256,128]{2,1,0:T(8,128)S(1)}, s32[4]{0:T(128)S(1)}, /*index=5*/bf...) while((s32[]{:T(128)}, f32[8,256]{1,0:T(8,128)S(1)}, ...), condition=%wide.region_6.7_spmd.clone, body=%wide.region_0.6_spmd.clone.sunk | while | flops 555511808 | bytes 16142713 | solution.py:73
  32.0 0.6 dynamic_slice.49
  33.3 0.9 fusion.41
  34.8 3.5 %conditional.3 = ((f32[8,256]{1,0:T(8,128)S(1)}, f32[8,256]{1,0:T(8,128)S(1)}, f32[8,256,128]{2,1,0:T(8,128)S(1)})) conditional(s32[]{:T(128)} %convert_element_type.48, (f32[8,256]{1,0:T(8,128)S(1)}, f32[8,256]{1,0:T(8,128)S(1)}, f32[8,256,128]{2,1,0:T(8,128)S(1)}) %tuple.55, (pred[256,512]{0,1:T(8,128)(4,1)S(1)}, s32[]{:T(128)}, ...), branch_computations={%region_2.2_spmd, %region_3.5_spmd} | conditional | flops 551030784 | bytes 15990858 | solution.py:42
  34.8 0.8 fusion.2
  35.6 1.0 fusion.4
  36.7 1.6 %fusion.8 = f32[8,256,128]{2,1,0:T(8,128)S(1)} fusion(f32[512,256,8]{1,0,2:T(8,128)S(1)} %get-tuple-element.285, f32[8,256]{1,0:T(8,128)S(1)} %max.5, pred[256,512]{0,1:T(8,128)(4,1)S(1)} %get-tuple-element.207, f32[8,256,128]{2,1,0:T(8,128)S(1)} %get-tuple-element.212, f32[8,256]{1,0:T(8,128)S(1)} %get-tuple-element.283, ...), kind=kOutput, calls=%fused_computation.8 | convolution fusion | flops 274202624 | bytes 6569988 | tf_op jit(solution)/shard_map/while/body/eval_jaxpr/cond/branch_1_fun/hqk,kd->hqd/dot_general | solution.py:34
  38.3 0.6 dynamic_slice.49
  39.6 0.9 fusion.41
  41.2 0.6 dynamic_slice.49
  42.5 1.0 fusion.41
  44.0 0.6 dynamic_slice.49
  45.3 0.9 fusion.41
  46.9 0.3 copy.10
  47.2 0.1 divide_convert_fusion
  47.3 12.1 %fusion.27 = bf16[8192,256]{0,1:T(8,128)(2,1)} fusion(bf16[256,1024]{0,1:T(8,128)(2,1)S(1)} %bitcast.45, bf16[1024,8192]{1,0:T(8,128)(2,1)} %param.12), kind=kOutput, calls=%fused_computation.35 | convolution fusion | flops 4297064448 | bytes 21495808 | tf_op jit(solution)/shard_map/dot_general | solution.py:82
  59.4 0.0 reduce-scatter.2.cloned.1.call-update
  59.4 87.8 %reduce-scatter.2.cloned.1.call-done = bf16[2048,256]{0,1:T(8,128)(2,1)} async-done(((bf16[8192,256]{0,1:T(8,128)(2,1)}), bf16[2048,256]{0,1:T(8,128)(2,1)}) %reduce-scatter.2.cloned.1.call-update) | async-done | bytes 1048592 | tf_op jit(solution)/shard_map/reduce_scatter | solution.py:81
  (19 shorter events, 0.2 us)
Async XLA Ops:
  6.5 1.0 copy-start
  6.5 140.7 %reduce-scatter.2.cloned.1.call-start = ((), (), s32[]{:S(2)}) async-start(), calls=%async_computation.1 | async-start | bytes 5242880 | tf_op jit(solution)/shard_map/reduce_scatter | solution.py:81
Sparse Core Ops, SparseCore 0:
  59.5 87.6 reduce-scatter.1
where the time goes:
time: 154 us
  waiting for transfers between devices  87.8 us (57%)
  blocking collectives  21.1 us (14%)
  matrix products  19.2 us (12%)
  between operations  13.4 us (9%)
  local copies, waits for them, and re-layouts  6.22 us (4%)
  loops' own time  5.09 us (3%)
    reduce_scatter x1, waiting for transfers between devices, body(): lax.psum_scatter(lax.dot_general(out_weight, attended, (((0,), (1,)), (()...  87.8 us
    dot_general x1, matrix products, body(): lax.dot_general(out_weight, attended, (((0,), (1,)), ((), ())), preferred...  12.1 us
    all_gather x1, blocking collectives, body(): values_part = lax.all_gather(own_values, 'ctx', axis=0, tiled=True)  11.3 us
    all_gather x1, blocking collectives, body(): keys_part = lax.all_gather(local_keys, 'ctx', axis=0, tiled=True)  9.82 us
    another operation x1, loops' own time, body(): carry, unused = lax.scan(inner, carry, jnp.arange(count // stride))  4.98 us
    dot_general x4, matrix products, update(): allowed = jnp.dot(row_mask, one_hot) > 0.5  3.79 us
  transfers between devices with their start and end apart: 1, of which 1 were waited for; matrix products, arithmetic and copies ran while one was open for 0% of the time, Pallas kernels for 0%

commit v1 on v0

v1 whole, which is shorter than its diff:
```python
import functools
import math

import jax
import jax.numpy as jnp
from jax import lax
from jax.experimental import pallas as pl
from jax.experimental.pallas import tpu as pltpu
from jax.sharding import PartitionSpec as P

HDIM = 128
BLOCK = 128
GQ = 8
TILE = 512
EXPONENT = HDIM ** (-0.5) * math.log2(math.e)
VMEM_LIMIT = 48 * 1024 * 1024


def pack_kernel(head_ref, keys_ref, values_ref, out_ref):
    out_ref[:, :HDIM] = keys_ref[...]
    out_ref[:, HDIM:] = values_ref[...]


def pack_head(keys, values, head):
    rows = keys.shape[0]
    block = pl.BlockSpec((rows, HDIM), lambda i, head: (0, head[0]))
    return pl.pallas_call(
        pack_kernel,
        grid_spec=pltpu.PrefetchScalarGridSpec(
            num_scalar_prefetch=1,
            grid=(1,),
            in_specs=[block, block],
            out_specs=pl.BlockSpec((rows, 2 * HDIM), lambda i, head: (0, 0)),
        ),
        out_shape=jax.ShapeDtypeStruct((rows, 2 * HDIM), keys.dtype),
        name="pack_head",
    )(head.reshape(1), keys, values)


def attention_kernel(parts, owners_ref, mask_ref, query_ref, *refs):
    kv_refs = refs[:parts]
    out_ref, kv, scores, peak, total, summed, chosen = refs[parts:]
    rows, width = query_ref.shape
    heads = width // HDIM
    per_device = rows // BLOCK
    place = owners_ref[kv.shape[0]]
    at = 0
    for ref in kv_refs:
        count = ref.shape[0]
        kv[at : at + count] = ref[...]
        at += count
    owners = at

    for block in range(per_device):
        row = place * per_device + block
        top = slice(block * BLOCK, (block + 1) * BLOCK)

        def choose(slot, found):
            for part in range(per_device):
                here = mask_ref[row, owners_ref[slot] * per_device + part] == 1
                chosen[found] = slot * per_device + part
                found = found + here.astype(jnp.int32)
            return found

        found = lax.fori_loop(0, owners, choose, jnp.int32(0))
        pairs = (found + 1) // 2

        @pl.when(found % 2 == 1)
        def _():
            chosen[found] = chosen[found - 1]

        def tile(number):
            index = chosen[number]
            slot = index // per_device
            first = pl.multiple_of((index % per_device) * BLOCK, BLOCK)
            return slot, pl.ds(first, BLOCK)

        peak[...] = jnp.full(peak.shape, -1e30, jnp.float32)
        total[...] = jnp.zeros(total.shape, jnp.float32)
        summed[...] = jnp.zeros(summed.shape, jnp.float32)

        def score(pair, carry):
            slot0, rows0 = tile(2 * pair)
            slot1, rows1 = tile(2 * pair + 1)
            keys = jnp.concatenate([kv[slot0, rows0, :HDIM], kv[slot1, rows1, :HDIM]], axis=0)
            for head in range(heads):
                query = query_ref[top, head * HDIM : (head + 1) * HDIM]
                found_scores = lax.dot_general(
                    query, keys, (((1,), (1,)), ((), ())), preferred_element_type=jnp.float32
                )
                scores[pair, head] = found_scores
                peak[head] = jnp.maximum(
                    peak[head], jnp.maximum(found_scores[:, :BLOCK], found_scores[:, BLOCK:])
                )
            return carry

        lax.fori_loop(0, pairs, score, 0)

        @pl.when(found % 2 == 1)
        def _():
            scores[pairs - 1, :, :, BLOCK:] = jnp.full((heads, BLOCK, BLOCK), -1e30, jnp.float32)

        for head in range(heads):
            peak[head] = jnp.broadcast_to(
                jnp.max(peak[head], axis=1, keepdims=True), (BLOCK, BLOCK)
            )

        def weigh(pair, carry):
            slot0, rows0 = tile(2 * pair)
            slot1, rows1 = tile(2 * pair + 1)
            values = jnp.concatenate([kv[slot0, rows0, HDIM:], kv[slot1, rows1, HDIM:]], axis=0)
            for head in range(heads):
                highest = peak[head]
                left = jnp.exp2((scores[pair, head, :, :BLOCK] - highest) * EXPONENT)
                right = jnp.exp2((scores[pair, head, :, BLOCK:] - highest) * EXPONENT)
                total[head] += left + right
                weights = jnp.concatenate([left, right], axis=1).astype(jnp.bfloat16)
                summed[head] += jnp.dot(weights, values, preferred_element_type=jnp.float32)
            return carry

        lax.fori_loop(0, pairs, weigh, 0)

        for head in range(heads):
            norm = jnp.sum(total[head], axis=1, keepdims=True)
            out_ref[top, head * HDIM : (head + 1) * HDIM] = (summed[head] / norm).astype(
                jnp.bfloat16
            )


def attend(query, kv_parts, owners, place, storm_mask):
    rows, width = query.shape
    heads = width // HDIM
    count = owners.shape[0]
    blocks = count * (rows // BLOCK)
    return pl.pallas_call(
        functools.partial(attention_kernel, len(kv_parts)),
        in_specs=[pl.BlockSpec(memory_space=pltpu.SMEM)] * 2
        + [pl.BlockSpec(memory_space=pltpu.VMEM)] * (1 + len(kv_parts)),
        out_specs=pl.BlockSpec(memory_space=pltpu.VMEM),
        out_shape=jax.ShapeDtypeStruct((rows, width), jnp.bfloat16),
        scratch_shapes=[
            pltpu.VMEM((count, rows, 2 * HDIM), jnp.bfloat16),
            pltpu.VMEM(((blocks + 1) // 2, heads, BLOCK, 2 * BLOCK), jnp.float32),
            pltpu.VMEM((heads, BLOCK, BLOCK), jnp.float32),
            pltpu.VMEM((heads, BLOCK, BLOCK), jnp.float32),
            pltpu.VMEM((heads, BLOCK, HDIM), jnp.float32),
            pltpu.SMEM((blocks + 2,), jnp.int32),
        ],
        compiler_params=pltpu.CompilerParams(vmem_limit_bytes=VMEM_LIMIT),
        name="attend",
    )(jnp.append(owners, place).astype(jnp.int32), storm_mask, query, *kv_parts)


def project_kernel(first_ref, attended_ref, weight_ref, out_ref):
    out_ref[...] = jnp.dot(
        attended_ref[...], weight_ref[...], preferred_element_type=jnp.float32
    ).astype(jnp.bfloat16)


def project(attended, out_weight, first, columns):
    rows, depth = attended.shape
    tile = min(TILE, columns)
    return pl.pallas_call(
        project_kernel,
        grid_spec=pltpu.PrefetchScalarGridSpec(
            num_scalar_prefetch=1,
            grid=(columns // tile,),
            in_specs=[
                pl.BlockSpec((rows, depth), lambda i, first: (0, 0)),
                pl.BlockSpec((depth, tile), lambda i, first: (0, first[0] + i)),
            ],
            out_specs=pl.BlockSpec((rows, tile), lambda i, first: (0, i)),
        ),
        out_shape=jax.ShapeDtypeStruct((rows, columns), jnp.bfloat16),
        compiler_params=pltpu.CompilerParams(vmem_limit_bytes=VMEM_LIMIT),
        name="project",
    )((first // tile).astype(jnp.int32).reshape(1), attended, out_weight)


def gather_heads(packed, place, devices):
    if devices != 8:
        everyone = lax.all_gather(packed, "ctx", axis=0, tiled=False)
        order = jnp.arange(devices, dtype=jnp.int32)
        return [everyone], order
    packed = packed[None]

    def swap(array, bits):
        return lax.ppermute(array, "ctx", [(i, i ^ bits) for i in range(devices)])

    near = [packed] + [swap(packed, bits) for bits in (6, 2, 4)]
    other = [swap(array, 1) for array in near]
    order = place ^ jnp.array([0, 6, 2, 4, 1, 7, 3, 5], jnp.int32)
    return near + other, order


def added(*arrays):
    wide = [array.astype(jnp.float32) for array in arrays]
    return functools.reduce(lambda a, b: a + b, wide).astype(jnp.bfloat16)


def line_sum(attended, out_weight):
    place = lax.axis_index("tp")
    quarter = out_weight.shape[1] // 4
    upper = place >= 2
    outer = (place == 0) | (place == 3)
    far_outer = jnp.where(upper, 0, 3) * quarter
    far_inner = jnp.where(upper, 1, 2) * quarter
    near = jnp.where(upper, 5 - place, 1 - place) * quarter
    own = place * quarter

    def inward(array):
        return lax.ppermute(array, "tp", [(0, 1), (3, 2)])

    def across(array):
        return lax.ppermute(array, "tp", [(1, 2), (2, 1)])

    def outward(array):
        return lax.ppermute(array, "tp", [(1, 0), (2, 3)])

    def chunks(first, sizes):
        at = 0
        for size in sizes:
            yield project(attended, out_weight, first + at, size)
            at += size

    half = quarter // 2
    fourth = quarter // 4
    to_outer = []
    for partial in chunks(far_outer, (fourth, fourth, half)):
        to_outer.append(across(added(partial, inward(partial))))
    to_own = []
    for partial in chunks(far_inner, (half, half)):
        to_own.append(across(added(partial, inward(partial))))
    nearby = list(chunks(near, (fourth, fourth, half)))
    direct = [inward(partial) for partial in nearby]
    returned = [outward(added(partial, far)) for partial, far in zip(nearby, to_outer)]
    mine = project(attended, out_weight, own, quarter)
    return added(
        mine,
        jnp.concatenate(direct, axis=1),
        jnp.concatenate(to_own, axis=1),
        jnp.concatenate(returned, axis=1),
    )


def body(mesh, queries, keys, values, out_weight, storm_mask):
    place = lax.axis_index("ctx")
    heads = queries.shape[1] // HDIM
    shared_head = lax.axis_index("tp") * heads // GQ
    packed = pack_head(keys, values, shared_head)
    kv_parts, order = gather_heads(packed, place, mesh.shape["ctx"])
    attended = attend(queries, kv_parts, order, place, storm_mask)
    if mesh.shape["tp"] == 4:
        return line_sum(attended, out_weight)
    partial = project(attended, out_weight, jnp.int32(0), out_weight.shape[1])
    return lax.psum_scatter(partial, "tp", scatter_dimension=1, tiled=True)


def solution(mesh):
    placed = (P("ctx", "tp"), P("ctx", None), P("ctx", None), P("tp", None), P())
    return jax.shard_map(
        functools.partial(body, mesh),
        mesh=mesh,
        in_specs=placed,
        out_specs=P("ctx", "tp"),
        check_vma=False,
    )
```

time: 154 us -> 125 us (0.81)
  starting transfers between devices: 0.01 us -> 28.8 us
  waiting for transfers between devices: 87.8 us -> 61.7 us
  Pallas kernels: 0 us -> 24.1 us
  blocking collectives: 21.1 us -> 0 us
  matrix products: 19.2 us -> 0 us
  between operations: 13.4 us -> 0.43 us
  loops' own time: 5.09 us -> 0 us
  other arithmetic: 1.17 us -> 6.15 us
  local copies, waits for them, and re-layouts: 6.22 us -> 2.65 us
    reduce_scatter x1 -> x0, waiting for transfers between devices: 87.8 us -> none  [body(): lax.psum_scatter(lax.dot_general(out_weight, attended, (((0,), (1,)), (()...]
    ppermute x0 -> x23, waiting for transfers between devices: none -> 61.7 us  [the longest x8 33.7 us: inward(): return lax.ppermute(array, 'tp', [(0, 1), (3, 2)])]
    ppermute x0 -> x23, starting transfers between devices: none -> 28.8 us  [the longest x8 15.8 us: inward(): return lax.ppermute(array, 'tp', [(0, 1), (3, 2)])]
    pallas_call x0 -> x11, Pallas kernels: none -> 24.1 us  [the longest x9 19.2 us: project(): pl.pallas_call(project_kernel, grid_spec=pltpu.PrefetchScalarGridSpec(num...]
    all_gather x2 -> x0, blocking collectives: 21.1 us -> none  [the longest x1 11.3 us: body(): values_part = lax.all_gather(own_values, 'ctx', axis=0, tiled=True)]
    dot_general x8 -> x0, matrix products: 19.2 us -> none  [the longest x1 12.1 us: body(): lax.dot_general(out_weight, attended, (((0,), (1,)), ((), ())), preferred...]
    convert_element_type x1 -> x9, other arithmetic: 0.1 us -> 5.42 us  [added(): return functools.reduce(lambda a, b: a + b, wide).astype(jnp.bfloat16)]
    another operation x5 -> x0, loops' own time: 5.09 us -> none  [the longest x1 4.98 us: body(): carry, unused = lax.scan(inner, carry, jnp.arange(count // stride))]
  transfers between devices with their start and end apart: 1 -> 23, of which waited for: 1 -> 11; matrix products, arithmetic and copies ran while one was open for 0% -> 3% of each run, Pallas kernels for 0% -> 14%
where the time goes in v1:
time: 125 us; the launch traced here: 124 us
  waiting for transfers between devices  61.7 us (49%)
  starting transfers between devices  28.8 us (23%)
  Pallas kernels  24.1 us (19%)
  other arithmetic  6.15 us (5%)
  local copies, waits for them, and re-layouts  2.65 us (2%)
    ppermute x8, waiting for transfers between devices, inward(): return lax.ppermute(array, 'tp', [(0, 1), (3, 2)])  33.7 us
    ppermute x3, waiting for transfers between devices, outward(): return lax.ppermute(array, 'tp', [(1, 0), (2, 3)])  21.5 us
    pallas_call x9, Pallas kernels, project(): pl.pallas_call(project_kernel, grid_spec=pltpu.PrefetchScalarGridSpec(num...  19.2 us
    ppermute x8, starting transfers between devices, inward(): return lax.ppermute(array, 'tp', [(0, 1), (3, 2)])  15.8 us
    ppermute x7, waiting for transfers between devices, swap(): return lax.ppermute(array, 'ctx', [(i, i ^ bits) for i in range(devices)])  6.48 us
    convert_element_type x9, other arithmetic, added(): return functools.reduce(lambda a, b: a + b, wide).astype(jnp.bfloat16)  5.42 us
    ppermute x7, starting transfers between devices, swap(): return lax.ppermute(array, 'ctx', [(i, i ^ bits) for i in range(devices)])  4.98 us
    ppermute x5, starting transfers between devices, across(): return lax.ppermute(array, 'tp', [(1, 2), (2, 1)])  4.19 us
  transfers between devices with their start and end apart: 23, of which 11 were waited for; matrix products, arithmetic and copies ran while one was open for 3% of the time, Pallas kernels for 14%

profile of v1, /device:TPU:0, one launch (start us, length us, event | category | flops | bytes accessed | tf_op | source)
XLA Modules:
  0.0 123.9 jit_solution(6649633845939890143)
XLA Ops:
  0.0 1.6 %pack_head.1 = bf16[256,256]{1,0:T(8,128)(2,1)} custom-call(s32[1]{0:T(128)} %bitcast.2.head_ref, bf16[256,512]{1,0:T(8,128)(2,1)} %keys_ref.1, bf16[256,512]{1,0:T(8,128)(2,1)} %values_ref.1), custom_call_target="tpu_custom_call" | custom-call | tf_op jit(solution)/shard_map/pack_head/pallas_call | solution.py:27
  1.6 3.9 %collective-permute-start = (bf16[1,256,256]{2,1,0:T(8,128)(2,1)}, bf16[1,256,256]{2,1,0:T(8,128)(2,1)S(1)}, u32[]{:S(2)}, u32[]{:S(2)}) collective-permute-start(bf16[1,256,256]{2,1,0:T(8,128)(2,1)} %bitcast.12), channel_id=1, source_target_pairs={{0,24},{4,28},{8,16},{12,20},{16,8},{20,12},{24,0},{28,4},{1,25},{... | collective-permute-start | bytes 393224 | tf_op jit(solution)/shard_map/ppermute | solution.py:188
  5.4 0.5 collective-permute-start.1
  6.0 0.0 collective-permute-start.2
  6.0 0.0 collective-permute-start.3
  6.0 4.0 %collective-permute-done.refs_1_ = bf16[1,256,256]{2,1,0:T(8,128)(2,1)S(1)} collective-permute-done((bf16[1,256,256]{2,1,0:T(8,128)(2,1)}, bf16[1,256,256]{2,1,0:T(8,128)(2,1)S(1)}, u32[]{:S(2)}, u32[]{:S(2)}) %collective-permute-start) | collective-permute-done | bytes 131104 | tf_op jit(solution)/shard_map/ppermute | solution.py:188
  10.0 0.0 collective-permute-start.4
  10.0 2.2 %collective-permute-done.1.refs_2_ = bf16[1,256,256]{2,1,0:T(8,128)(2,1)S(1)} collective-permute-done((bf16[1,256,256]{2,1,0:T(8,128)(2,1)}, bf16[1,256,256]{2,1,0:T(8,128)(2,1)S(1)}, u32[]{:S(2)}, u32[]{:S(2)}) %collective-permute-start.1) | collective-permute-done | bytes 131104 | tf_op jit(solution)/shard_map/ppermute | solution.py:188
  12.2 0.0 collective-permute-start.5
  12.2 0.0 collective-permute-done.2.refs_3_
  12.2 0.5 collective-permute-start.6
  12.7 0.7 broadcast_xor_fusion
  13.4 0.1 pad_add_fusion.owners_ref
  13.5 0.1 collective-permute-done.5.refs_6_
  13.6 0.2 collective-permute-done.6.refs_7_
  13.8 1.0 copy-done
  14.8 0.9 copy-done.1
  15.7 0.7 copy-done.2
  16.4 3.3 %attend.1.attended_ref = bf16[256,1024]{1,0:T(8,128)(2,1)S(1)} custom-call(s32[9]{0:T(128)S(1)} %pad_add_fusion.owners_ref, s32[16,16]{1,0:T(8,128)S(1)} %copy-done.2, bf16[256,1024]{1,0:T(8,128)(2,1)S(1)} %copy-done, bf16[1,256,256]{2,1,0:T(8,128)(2,1)S(1)} %bitcast.16, bf16[1,256,256]{2,1,0:T(8,128)(2,1)S(1)} %collective-permute-done.refs_1_, ...), custom_call_target="tpu_custom_call" | custom-call | tf_op jit(solution)/shard_map/attend/pallas_call | solution.py:135
  19.7 1.7 %project.16 = bf16[256,512]{1,0:T(8,128)(2,1)S(1)} custom-call(s32[1]{0:T(128)} %bitcast.10.first_ref, bf16[256,1024]{1,0:T(8,128)(2,1)S(1)} %attend.1.attended_ref, bf16[1024,8192]{1,0:T(8,128)(2,1)} %weight_ref.17), custom_call_target="tpu_custom_call" | custom-call | tf_op jit(solution)/shard_map/project/pallas_call | solution.py:163
  21.4 3.5 %collective-permute-start.17 = (bf16[256,512]{1,0:T(8,128)(2,1)S(1)}, bf16[256,512]{1,0:T(8,128)(2,1)S(1)}, u32[]{:S(2)}, u32[]{:S(2)}) collective-permute-start(bf16[256,512]{1,0:T(8,128)(2,1)S(1)} %project.16), channel_id=1, source_target_pairs={{0,1},{3,2},{4,5},{7,6},{8,9},{11,10},{12,13},{15,14},{16,17},{19,... | collective-permute-start | bytes 786440 | tf_op jit(solution)/shard_map/ppermute | solution.py:212
  24.9 2.2 %project.17 = bf16[256,1024]{1,0:T(8,128)(2,1)S(1)} custom-call(s32[1]{0:T(128)} %bitcast.11.first_ref, bf16[256,1024]{1,0:T(8,128)(2,1)S(1)} %attend.1.attended_ref, bf16[1024,8192]{1,0:T(8,128)(2,1)} %weight_ref.17), custom_call_target="tpu_custom_call" | custom-call | tf_op jit(solution)/shard_map/project/pallas_call | solution.py:163
  27.1 1.3 %collective-permute-start.20 = (bf16[256,1024]{1,0:T(8,128)(2,1)S(1)}, bf16[256,1024]{1,0:T(8,128)(2,1)S(1)}, u32[]{:S(2)}, u32[]{:S(2)}) collective-permute-start(bf16[256,1024]{1,0:T(8,128)(2,1)S(1)} %project.17), channel_id=1, source_target_pairs={{0,1},{3,2},{4,5},{7,6},{8,9},{11,10},{12,13},{15,14},{16,17},{19,... | collective-permute-start | bytes 1572872 | tf_op jit(solution)/shard_map/ppermute | solution.py:212
  28.4 1.7 %project.15 = bf16[256,512]{1,0:T(8,128)(2,1)S(1)} custom-call(s32[1]{0:T(128)} %bitcast.9.first_ref, bf16[256,1024]{1,0:T(8,128)(2,1)S(1)} %attend.1.attended_ref, bf16[1024,8192]{1,0:T(8,128)(2,1)} %weight_ref.17), custom_call_target="tpu_custom_call" | custom-call | tf_op jit(solution)/shard_map/project/pallas_call | solution.py:163
  30.1 1.3 %collective-permute-start.14 = (bf16[256,512]{1,0:T(8,128)(2,1)S(1)}, bf16[256,512]{1,0:T(8,128)(2,1)S(1)}, u32[]{:S(2)}, u32[]{:S(2)}) collective-permute-start(bf16[256,512]{1,0:T(8,128)(2,1)S(1)} %project.15), channel_id=1, source_target_pairs={{0,1},{3,2},{4,5},{7,6},{8,9},{11,10},{12,13},{15,14},{16,17},{19,... | collective-permute-start | bytes 786440 | tf_op jit(solution)/shard_map/ppermute | solution.py:212
  31.5 2.2 %project.12 = bf16[256,1024]{1,0:T(8,128)(2,1)S(1)} custom-call(s32[1]{0:T(128)} %bitcast.6.first_ref, bf16[256,1024]{1,0:T(8,128)(2,1)S(1)} %attend.1.attended_ref, bf16[1024,8192]{1,0:T(8,128)(2,1)} %weight_ref.17), custom_call_target="tpu_custom_call" | custom-call | tf_op jit(solution)/shard_map/project/pallas_call | solution.py:163
  33.6 1.7 %project.11 = bf16[256,512]{1,0:T(8,128)(2,1)S(1)} custom-call(s32[1]{0:T(128)} %bitcast.5.first_ref, bf16[256,1024]{1,0:T(8,128)(2,1)S(1)} %attend.1.attended_ref, bf16[1024,8192]{1,0:T(8,128)(2,1)} %weight_ref.17), custom_call_target="tpu_custom_call" | custom-call | tf_op jit(solution)/shard_map/project/pallas_call | solution.py:163
  35.3 1.7 %project.10 = bf16[256,512]{1,0:T(8,128)(2,1)S(1)} custom-call(s32[1]{0:T(128)} %bitcast.4.first_ref, bf16[256,1024]{1,0:T(8,128)(2,1)S(1)} %attend.1.attended_ref, bf16[1024,8192]{1,0:T(8,128)(2,1)} %weight_ref.17), custom_call_target="tpu_custom_call" | custom-call | tf_op jit(solution)/shard_map/project/pallas_call | solution.py:163
  37.0 2.2 %project.14 = bf16[256,1024]{1,0:T(8,128)(2,1)S(1)} custom-call(s32[1]{0:T(128)} %bitcast.8.first_ref, bf16[256,1024]{1,0:T(8,128)(2,1)S(1)} %attend.1.attended_ref, bf16[1024,8192]{1,0:T(8,128)(2,1)} %weight_ref.17), custom_call_target="tpu_custom_call" | custom-call | tf_op jit(solution)/shard_map/project/pallas_call | solution.py:163
  39.1 1.3 %collective-permute-start.12 = (bf16[256,1024]{1,0:T(8,128)(2,1)S(1)}, bf16[256,1024]{1,0:T(8,128)(2,1)S(1)}, u32[]{:S(2)}, u32[]{:S(2)}) collective-permute-start(bf16[256,1024]{1,0:T(8,128)(2,1)S(1)} %project.14), channel_id=1, source_target_pairs={{0,1},{3,2},{4,5},{7,6},{8,9},{11,10},{12,13},{15,14},{16,17},{19,... | collective-permute-start | bytes 1572872 | tf_op jit(solution)/shard_map/ppermute | solution.py:212
  40.5 2.2 %project.13 = bf16[256,1024]{1,0:T(8,128)(2,1)S(1)} custom-call(s32[1]{0:T(128)} %bitcast.7.first_ref, bf16[256,1024]{1,0:T(8,128)(2,1)S(1)} %attend.1.attended_ref, bf16[1024,8192]{1,0:T(8,128)(2,1)} %weight_ref.17), custom_call_target="tpu_custom_call" | custom-call | tf_op jit(solution)/shard_map/project/pallas_call | solution.py:163
  42.6 1.3 %collective-permute-start.10 = (bf16[256,1024]{1,0:T(8,128)(2,1)S(1)}, bf16[256,1024]{1,0:T(8,128)(2,1)S(1)}, u32[]{:S(2)}, u32[]{:S(2)}) collective-permute-start(bf16[256,1024]{1,0:T(8,128)(2,1)S(1)} %project.13), channel_id=1, source_target_pairs={{0,1},{3,2},{4,5},{7,6},{8,9},{11,10},{12,13},{15,14},{16,17},{19,... | collective-permute-start | bytes 1572872 | tf_op jit(solution)/shard_map/ppermute | solution.py:212
  44.0 0.0 collective-permute-done.17
  44.0 1.3 %collective-permute-start.9 = (bf16[256,1024]{1,0:T(8,128)(2,1)S(1)}, bf16[256,1024]{1,0:T(8,128)(2,1)S(1)}, u32[]{:S(2)}, u32[]{:S(2)}) collective-permute-start(bf16[256,1024]{1,0:T(8,128)(2,1)S(1)} %project.12), channel_id=1, source_target_pairs={{0,1},{3,2},{4,5},{7,6},{8,9},{11,10},{12,13},{15,14},{16,17},{19,... | collective-permute-start | bytes 1572872 | tf_op jit(solution)/shard_map/ppermute | solution.py:212
  45.3 0.1 add_convert_fusion.6
  45.4 2.5 %collective-permute-done.14 = bf16[256,512]{1,0:T(8,128)(2,1)S(1)} collective-permute-done((bf16[256,512]{1,0:T(8,128)(2,1)S(1)}, bf16[256,512]{1,0:T(8,128)(2,1)S(1)}, u32[]{:S(2)}, u32[]{:S(2)}) %collective-permute-start.14) | collective-permute-done | bytes 262176 | tf_op jit(solution)/shard_map/ppermute | solution.py:212
  47.8 4.4 %collective-permute-start.8 = (bf16[256,512]{1,0:T(8,128)(2,1)S(1)}, bf16[256,512]{1,0:T(8,128)(2,1)S(1)}, u32[]{:S(2)}, u32[]{:S(2)}) collective-permute-start(bf16[256,512]{1,0:T(8,128)(2,1)S(1)} %project.11), channel_id=1, source_target_pairs={{0,1},{3,2},{4,5},{7,6},{8,9},{11,10},{12,13},{15,14},{16,17},{19,... | collective-permute-start | bytes 786440 | tf_op jit(solution)/shard_map/ppermute | solution.py:212
  52.2 0.1 add_convert_fusion.8
  52.3 0.0 collective-permute-done.20
  52.3 1.3 %collective-permute-start.7 = (bf16[256,512]{1,0:T(8,128)(2,1)S(1)}, bf16[256,512]{1,0:T(8,128)(2,1)S(1)}, u32[]{:S(2)}, u32[]{:S(2)}) collective-permute-start(bf16[256,512]{1,0:T(8,128)(2,1)S(1)} %project.10), channel_id=1, source_target_pairs={{0,1},{3,2},{4,5},{7,6},{8,9},{11,10},{12,13},{15,14},{16,17},{19,... | collective-permute-start | bytes 786440 | tf_op jit(solution)/shard_map/ppermute | solution.py:212
  53.6 0.2 add_convert_fusion.2
  53.8 5.2 %collective-permute-done.12 = bf16[256,1024]{1,0:T(8,128)(2,1)S(1)} collective-permute-done((bf16[256,1024]{1,0:T(8,128)(2,1)S(1)}, bf16[256,1024]{1,0:T(8,128)(2,1)S(1)}, u32[]{:S(2)}, u32[]{:S(2)}) %collective-permute-start.12) | collective-permute-done | bytes 524320 | tf_op jit(solution)/shard_map/ppermute | solution.py:212
  59.1 0.7 collective-permute-start.21
  59.8 0.2 add_convert_fusion.3
  60.0 10.3 %collective-permute-done.10 = bf16[256,1024]{1,0:T(8,128)(2,1)S(1)} collective-permute-done((bf16[256,1024]{1,0:T(8,128)(2,1)S(1)}, bf16[256,1024]{1,0:T(8,128)(2,1)S(1)}, u32[]{:S(2)}, u32[]{:S(2)}) %collective-permute-start.10) | collective-permute-done | bytes 524320 | tf_op jit(solution)/shard_map/ppermute | solution.py:212
  70.3 0.7 collective-permute-start.18
  71.0 0.2 add_convert_fusion.4
  71.2 0.7 collective-permute-start.15
  71.9 0.2 add_convert_fusion.1
  72.1 15.1 %collective-permute-done.8 = bf16[256,512]{1,0:T(8,128)(2,1)S(1)} collective-permute-done((bf16[256,512]{1,0:T(8,128)(2,1)S(1)}, bf16[256,512]{1,0:T(8,128)(2,1)S(1)}, u32[]{:S(2)}, u32[]{:S(2)}) %collective-permute-start.8) | collective-permute-done | bytes 262176 | tf_op jit(solution)/shard_map/ppermute | solution.py:212
  87.2 0.7 collective-permute-start.13
  87.8 0.0 collective-permute-done.18
  87.9 1.5 %collective-permute-start.11 = (bf16[256,1024]{1,0:T(8,128)(2,1)S(1)}, bf16[256,1024]{1,0:T(8,128)(2,1)}, u32[]{:S(2)}, u32[]{:S(2)}) collective-permute-start(bf16[256,1024]{1,0:T(8,128)(2,1)S(1)} %add_convert_fusion.4), channel_id=1, source_target_pairs={{1,2},{2,1},{5,6},{6,5},{9,10},{10,9},{13,14},{14,13},{17,18},{18,... | collective-permute-start | bytes 1572872 | tf_op jit(solution)/shard_map/ppermute | solution.py:215
  89.3 1.3 %collective-permute-start.22 = (bf16[256,1024]{1,0:T(8,128)(2,1)S(1)}, bf16[256,1024]{1,0:T(8,128)(2,1)}, u32[]{:S(2)}, u32[]{:S(2)}) collective-permute-start(bf16[256,1024]{1,0:T(8,128)(2,1)S(1)} %add_convert_fusion.1), channel_id=1, source_target_pairs={{1,0},{2,3},{5,4},{6,7},{9,8},{10,11},{13,12},{14,15},{17,16},{18,... | collective-permute-start | bytes 1572872 | tf_op jit(solution)/shard_map/ppermute | solution.py:218
  90.6 0.8 add_convert_fusion.5
  91.4 0.8 add_convert_fusion.7
  92.2 0.6 collective-permute-done.7
  92.8 1.3 %collective-permute-start.19 = (bf16[256,512]{1,0:T(8,128)(2,1)}, bf16[256,512]{1,0:T(8,128)(2,1)}, u32[]{:S(2)}, u32[]{:S(2)}) collective-permute-start(bf16[256,512]{1,0:T(8,128)(2,1)} %add_convert_fusion.5), channel_id=1, source_target_pairs={{1,0},{2,3},{5,4},{6,7},{9,8},{10,11},{13,12},{14,15},{17,16},{18,... | collective-permute-start | bytes 786440 | tf_op jit(solution)/shard_map/ppermute | solution.py:218
  94.1 1.3 %collective-permute-start.16 = (bf16[256,512]{1,0:T(8,128)(2,1)}, bf16[256,512]{1,0:T(8,128)(2,1)}, u32[]{:S(2)}, u32[]{:S(2)}) collective-permute-start(bf16[256,512]{1,0:T(8,128)(2,1)} %add_convert_fusion.7), channel_id=1, source_target_pairs={{1,0},{2,3},{5,4},{6,7},{9,8},{10,11},{13,12},{14,15},{17,16},{18,... | collective-permute-start | bytes 786440 | tf_op jit(solution)/shard_map/ppermute | solution.py:218
  95.4 0.0 copy-start.4
  95.4 3.9 %project.9 = bf16[256,2048]{1,0:T(8,128)(2,1)S(1)} custom-call(s32[1]{0:T(128)} %bitcast.first_ref, bf16[256,1024]{1,0:T(8,128)(2,1)S(1)} %attend.1.attended_ref, bf16[1024,8192]{1,0:T(8,128)(2,1)} %weight_ref.17), custom_call_target="tpu_custom_call" | custom-call | tf_op jit(solution)/shard_map/project/pallas_call | solution.py:163
  99.4 15.9 %collective-permute-done.19 = bf16[256,512]{1,0:T(8,128)(2,1)} collective-permute-done((bf16[256,512]{1,0:T(8,128)(2,1)}, bf16[256,512]{1,0:T(8,128)(2,1)}, u32[]{:S(2)}, u32[]{:S(2)}) %collective-permute-start.19) | collective-permute-done | bytes 262176 | tf_op jit(solution)/shard_map/ppermute | solution.py:218
  115.3 5.6 %collective-permute-done.16 = bf16[256,512]{1,0:T(8,128)(2,1)} collective-permute-done((bf16[256,512]{1,0:T(8,128)(2,1)}, bf16[256,512]{1,0:T(8,128)(2,1)}, u32[]{:S(2)}, u32[]{:S(2)}) %collective-permute-start.16) | collective-permute-done | bytes 262176 | tf_op jit(solution)/shard_map/ppermute | solution.py:218
  120.9 3.0 %add_convert_fusion = bf16[256,2048]{1,0:T(8,128)(2,1)} fusion(bf16[256,2048]{1,0:T(8,128)(2,1)S(1)} %project.9, bf16[256,1024]{1,0:T(8,128)(2,1)S(1)} %collective-permute-done.9, bf16[256,512]{1,0:T(8,128)(2,1)S(1)} %collective-permute-done.8, bf16[256,512]{1,0:T(8,128)(2,1)S(1)} %copy-done.4, bf16[256,1024]{1,0:T(8,128)(2,1)S(1)} %collective-permute-done.13, ...), kind=kLoop, calls=%fused_computation | loop fusion | flops 11010048 | bytes 5242880 | tf_op jit(solution)/shard_map/convert_element_type | solution.py:198
  (14 shorter events, 0.0 us)
Async XLA Ops:
  1.6 8.4 %collective-permute-start = (bf16[1,256,256]{2,1,0:T(8,128)(2,1)}, bf16[1,256,256]{2,1,0:T(8,128)(2,1)S(1)}, u32[]{:S(2)}, u32[]{:S(2)}) collective-permute-start(bf16[1,256,256]{2,1,0:T(8,128)(2,1)} %bitcast.12), channel_id=1, source_target_pairs={{0,24},{4,28},{8,16},{12,20},{16,8},{20,12},{24,0},{28,4},{1,25},{... | collective-permute-start | bytes 393224 | tf_op jit(solution)/shard_map/ppermute | solution.py:188
  5.4 6.8 %collective-permute-start.1 = (bf16[1,256,256]{2,1,0:T(8,128)(2,1)}, bf16[1,256,256]{2,1,0:T(8,128)(2,1)S(1)}, u32[]{:S(2)}, u32[]{:S(2)}) collective-permute-start(bf16[1,256,256]{2,1,0:T(8,128)(2,1)} %bitcast.13), channel_id=1, source_target_pairs={{0,8},{4,12},{8,0},{12,4},{16,24},{20,28},{24,16},{28,20},{1,9},{5... | collective-permute-start | bytes 393224 | tf_op jit(solution)/shard_map/ppermute | solution.py:188
  6.0 6.2 %collective-permute-start.2 = (bf16[1,256,256]{2,1,0:T(8,128)(2,1)}, bf16[1,256,256]{2,1,0:T(8,128)(2,1)S(1)}, u32[]{:S(2)}, u32[]{:S(2)}) collective-permute-start(bf16[1,256,256]{2,1,0:T(8,128)(2,1)} %bitcast.14), channel_id=1, source_target_pairs={{0,16},{4,20},{8,24},{12,28},{16,0},{20,4},{24,8},{28,12},{1,17},{... | collective-permute-start | bytes 393224 | tf_op jit(solution)/shard_map/ppermute | solution.py:188
  6.0 7.5 %collective-permute-start.3 = (bf16[1,256,256]{2,1,0:T(8,128)(2,1)}, bf16[1,256,256]{2,1,0:T(8,128)(2,1)S(1)}, u32[]{:S(2)}, u32[]{:S(2)}) collective-permute-start(bf16[1,256,256]{2,1,0:T(8,128)(2,1)} %bitcast.15), channel_id=1, source_target_pairs={{0,4},{4,0},{8,12},{12,8},{16,20},{20,16},{24,28},{28,24},{1,5},{5... | collective-permute-start | bytes 393224 | tf_op jit(solution)/shard_map/ppermute | solution.py:188
  10.0 3.5 %collective-permute-start.4 = (bf16[1,256,256]{2,1,0:T(8,128)(2,1)S(1)}, bf16[1,256,256]{2,1,0:T(8,128)(2,1)S(1)}, u32[]{:S(2)}, u32[]{:S(2)}) collective-permute-start(bf16[1,256,256]{2,1,0:T(8,128)(2,1)S(1)} %collective-permute-done.refs_1_), channel_id=1, source_target_pairs={{0,4},{4,0},{8,12},{12,8},{16,20},{20,16},{24,28},{28,24},{1,5},{5... | collective-permute-start | bytes 393224 | tf_op jit(solution)/shard_map/ppermute | solution.py:188
  12.2 1.3 %collective-permute-start.5 = (bf16[1,256,256]{2,1,0:T(8,128)(2,1)S(1)}, bf16[1,256,256]{2,1,0:T(8,128)(2,1)S(1)}, u32[]{:S(2)}, u32[]{:S(2)}) collective-permute-start(bf16[1,256,256]{2,1,0:T(8,128)(2,1)S(1)} %collective-permute-done.1.refs_2_), channel_id=1, source_target_pairs={{0,4},{4,0},{8,12},{12,8},{16,20},{20,16},{24,28},{28,24},{1,5},{5... | collective-permute-start | bytes 393224 | tf_op jit(solution)/shard_map/ppermute | solution.py:188
  12.2 1.5 %collective-permute-start.6 = (bf16[1,256,256]{2,1,0:T(8,128)(2,1)S(1)}, bf16[1,256,256]{2,1,0:T(8,128)(2,1)S(1)}, u32[]{:S(2)}, u32[]{:S(2)}) collective-permute-start(bf16[1,256,256]{2,1,0:T(8,128)(2,1)S(1)} %collective-permute-done.2.refs_3_), channel_id=1, source_target_pairs={{0,4},{4,0},{8,12},{12,8},{16,20},{20,16},{24,28},{28,24},{1,5},{5... | collective-permute-start | bytes 393224 | tf_op jit(solution)/shard_map/ppermute | solution.py:188
  13.7 1.0 copy-start
  14.8 0.9 copy-start.1
  15.7 0.7 copy-start.2
  21.4 22.5 %collective-permute-start.17 = (bf16[256,512]{1,0:T(8,128)(2,1)S(1)}, bf16[256,512]{1,0:T(8,128)(2,1)S(1)}, u32[]{:S(2)}, u32[]{:S(2)}) collective-permute-start(bf16[256,512]{1,0:T(8,128)(2,1)S(1)} %project.16), channel_id=1, source_target_pairs={{0,1},{3,2},{4,5},{7,6},{8,9},{11,10},{12,13},{15,14},{16,17},{19,... | collective-permute-start | bytes 786440 | tf_op jit(solution)/shard_map/ppermute | solution.py:212
  27.1 25.2 %collective-permute-start.20 = (bf16[256,1024]{1,0:T(8,128)(2,1)S(1)}, bf16[256,1024]{1,0:T(8,128)(2,1)S(1)}, u32[]{:S(2)}, u32[]{:S(2)}) collective-permute-start(bf16[256,1024]{1,0:T(8,128)(2,1)S(1)} %project.17), channel_id=1, source_target_pairs={{0,1},{3,2},{4,5},{7,6},{8,9},{11,10},{12,13},{15,14},{16,17},{19,... | collective-permute-start | bytes 1572872 | tf_op jit(solution)/shard_map/ppermute | solution.py:212
  30.1 17.8 %collective-permute-start.14 = (bf16[256,512]{1,0:T(8,128)(2,1)S(1)}, bf16[256,512]{1,0:T(8,128)(2,1)S(1)}, u32[]{:S(2)}, u32[]{:S(2)}) collective-permute-start(bf16[256,512]{1,0:T(8,128)(2,1)S(1)} %project.15), channel_id=1, source_target_pairs={{0,1},{3,2},{4,5},{7,6},{8,9},{11,10},{12,13},{15,14},{16,17},{19,... | collective-permute-start | bytes 786440 | tf_op jit(solution)/shard_map/ppermute | solution.py:212
  39.1 19.9 %collective-permute-start.12 = (bf16[256,1024]{1,0:T(8,128)(2,1)S(1)}, bf16[256,1024]{1,0:T(8,128)(2,1)S(1)}, u32[]{:S(2)}, u32[]{:S(2)}) collective-permute-start(bf16[256,1024]{1,0:T(8,128)(2,1)S(1)} %project.14), channel_id=1, source_target_pairs={{0,1},{3,2},{4,5},{7,6},{8,9},{11,10},{12,13},{15,14},{16,17},{19,... | collective-permute-start | bytes 1572872 | tf_op jit(solution)/shard_map/ppermute | solution.py:212
  42.6 27.7 %collective-permute-start.10 = (bf16[256,1024]{1,0:T(8,128)(2,1)S(1)}, bf16[256,1024]{1,0:T(8,128)(2,1)S(1)}, u32[]{:S(2)}, u32[]{:S(2)}) collective-permute-start(bf16[256,1024]{1,0:T(8,128)(2,1)S(1)} %project.13), channel_id=1, source_target_pairs={{0,1},{3,2},{4,5},{7,6},{8,9},{11,10},{12,13},{15,14},{16,17},{19,... | collective-permute-start | bytes 1572872 | tf_op jit(solution)/shard_map/ppermute | solution.py:212
  44.0 50.1 %collective-permute-start.9 = (bf16[256,1024]{1,0:T(8,128)(2,1)S(1)}, bf16[256,1024]{1,0:T(8,128)(2,1)S(1)}, u32[]{:S(2)}, u32[]{:S(2)}) collective-permute-start(bf16[256,1024]{1,0:T(8,128)(2,1)S(1)} %project.12), channel_id=1, source_target_pairs={{0,1},{3,2},{4,5},{7,6},{8,9},{11,10},{12,13},{15,14},{16,17},{19,... | collective-permute-start | bytes 1572872 | tf_op jit(solution)/shard_map/ppermute | solution.py:212
  47.8 39.3 %collective-permute-start.8 = (bf16[256,512]{1,0:T(8,128)(2,1)S(1)}, bf16[256,512]{1,0:T(8,128)(2,1)S(1)}, u32[]{:S(2)}, u32[]{:S(2)}) collective-permute-start(bf16[256,512]{1,0:T(8,128)(2,1)S(1)} %project.11), channel_id=1, source_target_pairs={{0,1},{3,2},{4,5},{7,6},{8,9},{11,10},{12,13},{15,14},{16,17},{19,... | collective-permute-start | bytes 786440 | tf_op jit(solution)/shard_map/ppermute | solution.py:212
  52.3 40.5 %collective-permute-start.7 = (bf16[256,512]{1,0:T(8,128)(2,1)S(1)}, bf16[256,512]{1,0:T(8,128)(2,1)S(1)}, u32[]{:S(2)}, u32[]{:S(2)}) collective-permute-start(bf16[256,512]{1,0:T(8,128)(2,1)S(1)} %project.10), channel_id=1, source_target_pairs={{0,1},{3,2},{4,5},{7,6},{8,9},{11,10},{12,13},{15,14},{16,17},{19,... | collective-permute-start | bytes 786440 | tf_op jit(solution)/shard_map/ppermute | solution.py:212
  59.1 12.1 %collective-permute-start.21 = (bf16[256,1024]{1,0:T(8,128)(2,1)S(1)}, bf16[256,1024]{1,0:T(8,128)(2,1)S(1)}, u32[]{:S(2)}, u32[]{:S(2)}) collective-permute-start(bf16[256,1024]{1,0:T(8,128)(2,1)S(1)} %add_convert_fusion.2), channel_id=1, source_target_pairs={{1,2},{2,1},{5,6},{6,5},{9,10},{10,9},{13,14},{14,13},{17,18},{18,... | collective-permute-start | bytes 1572872 | tf_op jit(solution)/shard_map/ppermute | solution.py:215
  70.3 17.5 %collective-permute-start.18 = (bf16[256,512]{1,0:T(8,128)(2,1)S(1)}, bf16[256,512]{1,0:T(8,128)(2,1)S(1)}, u32[]{:S(2)}, u32[]{:S(2)}) collective-permute-start(bf16[256,512]{1,0:T(8,128)(2,1)S(1)} %add_convert_fusion.6), channel_id=1, source_target_pairs={{1,2},{2,1},{5,6},{6,5},{9,10},{10,9},{13,14},{14,13},{17,18},{18,... | collective-permute-start | bytes 786440 | tf_op jit(solution)/shard_map/ppermute | solution.py:215
  71.2 18.2 %collective-permute-start.15 = (bf16[256,512]{1,0:T(8,128)(2,1)S(1)}, bf16[256,512]{1,0:T(8,128)(2,1)S(1)}, u32[]{:S(2)}, u32[]{:S(2)}) collective-permute-start(bf16[256,512]{1,0:T(8,128)(2,1)S(1)} %add_convert_fusion.8), channel_id=1, source_target_pairs={{1,2},{2,1},{5,6},{6,5},{9,10},{10,9},{13,14},{14,13},{17,18},{18,... | collective-permute-start | bytes 786440 | tf_op jit(solution)/shard_map/ppermute | solution.py:215
  87.2 33.7 %collective-permute-start.13 = (bf16[256,1024]{1,0:T(8,128)(2,1)S(1)}, bf16[256,1024]{1,0:T(8,128)(2,1)S(1)}, u32[]{:S(2)}, u32[]{:S(2)}) collective-permute-start(bf16[256,1024]{1,0:T(8,128)(2,1)S(1)} %add_convert_fusion.3), channel_id=1, source_target_pairs={{1,2},{2,1},{5,6},{6,5},{9,10},{10,9},{13,14},{14,13},{17,18},{18,... | collective-permute-start | bytes 1572872 | tf_op jit(solution)/shard_map/ppermute | solution.py:215
  87.9 33.0 %collective-permute-start.11 = (bf16[256,1024]{1,0:T(8,128)(2,1)S(1)}, bf16[256,1024]{1,0:T(8,128)(2,1)}, u32[]{:S(2)}, u32[]{:S(2)}) collective-permute-start(bf16[256,1024]{1,0:T(8,128)(2,1)S(1)} %add_convert_fusion.4), channel_id=1, source_target_pairs={{1,2},{2,1},{5,6},{6,5},{9,10},{10,9},{13,14},{14,13},{17,18},{18,... | collective-permute-start | bytes 1572872 | tf_op jit(solution)/shard_map/ppermute | solution.py:215
  89.3 31.5 %collective-permute-start.22 = (bf16[256,1024]{1,0:T(8,128)(2,1)S(1)}, bf16[256,1024]{1,0:T(8,128)(2,1)}, u32[]{:S(2)}, u32[]{:S(2)}) collective-permute-start(bf16[256,1024]{1,0:T(8,128)(2,1)S(1)} %add_convert_fusion.1), channel_id=1, source_target_pairs={{1,0},{2,3},{5,4},{6,7},{9,8},{10,11},{13,12},{14,15},{17,16},{18,... | collective-permute-start | bytes 1572872 | tf_op jit(solution)/shard_map/ppermute | solution.py:218
  92.8 1.3 %copy-start.3 = (bf16[256,512]{1,0:T(8,128)(2,1)}, bf16[256,512]{1,0:T(8,128)(2,1)S(1)}, u32[]{:S(2)}) copy-start(bf16[256,512]{1,0:T(8,128)(2,1)S(1)} %collective-permute-done.7) | copy-start | bytes 786436
  92.8 22.5 %collective-permute-start.19 = (bf16[256,512]{1,0:T(8,128)(2,1)}, bf16[256,512]{1,0:T(8,128)(2,1)}, u32[]{:S(2)}, u32[]{:S(2)}) collective-permute-start(bf16[256,512]{1,0:T(8,128)(2,1)} %add_convert_fusion.5), channel_id=1, source_target_pairs={{1,0},{2,3},{5,4},{6,7},{9,8},{10,11},{13,12},{14,15},{17,16},{18,... | collective-permute-start | bytes 786440 | tf_op jit(solution)/shard_map/ppermute | solution.py:218
  94.1 26.8 %collective-permute-start.16 = (bf16[256,512]{1,0:T(8,128)(2,1)}, bf16[256,512]{1,0:T(8,128)(2,1)}, u32[]{:S(2)}, u32[]{:S(2)}) collective-permute-start(bf16[256,512]{1,0:T(8,128)(2,1)} %add_convert_fusion.7), channel_id=1, source_target_pairs={{1,0},{2,3},{5,4},{6,7},{9,8},{10,11},{13,12},{14,15},{17,16},{18,... | collective-permute-start | bytes 786440 | tf_op jit(solution)/shard_map/ppermute | solution.py:218
  95.4 25.5 %copy-start.4 = (bf16[256,512]{1,0:T(8,128)(2,1)S(1)}, bf16[256,512]{1,0:T(8,128)(2,1)}, u32[]{:S(2)}) copy-start(bf16[256,512]{1,0:T(8,128)(2,1)} %copy-done.3) | copy-start | bytes 786436

commit v2 on v1

--- a/solution.py
+++ b/solution.py
@@ -37,32 +37,45 @@
     )(head.reshape(1), keys, values)
 
 
-def attention_kernel(parts, owners_ref, mask_ref, query_ref, *refs):
+def attention_kernel(parts, swaps, place_ref, mask_ref, query_hbm, own_hbm, *refs):
     kv_refs = refs[:parts]
-    out_ref, kv, scores, peak, total, summed, chosen = refs[parts:]
+    out_ref, query_ref, kv, scores, peak, total, summed, chosen, arrived = refs[parts:]
     rows, width = query_ref.shape
     heads = width // HDIM
     per_device = rows // BLOCK
-    place = owners_ref[kv.shape[0]]
-    at = 0
+    place = place_ref[0]
+    owners = kv.shape[0]
+    loads = [pltpu.make_async_copy(query_hbm, query_ref, arrived.at[0])]
+    if swaps:
+        loads.append(pltpu.make_async_copy(own_hbm, kv.at[0], arrived.at[1]))
+    for load in loads:
+        load.start()
+    at = len(loads) - 1
     for ref in kv_refs:
         count = ref.shape[0]
         kv[at : at + count] = ref[...]
         at += count
-    owners = at
+    for load in loads:
+        load.wait()
 
     for block in range(per_device):
         row = place * per_device + block
         top = slice(block * BLOCK, (block + 1) * BLOCK)
 
         def choose(slot, found):
+            owner = place ^ swaps[slot] if swaps else slot
             for part in range(per_device):
-                here = mask_ref[row, owners_ref[slot] * per_device + part] == 1
+                here = mask_ref[row, owner * per_device + part] == 1
                 chosen[found] = slot * per_device + part
                 found = found + here.astype(jnp.int32)
             return found
 
-        found = lax.fori_loop(0, owners, choose, jnp.int32(0))
+        found = jnp.int32(0)
+        if swaps:
+            for slot in range(owners):
+                found = choose(slot, found)
+        else:
+            found = lax.fori_loop(0, owners, choose, found)
         pairs = (found + 1) // 2
 
         @pl.when(found % 2 == 1)
@@ -127,28 +140,34 @@
             )
 
 
-def attend(query, kv_parts, owners, place, storm_mask):
+def attend(query, own, others, swaps, place, storm_mask):
     rows, width = query.shape
     heads = width // HDIM
-    count = owners.shape[0]
+    count = len(swaps) if swaps else others[0].shape[0]
     blocks = count * (rows // BLOCK)
     return pl.pallas_call(
-        functools.partial(attention_kernel, len(kv_parts)),
-        in_specs=[pl.BlockSpec(memory_space=pltpu.SMEM)] * 2
-        + [pl.BlockSpec(memory_space=pltpu.VMEM)] * (1 + len(kv_parts)),
-        out_specs=pl.BlockSpec(memory_space=pltpu.VMEM),
+        functools.partial(attention_kernel, len(others), swaps),
+        grid_spec=pltpu.PrefetchScalarGridSpec(
+            num_scalar_prefetch=2,
+            grid=(1,),
+            in_specs=[pl.BlockSpec(memory_space=pltpu.HBM)] * 2
+            + [pl.BlockSpec(memory_space=pltpu.VMEM)] * len(others),
+            out_specs=pl.BlockSpec(memory_space=pltpu.VMEM),
+            scratch_shapes=[
+                pltpu.VMEM((rows, width), jnp.bfloat16),
+                pltpu.VMEM((count, rows, 2 * HDIM), jnp.bfloat16),
+                pltpu.VMEM(((blocks + 1) // 2, heads, BLOCK, 2 * BLOCK), jnp.float32),
+                pltpu.VMEM((heads, BLOCK, BLOCK), jnp.float32),
+                pltpu.VMEM((heads, BLOCK, BLOCK), jnp.float32),
+                pltpu.VMEM((heads, BLOCK, HDIM), jnp.float32),
+                pltpu.SMEM((blocks + 2,), jnp.int32),
+                pltpu.SemaphoreType.DMA((2,)),
+            ],
+        ),
         out_shape=jax.ShapeDtypeStruct((rows, width), jnp.bfloat16),
-        scratch_shapes=[
-            pltpu.VMEM((count, rows, 2 * HDIM), jnp.bfloat16),
-            pltpu.VMEM(((blocks + 1) // 2, heads, BLOCK, 2 * BLOCK), jnp.float32),
-            pltpu.VMEM((heads, BLOCK, BLOCK), jnp.float32),
-            pltpu.VMEM((heads, BLOCK, BLOCK), jnp.float32),
-            pltpu.VMEM((heads, BLOCK, HDIM), jnp.float32),
-            pltpu.SMEM((blocks + 2,), jnp.int32),
-        ],
         compiler_params=pltpu.CompilerParams(vmem_limit_bytes=VMEM_LIMIT),
         name="attend",
-    )(jnp.append(owners, place).astype(jnp.int32), storm_mask, query, *kv_parts)
+    )(place.astype(jnp.int32).reshape(1), storm_mask, query, own, *others)
 
 
 def project_kernel(first_ref, attended_ref, weight_ref, out_ref):
@@ -177,20 +196,20 @@
     )((first // tile).astype(jnp.int32).reshape(1), attended, out_weight)
 
 
-def gather_heads(packed, place, devices):
+def gather_heads(packed, devices):
     if devices != 8:
-        everyone = lax.all_gather(packed, "ctx", axis=0, tiled=False)
-        order = jnp.arange(devices, dtype=jnp.int32)
-        return [everyone], order
-    packed = packed[None]
+        return [lax.all_gather(packed, "ctx", axis=0, tiled=False)], ()
 
     def swap(array, bits):
         return lax.ppermute(array, "ctx", [(i, i ^ bits) for i in range(devices)])
 
-    near = [packed] + [swap(packed, bits) for bits in (6, 2, 4)]
+    near = [packed[None]] + [swap(packed[None], bits) for bits in (6, 2, 4)]
     other = [swap(array, 1) for array in near]
-    order = place ^ jnp.array([0, 6, 2, 4, 1, 7, 3, 5], jnp.int32)
-    return near + other, order
+    return near[1:] + other, (0, 6, 2, 4, 1, 7, 3, 5)
+
+
+def after(array, *earlier):
+    return lax.optimization_barrier((array, *earlier))[0]
 
 
 def added(*arrays):
@@ -202,11 +221,25 @@
     place = lax.axis_index("tp")
     quarter = out_weight.shape[1] // 4
     upper = place >= 2
-    outer = (place == 0) | (place == 3)
     far_outer = jnp.where(upper, 0, 3) * quarter
     far_inner = jnp.where(upper, 1, 2) * quarter
     near = jnp.where(upper, 5 - place, 1 - place) * quarter
     own = place * quarter
+    half = quarter // 2
+    fourth = quarter // 4
+    pieces = ((0, fourth), (fourth, fourth), (half, half))
+    halves = ((0, half), (half, half))
+    projected, chain = [], []
+
+    def part(first, columns):
+        source = after(attended, projected[-1]) if projected else attended
+        projected.append(project(source, out_weight, first, columns))
+        return projected[-1]
+
+    def step(*arrays):
+        first = after(arrays[0], chain[-1]) if chain else arrays[0]
+        chain.append(added(first, *arrays[1:]))
+        return chain[-1]
 
     def inward(array):
         return lax.ppermute(array, "tp", [(0, 1), (3, 2)])
@@ -217,30 +250,26 @@
     def outward(array):
         return lax.ppermute(array, "tp", [(1, 0), (2, 3)])
 
-    def chunks(first, sizes):
-        at = 0
-        for size in sizes:
-            yield project(attended, out_weight, first + at, size)
-            at += size
-
-    half = quarter // 2
-    fourth = quarter // 4
-    to_outer = []
-    for partial in chunks(far_outer, (fourth, fourth, half)):
-        to_outer.append(across(added(partial, inward(partial))))
-    to_own = []
-    for partial in chunks(far_inner, (half, half)):
-        to_own.append(across(added(partial, inward(partial))))
-    nearby = list(chunks(near, (fourth, fourth, half)))
-    direct = [inward(partial) for partial in nearby]
-    returned = [outward(added(partial, far)) for partial, far in zip(nearby, to_outer)]
-    mine = project(attended, out_weight, own, quarter)
-    return added(
-        mine,
-        jnp.concatenate(direct, axis=1),
-        jnp.concatenate(to_own, axis=1),
-        jnp.concatenate(returned, axis=1),
-    )
+    outer_parts = [part(far_outer + at, size) for at, size in pieces]
+    outer_sums = [inward(array) for array in outer_parts]
+    inner_parts = [part(far_inner + at, size) for at, size in halves]
+    inner_sums = [inward(array) for array in inner_parts]
+    near_parts = [part(near + at, size) for at, size in halves]
+    direct = [inward(array) for array in near_parts]
+    mine = part(own, quarter)
+    near_pieces = [near_parts[0][:, :fourth], near_parts[0][:, fourth:], near_parts[1]]
+
+    to_outer, to_own, returned = [None] * 3, [None] * 2, [None] * 3
+    for kind, at in (("f", 0), ("f", 1), ("o", 0), ("o", 1), ("f", 2), ("n", 0), ("o", 2), ("n", 1)):
+        if kind == "f":
+            to_outer[at] = across(step(outer_parts[at], outer_sums[at]))
+        elif kind == "o":
+            returned[at] = outward(step(near_pieces[at], to_outer[at]))
+        else:
+            to_own[at] = across(step(inner_parts[at], inner_sums[at]))
+    left = step(mine[:, :half], jnp.concatenate(returned[:2], axis=1), to_own[0], direct[0])
+    right = step(mine[:, half:], returned[2], to_own[1], direct[1])
+    return jnp.concatenate([left, right], axis=1)
 
 
 def body(mesh, queries, keys, values, out_weight, storm_mask):
@@ -248,8 +277,8 @@
     heads = queries.shape[1] // HDIM
     shared_head = lax.axis_index("tp") * heads // GQ
     packed = pack_head(keys, values, shared_head)
-    kv_parts, order = gather_heads(packed, place, mesh.shape["ctx"])
-    attended = attend(queries, kv_parts, order, place, storm_mask)
+    others, swaps = gather_heads(packed, mesh.shape["ctx"])
+    attended = attend(queries, packed, others, swaps, place, storm_mask)
     if mesh.shape["tp"] == 4:
         return line_sum(attended, out_weight)
     partial = project(attended, out_weight, jnp.int32(0), out_weight.shape[1])

time: 125 us -> 104 us (0.83)
  waiting for transfers between devices: 61.7 us -> 35.1 us
  starting transfers between devices: 28.8 us -> 35.4 us
  Pallas kernels: 24.1 us -> 22.8 us
    ppermute x3, waiting for transfers between devices: 21.5 us -> 4.32 us  [outward(): return lax.ppermute(array, 'tp', [(1, 0), (2, 3)])]
    ppermute x8 -> x7, waiting for transfers between devices: 33.7 us -> 23.6 us  [inward(): return lax.ppermute(array, 'tp', [(0, 1), (3, 2)])]
    ppermute x8 -> x7, starting transfers between devices: 15.8 us -> 23.2 us  [inward(): return lax.ppermute(array, 'tp', [(0, 1), (3, 2)])]
    convert_element_type x9 -> x10, other arithmetic: 5.42 us -> 4.18 us  [added(): return functools.reduce(lambda a, b: a + b, wide).astype(jnp.bfloat16)]
    pallas_call x9 -> x8, Pallas kernels: 19.2 us -> 18 us  [project(): pl.pallas_call(project_kernel, grid_spec=pltpu.PrefetchScalarGridSpec(num...]
    unnamed x10 -> x8, local copies, waits for them, and re-layouts: 2.65 us -> 2.65 us
  transfers between devices with their start and end apart: 23 -> 22, of which waited for: 11 -> 10; matrix products, arithmetic and copies ran while one was open for 3% -> 4% of each run, Pallas kernels for 14% -> 16%
where the time goes in v2:
time: 104 us; the launch traced here: 102 us
  starting transfers between devices  35.4 us (34%)
  waiting for transfers between devices  35.1 us (34%)
  Pallas kernels  22.8 us (22%)
  other arithmetic  5.23 us (5%)
  local copies, waits for them, and re-layouts  2.75 us (3%)
    ppermute x7, waiting for transfers between devices, inward(): return lax.ppermute(array, 'tp', [(0, 1), (3, 2)])  23.6 us
    ppermute x7, starting transfers between devices, inward(): return lax.ppermute(array, 'tp', [(0, 1), (3, 2)])  23.2 us
    pallas_call x8, Pallas kernels, project(): pl.pallas_call(project_kernel, grid_spec=pltpu.PrefetchScalarGridSpec(num...  18 us
    ppermute x7, waiting for transfers between devices, swap(): return lax.ppermute(array, 'ctx', [(i, i ^ bits) for i in range(devices)])  7.21 us
    ppermute x7, starting transfers between devices, swap(): return lax.ppermute(array, 'ctx', [(i, i ^ bits) for i in range(devices)])  4.98 us
    ppermute x3, waiting for transfers between devices, outward(): return lax.ppermute(array, 'tp', [(1, 0), (2, 3)])  4.32 us
    convert_element_type x10, other arithmetic, added(): return functools.reduce(lambda a, b: a + b, wide).astype(jnp.bfloat16)  4.18 us
    ppermute x3, starting transfers between devices, outward(): return lax.ppermute(array, 'tp', [(1, 0), (2, 3)])  3.85 us
  transfers between devices with their start and end apart: 22, of which 10 were waited for; matrix products, arithmetic and copies ran while one was open for 4% of the time, Pallas kernels for 16%

profile of v2, /device:TPU:0, one launch (start us, length us, event | category | flops | bytes accessed | tf_op | source)
XLA Modules:
  0.0 101.7 jit_solution(12040677451999492649)
XLA Ops:
  0.0 1.6 %pack_head.1.own_hbm = bf16[256,256]{1,0:T(8,128)(2,1)} custom-call(s32[1]{0:T(128)} %bitcast.2.head_ref, bf16[256,512]{1,0:T(8,128)(2,1)} %keys_ref.1, bf16[256,512]{1,0:T(8,128)(2,1)} %values_ref.1), custom_call_target="tpu_custom_call" | custom-call | tf_op jit(solution)/shard_map/pack_head/pallas_call | solution.py:27
  1.6 3.9 %collective-permute-start = (bf16[1,256,256]{2,1,0:T(8,128)(2,1)}, bf16[1,256,256]{2,1,0:T(8,128)(2,1)S(1)}, u32[]{:S(2)}, u32[]{:S(2)}) collective-permute-start(bf16[1,256,256]{2,1,0:T(8,128)(2,1)} %bitcast.11), channel_id=1, source_target_pairs={{0,24},{4,28},{8,16},{12,20},{16,8},{20,12},{24,0},{28,4},{1,25},{... | collective-permute-start | bytes 393224 | tf_op jit(solution)/shard_map/ppermute | solution.py:204
  5.4 0.5 collective-permute-start.1
  6.0 0.0 collective-permute-start.2
  6.0 0.0 collective-permute-start.3
  6.0 4.0 %collective-permute-done.refs_0_ = bf16[1,256,256]{2,1,0:T(8,128)(2,1)S(1)} collective-permute-done((bf16[1,256,256]{2,1,0:T(8,128)(2,1)}, bf16[1,256,256]{2,1,0:T(8,128)(2,1)S(1)}, u32[]{:S(2)}, u32[]{:S(2)}) %collective-permute-start) | collective-permute-done | bytes 131104 | tf_op jit(solution)/shard_map/ppermute | solution.py:204
  10.0 2.2 %collective-permute-done.1.refs_1_ = bf16[1,256,256]{2,1,0:T(8,128)(2,1)S(1)} collective-permute-done((bf16[1,256,256]{2,1,0:T(8,128)(2,1)}, bf16[1,256,256]{2,1,0:T(8,128)(2,1)S(1)}, u32[]{:S(2)}, u32[]{:S(2)}) %collective-permute-start.1) | collective-permute-done | bytes 131104 | tf_op jit(solution)/shard_map/ppermute | solution.py:204
  12.2 0.5 collective-permute-start.6
  12.7 0.0 collective-permute-done.3.refs_3_
  12.7 0.0 collective-permute-done.4.refs_4_
  12.7 0.8 collective-permute-done.5.refs_5_
  13.6 0.2 collective-permute-done.6.refs_6_
  13.8 1.0 %copy-done = bf16[256,1024]{1,0:T(8,128)(2,1)S(1)} copy-done((bf16[256,1024]{1,0:T(8,128)(2,1)S(1)}, bf16[256,1024]{1,0:T(8,128)(2,1)}, u32[]{:S(2)}) %copy-start) | copy-done | bytes 524312
  14.8 0.9 copy-done.1
  15.7 0.7 copy-done.2
  16.4 3.2 %attend.1.attended_ref = bf16[256,1024]{1,0:T(8,128)(2,1)S(1)} custom-call(s32[1]{0:T(128)} %bitcast.1.place_ref, s32[16,16]{1,0:T(8,128)S(1)} %copy-done.2, bf16[256,1024]{1,0:T(8,128)(2,1)S(1)} %copy-done, bf16[256,256]{1,0:T(8,128)(2,1)S(1)} %copy-done.1, bf16[1,256,256]{2,1,0:T(8,128)(2,1)S(1)} %collective-permute-done.refs_0_, ...), custom_call_target="tpu_custom_call" | custom-call | tf_op jit(solution)/shard_map/attend/pallas_call | solution.py:148
  19.6 1.7 %project.8 = bf16[256,512]{1,0:T(8,128)(2,1)S(1)} custom-call(s32[1]{0:T(128)} %bitcast.10.first_ref, bf16[256,1024]{1,0:T(8,128)(2,1)S(1)} %attend.1.attended_ref, bf16[1024,8192]{1,0:T(8,128)(2,1)} %weight_ref.15), custom_call_target="tpu_custom_call" | custom-call | tf_op jit(solution)/shard_map/project/pallas_call | solution.py:182
  21.3 3.5 %collective-permute-start.7 = (bf16[256,512]{1,0:T(8,128)(2,1)S(1)}, bf16[256,512]{1,0:T(8,128)(2,1)S(1)}, u32[]{:S(2)}, u32[]{:S(2)}) collective-permute-start(bf16[256,512]{1,0:T(8,128)(2,1)S(1)} %project.8), channel_id=1, source_target_pairs={{0,1},{3,2},{4,5},{7,6},{8,9},{11,10},{12,13},{15,14},{16,17},{19,... | collective-permute-start | bytes 786440 | tf_op jit(solution)/shard_map/ppermute | solution.py:245
  24.8 1.7 %project.9 = bf16[256,512]{1,0:T(8,128)(2,1)S(1)} custom-call(s32[1]{0:T(128)} %bitcast.9.first_ref, bf16[256,1024]{1,0:T(8,128)(2,1)S(1)} %attend.1.attended_ref, bf16[1024,8192]{1,0:T(8,128)(2,1)} %weight_ref.15), custom_call_target="tpu_custom_call" | custom-call | tf_op jit(solution)/shard_map/project/pallas_call | solution.py:182
  26.5 2.0 %collective-permute-start.8 = (bf16[256,512]{1,0:T(8,128)(2,1)S(1)}, bf16[256,512]{1,0:T(8,128)(2,1)}, u32[]{:S(2)}, u32[]{:S(2)}) collective-permute-start(bf16[256,512]{1,0:T(8,128)(2,1)S(1)} %project.9), channel_id=1, source_target_pairs={{0,1},{3,2},{4,5},{7,6},{8,9},{11,10},{12,13},{15,14},{16,17},{19,... | collective-permute-start | bytes 786440 | tf_op jit(solution)/shard_map/ppermute | solution.py:245
  28.5 2.1 %project.10 = bf16[256,1024]{1,0:T(8,128)(2,1)S(1)} custom-call(s32[1]{0:T(128)} %bitcast.8.first_ref, bf16[256,1024]{1,0:T(8,128)(2,1)S(1)} %attend.1.attended_ref, bf16[1024,8192]{1,0:T(8,128)(2,1)} %weight_ref.15), custom_call_target="tpu_custom_call" | custom-call | tf_op jit(solution)/shard_map/project/pallas_call | solution.py:182
  30.6 1.3 %collective-permute-start.11 = (bf16[256,1024]{1,0:T(8,128)(2,1)S(1)}, bf16[256,1024]{1,0:T(8,128)(2,1)S(1)}, u32[]{:S(2)}, u32[]{:S(2)}) collective-permute-start(bf16[256,1024]{1,0:T(8,128)(2,1)S(1)} %project.10), channel_id=1, source_target_pairs={{0,1},{3,2},{4,5},{7,6},{8,9},{11,10},{12,13},{15,14},{16,17},{19,... | collective-permute-start | bytes 1572872 | tf_op jit(solution)/shard_map/ppermute | solution.py:245
  31.9 2.2 %project.11 = bf16[256,1024]{1,0:T(8,128)(2,1)S(1)} custom-call(s32[1]{0:T(128)} %bitcast.7.first_ref, bf16[256,1024]{1,0:T(8,128)(2,1)S(1)} %attend.1.attended_ref, bf16[1024,8192]{1,0:T(8,128)(2,1)} %weight_ref.15), custom_call_target="tpu_custom_call" | custom-call | tf_op jit(solution)/shard_map/project/pallas_call | solution.py:182
  34.1 1.3 %collective-permute-start.12 = (bf16[256,1024]{1,0:T(8,128)(2,1)S(1)}, bf16[256,1024]{1,0:T(8,128)(2,1)S(1)}, u32[]{:S(2)}, u32[]{:S(2)}) collective-permute-start(bf16[256,1024]{1,0:T(8,128)(2,1)S(1)} %project.11), channel_id=1, source_target_pairs={{0,1},{3,2},{4,5},{7,6},{8,9},{11,10},{12,13},{15,14},{16,17},{19,... | collective-permute-start | bytes 1572872 | tf_op jit(solution)/shard_map/ppermute | solution.py:245
  35.4 2.2 %project.12 = bf16[256,1024]{1,0:T(8,128)(2,1)S(1)} custom-call(s32[1]{0:T(128)} %bitcast.6.first_ref, bf16[256,1024]{1,0:T(8,128)(2,1)S(1)} %attend.1.attended_ref, bf16[1024,8192]{1,0:T(8,128)(2,1)} %weight_ref.15), custom_call_target="tpu_custom_call" | custom-call | tf_op jit(solution)/shard_map/project/pallas_call | solution.py:182
  37.6 2.2 %project.13 = bf16[256,1024]{1,0:T(8,128)(2,1)S(1)} custom-call(s32[1]{0:T(128)} %bitcast.5.first_ref, bf16[256,1024]{1,0:T(8,128)(2,1)S(1)} %attend.1.attended_ref, bf16[1024,8192]{1,0:T(8,128)(2,1)} %weight_ref.15), custom_call_target="tpu_custom_call" | custom-call | tf_op jit(solution)/shard_map/project/pallas_call | solution.py:182
  39.8 0.1 add_convert_fusion.9
  39.9 0.7 collective-permute-start.9
  40.5 0.0 collective-permute-done.8
  40.6 1.0 add_convert_fusion.8
  41.6 0.7 collective-permute-start.10
  42.3 0.0 collective-permute-done.9
  42.3 0.1 add_convert_fusion.7
  42.4 0.0 collective-permute-done.10
  42.4 0.8 add_convert_fusion.6
  43.2 4.6 %collective-permute-done.11 = bf16[256,1024]{1,0:T(8,128)(2,1)S(1)} collective-permute-done((bf16[256,1024]{1,0:T(8,128)(2,1)S(1)}, bf16[256,1024]{1,0:T(8,128)(2,1)S(1)}, u32[]{:S(2)}, u32[]{:S(2)}) %collective-permute-start.11) | collective-permute-done | bytes 524320 | tf_op jit(solution)/shard_map/ppermute | solution.py:245
  47.7 1.0 add_convert_fusion.5
  48.7 0.7 collective-permute-start.13
  49.5 12.4 %collective-permute-start.14 = (bf16[256,1024]{1,0:T(8,128)(2,1)S(1)}, bf16[256,1024]{1,0:T(8,128)(2,1)S(1)}, u32[]{:S(2)}, u32[]{:S(2)}) collective-permute-start(bf16[256,1024]{1,0:T(8,128)(2,1)S(1)} %project.12), channel_id=1, source_target_pairs={{0,1},{3,2},{4,5},{7,6},{8,9},{11,10},{12,13},{15,14},{16,17},{19,... | collective-permute-start | bytes 1572872 | tf_op jit(solution)/shard_map/ppermute | solution.py:245
  61.9 1.3 %collective-permute-start.18 = (bf16[256,1024]{1,0:T(8,128)(2,1)S(1)}, bf16[256,1024]{1,0:T(8,128)(2,1)S(1)}, u32[]{:S(2)}, u32[]{:S(2)}) collective-permute-start(bf16[256,1024]{1,0:T(8,128)(2,1)S(1)} %project.13), channel_id=1, source_target_pairs={{0,1},{3,2},{4,5},{7,6},{8,9},{11,10},{12,13},{15,14},{16,17},{19,... | collective-permute-start | bytes 1572872 | tf_op jit(solution)/shard_map/ppermute | solution.py:245
  63.2 2.2 %project.14 = bf16[256,1024]{1,0:T(8,128)(2,1)S(1)} custom-call(s32[1]{0:T(128)} %bitcast.4.first_ref, bf16[256,1024]{1,0:T(8,128)(2,1)S(1)} %attend.1.attended_ref, bf16[1024,8192]{1,0:T(8,128)(2,1)} %weight_ref.15), custom_call_target="tpu_custom_call" | custom-call | tf_op jit(solution)/shard_map/project/pallas_call | solution.py:182
  65.3 1.3 %collective-permute-start.21 = (bf16[256,1024]{1,0:T(8,128)(2,1)S(1)}, bf16[256,1024]{1,0:T(8,128)(2,1)S(1)}, u32[]{:S(2)}, u32[]{:S(2)}) collective-permute-start(bf16[256,1024]{1,0:T(8,128)(2,1)S(1)} %project.14), channel_id=1, source_target_pairs={{0,1},{3,2},{4,5},{7,6},{8,9},{11,10},{12,13},{15,14},{16,17},{19,... | collective-permute-start | bytes 1572872 | tf_op jit(solution)/shard_map/ppermute | solution.py:245
  66.7 4.0 %project.15 = bf16[256,2048]{1,0:T(8,128)(2,1)S(1)} custom-call(s32[1]{0:T(128)} %bitcast.first_ref, bf16[256,1024]{1,0:T(8,128)(2,1)S(1)} %attend.1.attended_ref, bf16[1024,8192]{1,0:T(8,128)(2,1)} %weight_ref.15), custom_call_target="tpu_custom_call" | custom-call | tf_op jit(solution)/shard_map/project/pallas_call | solution.py:182
  70.6 0.0 collective-permute-done.12
  70.7 0.2 add_convert_fusion.4
  70.9 0.7 collective-permute-start.17
  71.6 0.0 collective-permute-done.13
  71.6 1.3 %collective-permute-start.16 = (bf16[256,512]{1,0:T(8,128)(2,1)S(1)}, bf16[256,512]{1,0:T(8,128)(2,1)S(1)}, u32[]{:S(2)}, u32[]{:S(2)}) collective-permute-start(bf16[256,512]{1,0:T(8,128)(2,1)S(1)} %copy-done.3), channel_id=1, source_target_pairs={{1,0},{2,3},{5,4},{6,7},{9,8},{10,11},{13,12},{14,15},{17,16},{18,... | collective-permute-start | bytes 786440 | tf_op jit(solution)/shard_map/ppermute | solution.py:251
  72.9 0.2 add_convert_fusion.3
  73.1 1.0 collective-permute-done.14
  74.1 1.3 %collective-permute-start.15 = (bf16[256,512]{1,0:T(8,128)(2,1)S(1)}, bf16[256,512]{1,0:T(8,128)(2,1)S(1)}, u32[]{:S(2)}, u32[]{:S(2)}) collective-permute-start(bf16[256,512]{1,0:T(8,128)(2,1)S(1)} %add_convert_fusion.7), channel_id=1, source_target_pairs={{1,0},{2,3},{5,4},{6,7},{9,8},{10,11},{13,12},{14,15},{17,16},{18,... | collective-permute-start | bytes 786440 | tf_op jit(solution)/shard_map/ppermute | solution.py:251
  75.3 0.2 add_convert_fusion.2
  75.5 9.7 %collective-permute-done.18 = bf16[256,1024]{1,0:T(8,128)(2,1)S(1)} collective-permute-done((bf16[256,1024]{1,0:T(8,128)(2,1)S(1)}, bf16[256,1024]{1,0:T(8,128)(2,1)S(1)}, u32[]{:S(2)}, u32[]{:S(2)}) %collective-permute-start.18) | collective-permute-done | bytes 524320 | tf_op jit(solution)/shard_map/ppermute | solution.py:245
  85.3 1.3 %collective-permute-start.19 = (bf16[256,1024]{1,0:T(8,128)(2,1)S(1)}, bf16[256,1024]{1,0:T(8,128)(2,1)S(1)}, u32[]{:S(2)}, u32[]{:S(2)}) collective-permute-start(bf16[256,1024]{1,0:T(8,128)(2,1)S(1)} %add_convert_fusion.3), channel_id=1, source_target_pairs={{1,0},{2,3},{5,4},{6,7},{9,8},{10,11},{13,12},{14,15},{17,16},{18,... | collective-permute-start | bytes 1572872 | tf_op jit(solution)/shard_map/ppermute | solution.py:251
  86.6 0.7 collective-permute-start.20
  87.3 0.1 fusion
  87.4 0.1 collective-permute-done.15
  87.5 0.0 collective-permute-done.17
  87.5 0.3 add_convert_fusion.1
  87.8 8.3 %collective-permute-done.21 = bf16[256,1024]{1,0:T(8,128)(2,1)S(1)} collective-permute-done((bf16[256,1024]{1,0:T(8,128)(2,1)S(1)}, bf16[256,1024]{1,0:T(8,128)(2,1)S(1)}, u32[]{:S(2)}, u32[]{:S(2)}) %collective-permute-start.21) | collective-permute-done | bytes 524320 | tf_op jit(solution)/shard_map/ppermute | solution.py:245
  96.0 0.0 collective-permute-done.20
  96.1 4.2 %collective-permute-done.19 = bf16[256,1024]{1,0:T(8,128)(2,1)S(1)} collective-permute-done((bf16[256,1024]{1,0:T(8,128)(2,1)S(1)}, bf16[256,1024]{1,0:T(8,128)(2,1)S(1)}, u32[]{:S(2)}, u32[]{:S(2)}) %collective-permute-start.19) | collective-permute-done | bytes 524320 | tf_op jit(solution)/shard_map/ppermute | solution.py:251
  100.3 0.4 add_convert_fusion
  100.7 1.1 %pad_maximum_fusion = bf16[256,2048]{1,0:T(8,128)(2,1)} fusion(bf16[256,1024]{1,0:T(8,128)(2,1)S(1)} %add_convert_fusion, bf16[256,1024]{1,0:T(8,128)(2,1)S(1)} %add_convert_fusion.1), kind=kLoop, calls=%fused_computation | loop fusion | flops 2097152 | bytes 2097152 | tf_op jit(solution)/shard_map/concatenate | solution.py:272
  (11 shorter events, 0.1 us)
Async XLA Ops:
  1.6 8.4 %collective-permute-start = (bf16[1,256,256]{2,1,0:T(8,128)(2,1)}, bf16[1,256,256]{2,1,0:T(8,128)(2,1)S(1)}, u32[]{:S(2)}, u32[]{:S(2)}) collective-permute-start(bf16[1,256,256]{2,1,0:T(8,128)(2,1)} %bitcast.11), channel_id=1, source_target_pairs={{0,24},{4,28},{8,16},{12,20},{16,8},{20,12},{24,0},{28,4},{1,25},{... | collective-permute-start | bytes 393224 | tf_op jit(solution)/shard_map/ppermute | solution.py:204
  5.4 6.8 %collective-permute-start.1 = (bf16[1,256,256]{2,1,0:T(8,128)(2,1)}, bf16[1,256,256]{2,1,0:T(8,128)(2,1)S(1)}, u32[]{:S(2)}, u32[]{:S(2)}) collective-permute-start(bf16[1,256,256]{2,1,0:T(8,128)(2,1)} %bitcast.12), channel_id=1, source_target_pairs={{0,8},{4,12},{8,0},{12,4},{16,24},{20,28},{24,16},{28,20},{1,9},{5... | collective-permute-start | bytes 393224 | tf_op jit(solution)/shard_map/ppermute | solution.py:204
  6.0 6.2 %collective-permute-start.2 = (bf16[1,256,256]{2,1,0:T(8,128)(2,1)}, bf16[1,256,256]{2,1,0:T(8,128)(2,1)S(1)}, u32[]{:S(2)}, u32[]{:S(2)}) collective-permute-start(bf16[1,256,256]{2,1,0:T(8,128)(2,1)} %bitcast.13), channel_id=1, source_target_pairs={{0,16},{4,20},{8,24},{12,28},{16,0},{20,4},{24,8},{28,12},{1,17},{... | collective-permute-start | bytes 393224 | tf_op jit(solution)/shard_map/ppermute | solution.py:204
  6.0 6.7 %collective-permute-start.3 = (bf16[1,256,256]{2,1,0:T(8,128)(2,1)}, bf16[1,256,256]{2,1,0:T(8,128)(2,1)S(1)}, u32[]{:S(2)}, u32[]{:S(2)}) collective-permute-start(bf16[1,256,256]{2,1,0:T(8,128)(2,1)} %bitcast.14), channel_id=1, source_target_pairs={{0,4},{4,0},{8,12},{12,8},{16,20},{20,16},{24,28},{28,24},{1,5},{5... | collective-permute-start | bytes 393224 | tf_op jit(solution)/shard_map/ppermute | solution.py:204
  10.0 2.8 %collective-permute-start.4 = (bf16[1,256,256]{2,1,0:T(8,128)(2,1)S(1)}, bf16[1,256,256]{2,1,0:T(8,128)(2,1)S(1)}, u32[]{:S(2)}, u32[]{:S(2)}) collective-permute-start(bf16[1,256,256]{2,1,0:T(8,128)(2,1)S(1)} %collective-permute-done.refs_0_), channel_id=1, source_target_pairs={{0,4},{4,0},{8,12},{12,8},{16,20},{20,16},{24,28},{28,24},{1,5},{5... | collective-permute-start | bytes 393224 | tf_op jit(solution)/shard_map/ppermute | solution.py:204
  12.2 1.3 %collective-permute-start.5 = (bf16[1,256,256]{2,1,0:T(8,128)(2,1)S(1)}, bf16[1,256,256]{2,1,0:T(8,128)(2,1)S(1)}, u32[]{:S(2)}, u32[]{:S(2)}) collective-permute-start(bf16[1,256,256]{2,1,0:T(8,128)(2,1)S(1)} %collective-permute-done.1.refs_1_), channel_id=1, source_target_pairs={{0,4},{4,0},{8,12},{12,8},{16,20},{20,16},{24,28},{28,24},{1,5},{5... | collective-permute-start | bytes 393224 | tf_op jit(solution)/shard_map/ppermute | solution.py:204
  12.2 1.5 %collective-permute-start.6 = (bf16[1,256,256]{2,1,0:T(8,128)(2,1)S(1)}, bf16[1,256,256]{2,1,0:T(8,128)(2,1)S(1)}, u32[]{:S(2)}, u32[]{:S(2)}) collective-permute-start(bf16[1,256,256]{2,1,0:T(8,128)(2,1)S(1)} %collective-permute-done.2.refs_2_), channel_id=1, source_target_pairs={{0,4},{4,0},{8,12},{12,8},{16,20},{20,16},{24,28},{28,24},{1,5},{5... | collective-permute-start | bytes 393224 | tf_op jit(solution)/shard_map/ppermute | solution.py:204
  13.7 1.0 %copy-start = (bf16[256,1024]{1,0:T(8,128)(2,1)S(1)}, bf16[256,1024]{1,0:T(8,128)(2,1)}, u32[]{:S(2)}) copy-start(bf16[256,1024]{1,0:T(8,128)(2,1)} %query_hbm.1) | copy-start | bytes 1572868
  14.8 0.9 copy-start.1
  15.7 0.7 copy-start.2
  21.3 18.5 %collective-permute-start.7 = (bf16[256,512]{1,0:T(8,128)(2,1)S(1)}, bf16[256,512]{1,0:T(8,128)(2,1)S(1)}, u32[]{:S(2)}, u32[]{:S(2)}) collective-permute-start(bf16[256,512]{1,0:T(8,128)(2,1)S(1)} %project.8), channel_id=1, source_target_pairs={{0,1},{3,2},{4,5},{7,6},{8,9},{11,10},{12,13},{15,14},{16,17},{19,... | collective-permute-start | bytes 786440 | tf_op jit(solution)/shard_map/ppermute | solution.py:245
  26.5 14.1 %collective-permute-start.8 = (bf16[256,512]{1,0:T(8,128)(2,1)S(1)}, bf16[256,512]{1,0:T(8,128)(2,1)}, u32[]{:S(2)}, u32[]{:S(2)}) collective-permute-start(bf16[256,512]{1,0:T(8,128)(2,1)S(1)} %project.9), channel_id=1, source_target_pairs={{0,1},{3,2},{4,5},{7,6},{8,9},{11,10},{12,13},{15,14},{16,17},{19,... | collective-permute-start | bytes 786440 | tf_op jit(solution)/shard_map/ppermute | solution.py:245
  30.6 17.1 %collective-permute-start.11 = (bf16[256,1024]{1,0:T(8,128)(2,1)S(1)}, bf16[256,1024]{1,0:T(8,128)(2,1)S(1)}, u32[]{:S(2)}, u32[]{:S(2)}) collective-permute-start(bf16[256,1024]{1,0:T(8,128)(2,1)S(1)} %project.10), channel_id=1, source_target_pairs={{0,1},{3,2},{4,5},{7,6},{8,9},{11,10},{12,13},{15,14},{16,17},{19,... | collective-permute-start | bytes 1572872 | tf_op jit(solution)/shard_map/ppermute | solution.py:245
  34.1 36.5 %collective-permute-start.12 = (bf16[256,1024]{1,0:T(8,128)(2,1)S(1)}, bf16[256,1024]{1,0:T(8,128)(2,1)S(1)}, u32[]{:S(2)}, u32[]{:S(2)}) collective-permute-start(bf16[256,1024]{1,0:T(8,128)(2,1)S(1)} %project.11), channel_id=1, source_target_pairs={{0,1},{3,2},{4,5},{7,6},{8,9},{11,10},{12,13},{15,14},{16,17},{19,... | collective-permute-start | bytes 1572872 | tf_op jit(solution)/shard_map/ppermute | solution.py:245
  39.9 2.4 %collective-permute-start.9 = (bf16[256,512]{1,0:T(8,128)(2,1)S(1)}, bf16[256,512]{1,0:T(8,128)(2,1)S(1)}, u32[]{:S(2)}, u32[]{:S(2)}) collective-permute-start(bf16[256,512]{1,0:T(8,128)(2,1)S(1)} %add_convert_fusion.9), channel_id=1, source_target_pairs={{1,2},{2,1},{5,6},{6,5},{9,10},{10,9},{13,14},{14,13},{17,18},{18,... | collective-permute-start | bytes 786440 | tf_op jit(solution)/shard_map/ppermute | solution.py:248
  41.6 0.8 collective-permute-start.10
  48.7 22.8 %collective-permute-start.13 = (bf16[256,1024]{1,0:T(8,128)(2,1)}, bf16[256,1024]{1,0:T(8,128)(2,1)S(1)}, u32[]{:S(2)}, u32[]{:S(2)}) collective-permute-start(bf16[256,1024]{1,0:T(8,128)(2,1)} %add_convert_fusion.5), channel_id=1, source_target_pairs={{1,2},{2,1},{5,6},{6,5},{9,10},{10,9},{13,14},{14,13},{17,18},{18,... | collective-permute-start | bytes 1572872 | tf_op jit(solution)/shard_map/ppermute | solution.py:248
  49.5 24.6 %collective-permute-start.14 = (bf16[256,1024]{1,0:T(8,128)(2,1)S(1)}, bf16[256,1024]{1,0:T(8,128)(2,1)S(1)}, u32[]{:S(2)}, u32[]{:S(2)}) collective-permute-start(bf16[256,1024]{1,0:T(8,128)(2,1)S(1)} %project.12), channel_id=1, source_target_pairs={{0,1},{3,2},{4,5},{7,6},{8,9},{11,10},{12,13},{15,14},{16,17},{19,... | collective-permute-start | bytes 1572872 | tf_op jit(solution)/shard_map/ppermute | solution.py:245
  61.9 23.4 %collective-permute-start.18 = (bf16[256,1024]{1,0:T(8,128)(2,1)S(1)}, bf16[256,1024]{1,0:T(8,128)(2,1)S(1)}, u32[]{:S(2)}, u32[]{:S(2)}) collective-permute-start(bf16[256,1024]{1,0:T(8,128)(2,1)S(1)} %project.13), channel_id=1, source_target_pairs={{0,1},{3,2},{4,5},{7,6},{8,9},{11,10},{12,13},{15,14},{16,17},{19,... | collective-permute-start | bytes 1572872 | tf_op jit(solution)/shard_map/ppermute | solution.py:245
  65.3 30.7 %collective-permute-start.21 = (bf16[256,1024]{1,0:T(8,128)(2,1)S(1)}, bf16[256,1024]{1,0:T(8,128)(2,1)S(1)}, u32[]{:S(2)}, u32[]{:S(2)}) collective-permute-start(bf16[256,1024]{1,0:T(8,128)(2,1)S(1)} %project.14), channel_id=1, source_target_pairs={{0,1},{3,2},{4,5},{7,6},{8,9},{11,10},{12,13},{15,14},{16,17},{19,... | collective-permute-start | bytes 1572872 | tf_op jit(solution)/shard_map/ppermute | solution.py:245
  66.7 4.9 %copy-start.3 = (bf16[256,512]{1,0:T(8,128)(2,1)S(1)}, bf16[256,512]{1,0:T(8,128)(2,1)}, u32[]{:S(2)}) copy-start(bf16[256,512]{1,0:T(8,128)(2,1)} %add_convert_fusion.6) | copy-start | bytes 786436
  70.9 16.6 %collective-permute-start.17 = (bf16[256,1024]{1,0:T(8,128)(2,1)S(1)}, bf16[256,1024]{1,0:T(8,128)(2,1)S(1)}, u32[]{:S(2)}, u32[]{:S(2)}) collective-permute-start(bf16[256,1024]{1,0:T(8,128)(2,1)S(1)} %add_convert_fusion.4), channel_id=1, source_target_pairs={{1,2},{2,1},{5,6},{6,5},{9,10},{10,9},{13,14},{14,13},{17,18},{18,... | collective-permute-start | bytes 1572872 | tf_op jit(solution)/shard_map/ppermute | solution.py:248
  71.6 15.0 %collective-permute-start.16 = (bf16[256,512]{1,0:T(8,128)(2,1)S(1)}, bf16[256,512]{1,0:T(8,128)(2,1)S(1)}, u32[]{:S(2)}, u32[]{:S(2)}) collective-permute-start(bf16[256,512]{1,0:T(8,128)(2,1)S(1)} %copy-done.3), channel_id=1, source_target_pairs={{1,0},{2,3},{5,4},{6,7},{9,8},{10,11},{13,12},{14,15},{17,16},{18,... | collective-permute-start | bytes 786440 | tf_op jit(solution)/shard_map/ppermute | solution.py:251
  74.1 13.4 %collective-permute-start.15 = (bf16[256,512]{1,0:T(8,128)(2,1)S(1)}, bf16[256,512]{1,0:T(8,128)(2,1)S(1)}, u32[]{:S(2)}, u32[]{:S(2)}) collective-permute-start(bf16[256,512]{1,0:T(8,128)(2,1)S(1)} %add_convert_fusion.7), channel_id=1, source_target_pairs={{1,0},{2,3},{5,4},{6,7},{9,8},{10,11},{13,12},{14,15},{17,16},{18,... | collective-permute-start | bytes 786440 | tf_op jit(solution)/shard_map/ppermute | solution.py:251
  85.3 15.0 %collective-permute-start.19 = (bf16[256,1024]{1,0:T(8,128)(2,1)S(1)}, bf16[256,1024]{1,0:T(8,128)(2,1)S(1)}, u32[]{:S(2)}, u32[]{:S(2)}) collective-permute-start(bf16[256,1024]{1,0:T(8,128)(2,1)S(1)} %add_convert_fusion.3), channel_id=1, source_target_pairs={{1,0},{2,3},{5,4},{6,7},{9,8},{10,11},{13,12},{14,15},{17,16},{18,... | collective-permute-start | bytes 1572872 | tf_op jit(solution)/shard_map/ppermute | solution.py:251
  86.6 9.5 %collective-permute-start.20 = (bf16[256,1024]{1,0:T(8,128)(2,1)S(1)}, bf16[256,1024]{1,0:T(8,128)(2,1)S(1)}, u32[]{:S(2)}, u32[]{:S(2)}) collective-permute-start(bf16[256,1024]{1,0:T(8,128)(2,1)S(1)} %add_convert_fusion.2), channel_id=1, source_target_pairs={{1,2},{2,1},{5,6},{6,5},{9,10},{10,9},{13,14},{14,13},{17,18},{18,... | collective-permute-start | bytes 1572872 | tf_op jit(solution)/shard_map/ppermute | solution.py:248

commit v3 on v2

v3 whole, which is shorter than its diff:
```python
import functools
import math

import jax
import jax.numpy as jnp
from jax import lax
from jax.experimental import pallas as pl
from jax.experimental.pallas import tpu as pltpu
from jax.sharding import PartitionSpec as P

HDIM = 128
BLOCK = 128
GQ = 8
TILE = 512
EXPONENT = HDIM ** (-0.5) * math.log2(math.e)
VMEM_LIMIT = 48 * 1024 * 1024


def pack_head(keys, values, head):
    return jnp.concatenate(
        [lax.dynamic_slice_in_dim(array, head * HDIM, HDIM, 1) for array in (keys, values)], axis=1
    )


def choose_blocks(place, swaps, owners, row, per_device, mask_ref, chosen):
    def choose(slot, found):
        owner = place ^ swaps[slot] if swaps else slot
        for part in range(per_device):
            here = mask_ref[row, owner * per_device + part] == 1
            chosen[found] = slot * per_device + part
            found = found + here.astype(jnp.int32)
        return found

    found = jnp.int32(0)
    if swaps:
        for slot in range(owners):
            found = choose(slot, found)
    else:
        found = lax.fori_loop(0, owners, choose, found)

    @pl.when(found % 2 == 1)
    def _():
        chosen[found] = chosen[found - 1]

    return found


def attention_kernel(parts, swaps, first, place_ref, mask_ref, query_ref, *refs):
    if first:
        own_hbm, *refs = refs
        kv_refs = refs[:parts]
        query_out, peaks_out, totals_out, sums_out, kv, scores, peak, chosen, arrived = refs[parts:]
        loads = [pltpu.make_async_copy(query_ref, query_out, arrived.at[0])]
        if swaps:
            loads.append(pltpu.make_async_copy(own_hbm, kv.at[0], arrived.at[1]))
        for load in loads:
            load.start()
        at = len(loads) - 1
    else:
        peaks_in, totals_in, sums_in, *refs = refs
        kv_refs = refs[:parts]
        out_ref, kv, scores, peak, total, summed, chosen = refs[parts:]
        at = 0
    for ref in kv_refs:
        count = ref.shape[0]
        kv[at : at + count] = ref[...]
        at += count
    if first:
        for load in loads:
            load.wait()
        query_ref = query_out
    rows, width = query_ref.shape
    heads = width // HDIM
    per_device = rows // BLOCK
    place = place_ref[0]
    owners = kv.shape[0]

    for block in range(per_device):
        top = slice(block * BLOCK, (block + 1) * BLOCK)
        found = choose_blocks(
            place, swaps, owners, place * per_device + block, per_device, mask_ref, chosen
        )
        pairs = (found + 1) // 2

        def tile(number):
            index = chosen[number]
            start = pl.multiple_of((index % per_device) * BLOCK, BLOCK)
            return index // per_device, pl.ds(start, BLOCK)

        if first:
            total, summed = totals_out.at[block], sums_out.at[block]
            peak[...] = jnp.full(peak.shape, -1e30, jnp.float32)
            total[...] = jnp.zeros(total.shape, jnp.float32)
            summed[...] = jnp.zeros(summed.shape, jnp.float32)
        else:
            peak[...] = peaks_in[block]

        def score(pair, carry):
            slot0, rows0 = tile(2 * pair)
            slot1, rows1 = tile(2 * pair + 1)
            keys = jnp.concatenate([kv[slot0, rows0, :HDIM], kv[slot1, rows1, :HDIM]], axis=0)
            for head in range(heads):
                query = query_ref[top, head * HDIM : (head + 1) * HDIM]
                here = lax.dot_general(
                    query, keys, (((1,), (1,)), ((), ())), preferred_element_type=jnp.float32
                )
                scores[pair, head] = here
                peak[head] = jnp.maximum(
                    peak[head], jnp.maximum(here[:, :BLOCK], here[:, BLOCK:])
                )
            return carry

        lax.fori_loop(0, pairs, score, 0)

        @pl.when(found % 2 == 1)
        def _():
            scores[pairs - 1, :, :, BLOCK:] = jnp.full((heads, BLOCK, BLOCK), -1e30, jnp.float32)

        for head in range(heads):
            highest = jnp.max(peak[head], axis=1, keepdims=True)
            peak[head] = jnp.broadcast_to(highest, (BLOCK, BLOCK))
            if not first:
                factor = jnp.exp2((peaks_in[block, head] - peak[head]) * EXPONENT)
                total[head] = totals_in[block, head] * factor
                summed[head] = sums_in[block, head] * factor

        def weigh(pair, carry):
            slot0, rows0 = tile(2 * pair)
            slot1, rows1 = tile(2 * pair + 1)
            values = jnp.concatenate([kv[slot0, rows0, HDIM:], kv[slot1, rows1, HDIM:]], axis=0)
            for head in range(heads):
                highest = peak[head]
                left = jnp.exp2((scores[pair, head, :, :BLOCK] - highest) * EXPONENT)
                right = jnp.exp2((scores[pair, head, :, BLOCK:] - highest) * EXPONENT)
                total[head] += left + right
                weights = jnp.concatenate([left, right], axis=1).astype(jnp.bfloat16)
                summed[head] += jnp.dot(weights, values, preferred_element_type=jnp.float32)
            return carry

        lax.fori_loop(0, pairs, weigh, 0)

        if first:
            peaks_out[block] = peak[...]
        else:
            for head in range(heads):
                norm = jnp.sum(total[head], axis=1, keepdims=True)
                out_ref[top, head * HDIM : (head + 1) * HDIM] = (summed[head] / norm).astype(
                    jnp.bfloat16
                )


def attention_part(first, swaps, count, place, storm_mask, query, state, parts):
    rows, width = query.shape
    heads = width // HDIM
    blocks = count * (rows // BLOCK)
    vmem = pl.BlockSpec(memory_space=pltpu.VMEM)
    hbm = pl.BlockSpec(memory_space=pl.ANY)
    running = (rows // BLOCK, heads, BLOCK, BLOCK)
    taken = jax.ShapeDtypeStruct((rows, width), jnp.bfloat16)
    scratch = [
        pltpu.VMEM((count, rows, 2 * HDIM), jnp.bfloat16),
        pltpu.VMEM(((blocks + 1) // 2, heads, BLOCK, 2 * BLOCK), jnp.float32),
        pltpu.VMEM((heads, BLOCK, BLOCK), jnp.float32),
    ]
    if first:
        specs = [hbm, hbm] + [vmem] * len(parts)
        out_shape = [taken] + [jax.ShapeDtypeStruct(running, jnp.float32)] * 3
    else:
        specs = [vmem] * (4 + len(parts))
        out_shape = taken
        scratch += [pltpu.VMEM((heads, BLOCK, BLOCK), jnp.float32)] * 2
    scratch += [pltpu.SMEM((blocks + 2,), jnp.int32)]
    if first:
        scratch += [pltpu.SemaphoreType.DMA((2,))]
    return pl.pallas_call(
        functools.partial(attention_kernel, len(parts), swaps, first),
        grid_spec=pltpu.PrefetchScalarGridSpec(
            num_scalar_prefetch=2,
            grid=(1,),
            in_specs=specs,
            out_specs=[vmem] * 4 if first else vmem,
            scratch_shapes=scratch,
        ),
        out_shape=out_shape,
        compiler_params=pltpu.CompilerParams(vmem_limit_bytes=VMEM_LIMIT),
        name="attend_first" if first else "attend_rest",
    )(place.astype(jnp.int32).reshape(1), storm_mask, query, *state, *parts)


def attend(queries, packed, place, devices, storm_mask):
    if devices != 8:
        everyone = lax.all_gather(packed, "ctx", axis=0, tiled=False)
        state = attention_part(
            True, (), devices, place, storm_mask, queries, [packed], [everyone]
        )
        query, *state = state
        nothing = jnp.zeros_like(storm_mask)
        return attention_part(
            False, (), 1, place, nothing, query, state, [everyone[:1]]
        )

    def swap(array, bits):
        return lax.ppermute(array, "ctx", [(i, i ^ bits) for i in range(devices)])

    near = [swap(packed[None], bits) for bits in (6, 2, 4)]
    query, *state = attention_part(
        True, (0, 1), 2, place, storm_mask, queries, [packed], [swap(packed[None], 1)]
    )
    other = [swap(array, 1) for array in near]
    return attention_part(
        False, (6, 2, 4, 7, 3, 5), 6, place, storm_mask, query, state, near + other
    )


def project_kernel(first_ref, attended_ref, weight_ref, out_ref):
    out_ref[...] = jnp.dot(
        attended_ref[...], weight_ref[...], preferred_element_type=jnp.float32
    ).astype(jnp.bfloat16)


def project(attended, out_weight, first, columns):
    rows, depth = attended.shape
    tile = min(TILE, columns)
    return pl.pallas_call(
        project_kernel,
        grid_spec=pltpu.PrefetchScalarGridSpec(
            num_scalar_prefetch=1,
            grid=(columns // tile,),
            in_specs=[
                pl.BlockSpec((rows, depth), lambda i, first: (0, 0)),
                pl.BlockSpec((depth, tile), lambda i, first: (0, first[0] + i)),
            ],
            out_specs=pl.BlockSpec((rows, tile), lambda i, first: (0, i)),
        ),
        out_shape=jax.ShapeDtypeStruct((rows, columns), jnp.bfloat16),
        compiler_params=pltpu.CompilerParams(vmem_limit_bytes=VMEM_LIMIT),
        name="project",
    )((first // tile).astype(jnp.int32).reshape(1), attended, out_weight)


def after(array, *earlier):
    return lax.optimization_barrier((array, *earlier))[0]


def added(*arrays):
    wide = [array.astype(jnp.float32) for array in arrays]
    return functools.reduce(lambda a, b: a + b, wide).astype(jnp.bfloat16)


def line_sum(attended, out_weight):
    place = lax.axis_index("tp")
    quarter = out_weight.shape[1] // 4
    upper = place >= 2
    far_outer = jnp.where(upper, 0, 3) * quarter
    far_inner = jnp.where(upper, 1, 2) * quarter
    near = jnp.where(upper, 5 - place, 1 - place) * quarter
    own = place * quarter
    half = quarter // 2
    fourth = quarter // 4
    pieces = ((0, fourth), (fourth, fourth), (half, half))
    halves = ((0, half), (half, half))
    projected, chain = [], []

    def part(first, columns):
        source = after(attended, projected[-1]) if projected else attended
        projected.append(project(source, out_weight, first, columns))
        return projected[-1]

    def step(*arrays):
        first = after(arrays[0], chain[-1]) if chain else arrays[0]
        chain.append(added(first, *arrays[1:]))
        return chain[-1]

    def inward(array):
        return lax.ppermute(array, "tp", [(0, 1), (3, 2)])

    def across(array):
        return lax.ppermute(array, "tp", [(1, 2), (2, 1)])

    def outward(array):
        return lax.ppermute(array, "tp", [(1, 0), (2, 3)])

    outer_parts = [part(far_outer + at, size) for at, size in pieces]
    outer_sums = [inward(array) for array in outer_parts]
    inner_parts = [part(far_inner + at, size) for at, size in halves]
    inner_sums = [inward(array) for array in inner_parts]
    to_outer, to_own, returned, direct = [None] * 3, [None] * 2, [None] * 3, [None] * 2

    def send_outer(at):
        to_outer[at] = across(step(outer_parts[at], outer_sums[at]))

    def send_inner(at):
        to_own[at] = across(step(inner_parts[at], inner_sums[at]))
        direct[at] = inward(after(near_parts[at], chain[-1]))

    def send_back(at):
        returned[at] = outward(step(near_pieces[at], to_outer[at]))

    send_outer(0)
    send_outer(1)
    projected.append(chain[-1])
    near_parts = [part(near + at, size) for at, size in halves]
    near_pieces = [near_parts[0][:, :fourth], near_parts[0][:, fourth:], near_parts[1]]
    send_outer(2)
    send_back(0)
    send_back(1)
    mine = part(own, quarter)
    send_inner(0)
    left = step(mine[:, :half], jnp.concatenate(returned[:2], axis=1))
    send_inner(1)
    send_back(2)
    left = step(left, to_own[0], direct[0])
    right = step(mine[:, half:], returned[2], to_own[1], direct[1])
    return jnp.concatenate([left, right], axis=1)


def body(mesh, queries, keys, values, out_weight, storm_mask):
    place = lax.axis_index("ctx")
    heads = queries.shape[1] // HDIM
    shared_head = lax.axis_index("tp") * heads // GQ
    packed = pack_head(keys, values, shared_head)
    attended = attend(queries, packed, place, mesh.shape["ctx"], storm_mask)
    if mesh.shape["tp"] == 4:
        return line_sum(attended, out_weight)
    partial = project(attended, out_weight, jnp.int32(0), out_weight.shape[1])
    return lax.psum_scatter(partial, "tp", scatter_dimension=1, tiled=True)


def solution(mesh):
    placed = (P("ctx", "tp"), P("ctx", None), P("ctx", None), P("tp", None), P())
    return jax.shard_map(
        functools.partial(body, mesh),
        mesh=mesh,
        in_specs=placed,
        out_specs=P("ctx", "tp"),
        check_vma=False,
    )
```

time: 104 us -> 97.1 us (0.934)
  the two profiles are of different devices: /device:TPU:0 before, /device:TPU:14 now
where the time goes in v3:
time: 97.1 us; the launch traced here: 95.7 us
  starting transfers between devices  36.1 us (37%)
  waiting for transfers between devices  27 us (28%)
  Pallas kernels  26.5 us (27%)
  other arithmetic  2.9 us (3%)
  local copies, waits for them, and re-layouts  2.73 us (3%)
    ppermute x7, waiting for transfers between devices, inward(): return lax.ppermute(array, 'tp', [(0, 1), (3, 2)])  20 us
    pallas_call x8, Pallas kernels, project(): pl.pallas_call(project_kernel, grid_spec=pltpu.PrefetchScalarGridSpec(num...  18 us
    ppermute x5, starting transfers between devices, across(): return lax.ppermute(array, 'tp', [(1, 2), (2, 1)])  16.3 us
    ppermute x7, starting transfers between devices, inward(): return lax.ppermute(array, 'tp', [(0, 1), (3, 2)])  9.04 us
    pallas_call x2, Pallas kernels, attention_part(): pl.pallas_call(functools.partial(attention_kernel, len(parts), swaps, fir...  8.45 us
    ppermute x3, starting transfers between devices, outward(): return lax.ppermute(array, 'tp', [(1, 0), (2, 3)])  7.22 us
    ppermute x7, waiting for transfers between devices, swap(): return lax.ppermute(array, 'ctx', [(i, i ^ bits) for i in range(devices)])  5.46 us
    ppermute x7, starting transfers between devices, swap(): return lax.ppermute(array, 'ctx', [(i, i ^ bits) for i in range(devices)])  3.56 us
  transfers between devices with their start and end apart: 22, of which 10 were waited for; matrix products, arithmetic and copies ran while one was open for 2% of the time, Pallas kernels for 20%

profile of v3, /device:TPU:14, one launch (start us, length us, event | category | flops | bytes accessed | tf_op | source)
XLA Modules:
  0.0 95.7 jit_solution(4926448573665367539)
XLA Ops:
  0.0 0.9 constant_dynamic-slice_fusion
  0.9 0.5 collective-permute-start.1
  1.5 1.5 %collective-permute-start.2 = (bf16[1,256,256]{2,1,0:T(8,128)(2,1)S(1)}, bf16[1,256,256]{2,1,0:T(8,128)(2,1)S(1)}, u32[]{:S(2)}, u32[]{:S(2)}) collective-permute-start(bf16[1,256,256]{2,1,0:T(8,128)(2,1)S(1)} %get-tuple-element.53), channel_id=1, source_target_pairs={{0,8},{4,12},{8,0},{12,4},{16,24},{20,28},{24,16},{28,20},{1,9},{5... | collective-permute-start | bytes 393224 | tf_op jit(solution)/shard_map/ppermute | solution.py:203
  3.0 1.5 %collective-permute-start.3 = (bf16[1,256,256]{2,1,0:T(8,128)(2,1)S(1)}, bf16[1,256,256]{2,1,0:T(8,128)(2,1)S(1)}, u32[]{:S(2)}, u32[]{:S(2)}) collective-permute-start(bf16[1,256,256]{2,1,0:T(8,128)(2,1)S(1)} %get-tuple-element.53), channel_id=1, source_target_pairs={{0,16},{4,20},{8,24},{12,28},{16,0},{20,4},{24,8},{28,12},{1,17},{... | collective-permute-start | bytes 393224 | tf_op jit(solution)/shard_map/ppermute | solution.py:203
  4.5 3.8 %collective-permute-done.1.refs_3_ = bf16[1,256,256]{2,1,0:T(8,128)(2,1)S(1)} collective-permute-done((bf16[1,256,256]{2,1,0:T(8,128)(2,1)S(1)}, bf16[1,256,256]{2,1,0:T(8,128)(2,1)S(1)}, u32[]{:S(2)}, u32[]{:S(2)}) %collective-permute-start.1) | collective-permute-done | bytes 131104 | tf_op jit(solution)/shard_map/ppermute | solution.py:203
  8.3 0.0 collective-permute-start.4
  8.3 0.7 collective-permute-done.2.refs_4_
  9.0 1.0 collective-permute-done.3.refs_5_
  9.9 0.0 collective-permute-start.6
  9.9 0.0 collective-permute-done.refs_1_
  9.9 1.0 %copy-done = bf16[256,1024]{1,0:T(8,128)(2,1)S(1)} copy-done((bf16[256,1024]{1,0:T(8,128)(2,1)S(1)}, bf16[256,1024]{1,0:T(8,128)(2,1)}, u32[]{:S(2)}) %copy-start) | copy-done | bytes 524312
  11.0 0.7 copy-done.1
  11.7 2.9 %attend_first.1 = (bf16[256,1024]{1,0:T(8,128)(2,1)S(1)}, f32[2,8,128,128]{3,2,1,0:T(8,128)S(1)}, f32[2,8,128,128]{3,2,1,0:T(8,128)S(1)}, f32[2,8,128,128]{3,2,1,0:T(8,128)S(1)}) custom-call(s32[1]{0:T(128)} %bitcast.1.place_ref, s32[16,16]{1,0:T(8,128)S(1)} %copy-done.1, bf16[256,1024]{1,0:T(8,128)(2,1)S(1)} %copy-done, ...), custom_call_target="tpu_custom_call" | custom-call | tf_op jit(solution)/shard_map/attend_first/pallas_call | solution.py:175
  14.6 0.0 collective-permute-done.5.refs_7_
  14.6 0.0 collective-permute-done.6.refs_8_
  14.7 5.5 %attend_rest.1.attended_ref = bf16[256,1024]{1,0:T(8,128)(2,1)S(1)} custom-call(s32[1]{0:T(128)} %bitcast.1.place_ref, s32[16,16]{1,0:T(8,128)S(1)} %copy-done.1, bf16[256,1024]{1,0:T(8,128)(2,1)S(1)} %get-tuple-element.27.query_ref, f32[2,8,128,128]{3,2,1,0:T(8,128)S(1)} %get-tuple-element.28.refs_0_, f32[2,8,128,128]{3,2,1,0:T(8,128)S(1)} %get-tuple-element.29.refs_1_, ...), custom_call_target="tpu_custom_call" | custom-call | tf_op jit(solution)/shard_map/attend_rest/pallas_call | solution.py:175
  20.2 1.7 %project.8 = bf16[256,512]{1,0:T(8,128)(2,1)S(1)} custom-call(s32[1]{0:T(128)} %bitcast.6.first_ref, bf16[256,1024]{1,0:T(8,128)(2,1)S(1)} %attend_rest.1.attended_ref, bf16[1024,8192]{1,0:T(8,128)(2,1)} %weight_ref.15), custom_call_target="tpu_custom_call" | custom-call | tf_op jit(solution)/shard_map/project/pallas_call | solution.py:224
  21.8 1.3 %collective-permute-start.7 = (bf16[256,512]{1,0:T(8,128)(2,1)S(1)}, bf16[256,512]{1,0:T(8,128)(2,1)S(1)}, u32[]{:S(2)}, u32[]{:S(2)}) collective-permute-start(bf16[256,512]{1,0:T(8,128)(2,1)S(1)} %project.8), channel_id=1, source_target_pairs={{0,1},{3,2},{4,5},{7,6},{8,9},{11,10},{12,13},{15,14},{16,17},{19,... | collective-permute-start | bytes 786440 | tf_op jit(solution)/shard_map/ppermute | solution.py:275
  23.1 1.7 %project.9 = bf16[256,512]{1,0:T(8,128)(2,1)S(1)} custom-call(s32[1]{0:T(128)} %bitcast.5.first_ref, bf16[256,1024]{1,0:T(8,128)(2,1)S(1)} %attend_rest.1.attended_ref, bf16[1024,8192]{1,0:T(8,128)(2,1)} %weight_ref.15), custom_call_target="tpu_custom_call" | custom-call | tf_op jit(solution)/shard_map/project/pallas_call | solution.py:224
  24.8 1.3 %collective-permute-start.8 = (bf16[256,512]{1,0:T(8,128)(2,1)S(1)}, bf16[256,512]{1,0:T(8,128)(2,1)S(1)}, u32[]{:S(2)}, u32[]{:S(2)}) collective-permute-start(bf16[256,512]{1,0:T(8,128)(2,1)S(1)} %project.9), channel_id=1, source_target_pairs={{0,1},{3,2},{4,5},{7,6},{8,9},{11,10},{12,13},{15,14},{16,17},{19,... | collective-permute-start | bytes 786440 | tf_op jit(solution)/shard_map/ppermute | solution.py:275
  26.2 2.2 %project.13 = bf16[256,1024]{1,0:T(8,128)(2,1)S(1)} custom-call(s32[1]{0:T(128)} %bitcast.8.first_ref, bf16[256,1024]{1,0:T(8,128)(2,1)S(1)} %attend_rest.1.attended_ref, bf16[1024,8192]{1,0:T(8,128)(2,1)} %weight_ref.15), custom_call_target="tpu_custom_call" | custom-call | tf_op jit(solution)/shard_map/project/pallas_call | solution.py:224
  28.3 1.3 %collective-permute-start.9 = (bf16[256,1024]{1,0:T(8,128)(2,1)S(1)}, bf16[256,1024]{1,0:T(8,128)(2,1)S(1)}, u32[]{:S(2)}, u32[]{:S(2)}) collective-permute-start(bf16[256,1024]{1,0:T(8,128)(2,1)S(1)} %project.13), channel_id=1, source_target_pairs={{0,1},{3,2},{4,5},{7,6},{8,9},{11,10},{12,13},{15,14},{16,17},{19,... | collective-permute-start | bytes 1572872 | tf_op jit(solution)/shard_map/ppermute | solution.py:275
  29.6 2.2 %project.14 = bf16[256,1024]{1,0:T(8,128)(2,1)S(1)} custom-call(s32[1]{0:T(128)} %bitcast.7.first_ref, bf16[256,1024]{1,0:T(8,128)(2,1)S(1)} %attend_rest.1.attended_ref, bf16[1024,8192]{1,0:T(8,128)(2,1)} %weight_ref.15), custom_call_target="tpu_custom_call" | custom-call | tf_op jit(solution)/shard_map/project/pallas_call | solution.py:224
  31.8 1.3 %collective-permute-start.12 = (bf16[256,1024]{1,0:T(8,128)(2,1)S(1)}, bf16[256,1024]{1,0:T(8,128)(2,1)S(1)}, u32[]{:S(2)}, u32[]{:S(2)}) collective-permute-start(bf16[256,1024]{1,0:T(8,128)(2,1)S(1)} %project.14), channel_id=1, source_target_pairs={{0,1},{3,2},{4,5},{7,6},{8,9},{11,10},{12,13},{15,14},{16,17},{19,... | collective-permute-start | bytes 1572872 | tf_op jit(solution)/shard_map/ppermute | solution.py:275
  33.1 2.2 %project.15 = bf16[256,1024]{1,0:T(8,128)(2,1)S(1)} custom-call(s32[1]{0:T(128)} %bitcast.9.first_ref, bf16[256,1024]{1,0:T(8,128)(2,1)S(1)} %attend_rest.1.attended_ref, bf16[1024,8192]{1,0:T(8,128)(2,1)} %weight_ref.15), custom_call_target="tpu_custom_call" | custom-call | tf_op jit(solution)/shard_map/project/pallas_call | solution.py:224
  35.3 1.3 %collective-permute-start.15 = (bf16[256,1024]{1,0:T(8,128)(2,1)S(1)}, bf16[256,1024]{1,0:T(8,128)(2,1)S(1)}, u32[]{:S(2)}, u32[]{:S(2)}) collective-permute-start(bf16[256,1024]{1,0:T(8,128)(2,1)S(1)} %project.15), channel_id=1, source_target_pairs={{0,1},{3,2},{4,5},{7,6},{8,9},{11,10},{12,13},{15,14},{16,17},{19,... | collective-permute-start | bytes 1572872 | tf_op jit(solution)/shard_map/ppermute | solution.py:275
  36.6 0.0 collective-permute-done.7
  36.6 0.1 add_convert_fusion.10
  36.7 1.8 %collective-permute-done.8 = bf16[256,512]{1,0:T(8,128)(2,1)S(1)} collective-permute-done((bf16[256,512]{1,0:T(8,128)(2,1)S(1)}, bf16[256,512]{1,0:T(8,128)(2,1)S(1)}, u32[]{:S(2)}, u32[]{:S(2)}) %collective-permute-start.8) | collective-permute-done | bytes 262176 | tf_op jit(solution)/shard_map/ppermute | solution.py:275
  38.4 0.1 add_convert_fusion.9
  38.5 3.5 %collective-permute-start.10 = (bf16[256,512]{1,0:T(8,128)(2,1)S(1)}, bf16[256,512]{1,0:T(8,128)(2,1)S(1)}, u32[]{:S(2)}, u32[]{:S(2)}) collective-permute-start(bf16[256,512]{1,0:T(8,128)(2,1)S(1)} %add_convert_fusion.10), channel_id=1, source_target_pairs={{1,2},{2,1},{5,6},{6,5},{9,10},{10,9},{13,14},{14,13},{17,18},{18,... | collective-permute-start | bytes 786440 | tf_op jit(solution)/shard_map/ppermute | solution.py:278
  42.0 2.3 %collective-permute-start.11 = (bf16[256,512]{1,0:T(8,128)(2,1)S(1)}, bf16[256,512]{1,0:T(8,128)(2,1)S(1)}, u32[]{:S(2)}, u32[]{:S(2)}) collective-permute-start(bf16[256,512]{1,0:T(8,128)(2,1)S(1)} %add_convert_fusion.9), channel_id=1, source_target_pairs={{1,2},{2,1},{5,6},{6,5},{9,10},{10,9},{13,14},{14,13},{17,18},{18,... | collective-permute-start | bytes 786440 | tf_op jit(solution)/shard_map/ppermute | solution.py:278
  44.4 2.2 %project.10 = bf16[256,1024]{1,0:T(8,128)(2,1)S(1)} custom-call(s32[1]{0:T(128)} %bitcast.4.first_ref, bf16[256,1024]{1,0:T(8,128)(2,1)S(1)} %attend_rest.1.attended_ref, bf16[1024,8192]{1,0:T(8,128)(2,1)} %weight_ref.15), custom_call_target="tpu_custom_call" | custom-call | tf_op jit(solution)/shard_map/project/pallas_call | solution.py:224
  46.5 2.2 %project.11 = bf16[256,1024]{1,0:T(8,128)(2,1)S(1)} custom-call(s32[1]{0:T(128)} %bitcast.3.first_ref, bf16[256,1024]{1,0:T(8,128)(2,1)S(1)} %attend_rest.1.attended_ref, bf16[1024,8192]{1,0:T(8,128)(2,1)} %weight_ref.15), custom_call_target="tpu_custom_call" | custom-call | tf_op jit(solution)/shard_map/project/pallas_call | solution.py:224
  48.7 3.9 %project.12 = bf16[256,2048]{1,0:T(8,128)(2,1)S(1)} custom-call(s32[1]{0:T(128)} %bitcast.first_ref, bf16[256,1024]{1,0:T(8,128)(2,1)S(1)} %attend_rest.1.attended_ref, bf16[1024,8192]{1,0:T(8,128)(2,1)} %weight_ref.15), custom_call_target="tpu_custom_call" | custom-call | tf_op jit(solution)/shard_map/project/pallas_call | solution.py:224
  52.7 0.1 fusion.1
  52.8 0.0 collective-permute-done.9
  52.8 0.2 add_convert_fusion.6
  53.0 0.0 collective-permute-done.10
  53.0 0.1 add_convert_fusion.8
  53.1 0.6 collective-permute-done.11
  53.6 0.1 add_convert_fusion.7
  53.7 1.3 %collective-permute-start.14 = (bf16[256,512]{1,0:T(8,128)(2,1)S(1)}, bf16[256,512]{1,0:T(8,128)(2,1)S(1)}, u32[]{:S(2)}, u32[]{:S(2)}) collective-permute-start(bf16[256,512]{1,0:T(8,128)(2,1)S(1)} %add_convert_fusion.7), channel_id=1, source_target_pairs={{1,0},{2,3},{5,4},{6,7},{9,8},{10,11},{13,12},{14,15},{17,16},{18,... | collective-permute-start | bytes 786440 | tf_op jit(solution)/shard_map/ppermute | solution.py:281
  55.0 1.3 %collective-permute-start.13 = (bf16[256,512]{1,0:T(8,128)(2,1)S(1)}, bf16[256,512]{1,0:T(8,128)(2,1)S(1)}, u32[]{:S(2)}, u32[]{:S(2)}) collective-permute-start(bf16[256,512]{1,0:T(8,128)(2,1)S(1)} %add_convert_fusion.8), channel_id=1, source_target_pairs={{1,0},{2,3},{5,4},{6,7},{9,8},{10,11},{13,12},{14,15},{17,16},{18,... | collective-permute-start | bytes 786440 | tf_op jit(solution)/shard_map/ppermute | solution.py:281
  56.3 3.5 %collective-permute-start.16 = (bf16[256,1024]{1,0:T(8,128)(2,1)S(1)}, bf16[256,1024]{1,0:T(8,128)(2,1)S(1)}, u32[]{:S(2)}, u32[]{:S(2)}) collective-permute-start(bf16[256,1024]{1,0:T(8,128)(2,1)S(1)} %add_convert_fusion.6), channel_id=1, source_target_pairs={{1,2},{2,1},{5,6},{6,5},{9,10},{10,9},{13,14},{14,13},{17,18},{18,... | collective-permute-start | bytes 1572872 | tf_op jit(solution)/shard_map/ppermute | solution.py:278
  59.8 1.1 %collective-permute-done.12 = bf16[256,1024]{1,0:T(8,128)(2,1)S(1)} collective-permute-done((bf16[256,1024]{1,0:T(8,128)(2,1)S(1)}, bf16[256,1024]{1,0:T(8,128)(2,1)S(1)}, u32[]{:S(2)}, u32[]{:S(2)}) %collective-permute-start.12) | collective-permute-done | bytes 524320 | tf_op jit(solution)/shard_map/ppermute | solution.py:275
  60.9 0.2 add_convert_fusion.5
  61.1 3.5 %collective-permute-start.17 = (bf16[256,1024]{1,0:T(8,128)(2,1)S(1)}, bf16[256,1024]{1,0:T(8,128)(2,1)S(1)}, u32[]{:S(2)}, u32[]{:S(2)}) collective-permute-start(bf16[256,1024]{1,0:T(8,128)(2,1)S(1)} %add_convert_fusion.5), channel_id=1, source_target_pairs={{1,2},{2,1},{5,6},{6,5},{9,10},{10,9},{13,14},{14,13},{17,18},{18,... | collective-permute-start | bytes 1572872 | tf_op jit(solution)/shard_map/ppermute | solution.py:278
  64.6 1.3 %collective-permute-start.18 = (bf16[256,1024]{1,0:T(8,128)(2,1)S(1)}, bf16[256,1024]{1,0:T(8,128)(2,1)S(1)}, u32[]{:S(2)}, u32[]{:S(2)}) collective-permute-start(bf16[256,1024]{1,0:T(8,128)(2,1)S(1)} %project.10), channel_id=1, source_target_pairs={{0,1},{3,2},{4,5},{7,6},{8,9},{11,10},{12,13},{15,14},{16,17},{19,... | collective-permute-start | bytes 1572872 | tf_op jit(solution)/shard_map/ppermute | solution.py:275
  65.9 0.0 collective-permute-done.13
  65.9 0.2 add_convert_fusion.4
  66.1 6.0 %collective-permute-done.15 = bf16[256,1024]{1,0:T(8,128)(2,1)S(1)} collective-permute-done((bf16[256,1024]{1,0:T(8,128)(2,1)S(1)}, bf16[256,1024]{1,0:T(8,128)(2,1)S(1)}, u32[]{:S(2)}, u32[]{:S(2)}) %collective-permute-start.15) | collective-permute-done | bytes 524320 | tf_op jit(solution)/shard_map/ppermute | solution.py:275
  72.2 0.2 add_convert_fusion.3
  72.4 3.5 %collective-permute-start.20 = (bf16[256,1024]{1,0:T(8,128)(2,1)S(1)}, bf16[256,1024]{1,0:T(8,128)(2,1)S(1)}, u32[]{:S(2)}, u32[]{:S(2)}) collective-permute-start(bf16[256,1024]{1,0:T(8,128)(2,1)S(1)} %add_convert_fusion.3), channel_id=1, source_target_pairs={{1,2},{2,1},{5,6},{6,5},{9,10},{10,9},{13,14},{14,13},{17,18},{18,... | collective-permute-start | bytes 1572872 | tf_op jit(solution)/shard_map/ppermute | solution.py:278
  75.9 1.3 %collective-permute-start.21 = (bf16[256,1024]{1,0:T(8,128)(2,1)S(1)}, bf16[256,1024]{1,0:T(8,128)(2,1)S(1)}, u32[]{:S(2)}, u32[]{:S(2)}) collective-permute-start(bf16[256,1024]{1,0:T(8,128)(2,1)S(1)} %project.11), channel_id=1, source_target_pairs={{0,1},{3,2},{4,5},{7,6},{8,9},{11,10},{12,13},{15,14},{16,17},{19,... | collective-permute-start | bytes 1572872 | tf_op jit(solution)/shard_map/ppermute | solution.py:275
  77.2 0.0 collective-permute-done.16
  77.2 0.2 add_convert_fusion.2
  77.4 4.6 %collective-permute-start.19 = (bf16[256,1024]{1,0:T(8,128)(2,1)S(1)}, bf16[256,1024]{1,0:T(8,128)(2,1)S(1)}, u32[]{:S(2)}, u32[]{:S(2)}) collective-permute-start(bf16[256,1024]{1,0:T(8,128)(2,1)S(1)} %add_convert_fusion.2), channel_id=1, source_target_pairs={{1,0},{2,3},{5,4},{6,7},{9,8},{10,11},{13,12},{14,15},{17,16},{18,... | collective-permute-start | bytes 1572872 | tf_op jit(solution)/shard_map/ppermute | solution.py:281
  82.0 1.4 %collective-permute-done.18 = bf16[256,1024]{1,0:T(8,128)(2,1)S(1)} collective-permute-done((bf16[256,1024]{1,0:T(8,128)(2,1)S(1)}, bf16[256,1024]{1,0:T(8,128)(2,1)S(1)}, u32[]{:S(2)}, u32[]{:S(2)}) %collective-permute-start.18) | collective-permute-done | bytes 524320 | tf_op jit(solution)/shard_map/ppermute | solution.py:275
  83.4 0.9 collective-permute-done.17
  84.3 0.3 add_convert_fusion.1
  84.6 9.7 %collective-permute-done.21 = bf16[256,1024]{1,0:T(8,128)(2,1)S(1)} collective-permute-done((bf16[256,1024]{1,0:T(8,128)(2,1)S(1)}, bf16[256,1024]{1,0:T(8,128)(2,1)S(1)}, u32[]{:S(2)}, u32[]{:S(2)}) %collective-permute-start.21) | collective-permute-done | bytes 524320 | tf_op jit(solution)/shard_map/ppermute | solution.py:275
  94.3 0.4 add_convert_fusion
  94.6 1.1 %pad_maximum_fusion = bf16[256,2048]{1,0:T(8,128)(2,1)} fusion(bf16[256,1024]{1,0:T(8,128)(2,1)S(1)} %add_convert_fusion, bf16[256,1024]{1,0:T(8,128)(2,1)S(1)} %add_convert_fusion.1), kind=kLoop, calls=%fused_computation | loop fusion | flops 2097152 | bytes 2097152 | tf_op jit(solution)/shard_map/concatenate | solution.py:314
  (10 shorter events, 0.1 us)
Async XLA Ops:
  0.9 7.3 %collective-permute-start.1 = (bf16[1,256,256]{2,1,0:T(8,128)(2,1)S(1)}, bf16[1,256,256]{2,1,0:T(8,128)(2,1)S(1)}, u32[]{:S(2)}, u32[]{:S(2)}) collective-permute-start(bf16[1,256,256]{2,1,0:T(8,128)(2,1)S(1)} %get-tuple-element.53), channel_id=1, source_target_pairs={{0,24},{4,28},{8,16},{12,20},{16,8},{20,12},{24,0},{28,4},{1,25},{... | collective-permute-start | bytes 393224 | tf_op jit(solution)/shard_map/ppermute | solution.py:203
  1.5 7.5 %collective-permute-start.2 = (bf16[1,256,256]{2,1,0:T(8,128)(2,1)S(1)}, bf16[1,256,256]{2,1,0:T(8,128)(2,1)S(1)}, u32[]{:S(2)}, u32[]{:S(2)}) collective-permute-start(bf16[1,256,256]{2,1,0:T(8,128)(2,1)S(1)} %get-tuple-element.53), channel_id=1, source_target_pairs={{0,8},{4,12},{8,0},{12,4},{16,24},{20,28},{24,16},{28,20},{1,9},{5... | collective-permute-start | bytes 393224 | tf_op jit(solution)/shard_map/ppermute | solution.py:203
  3.0 7.0 %collective-permute-start.3 = (bf16[1,256,256]{2,1,0:T(8,128)(2,1)S(1)}, bf16[1,256,256]{2,1,0:T(8,128)(2,1)S(1)}, u32[]{:S(2)}, u32[]{:S(2)}) collective-permute-start(bf16[1,256,256]{2,1,0:T(8,128)(2,1)S(1)} %get-tuple-element.53), channel_id=1, source_target_pairs={{0,16},{4,20},{8,24},{12,28},{16,0},{20,4},{24,8},{28,12},{1,17},{... | collective-permute-start | bytes 393224 | tf_op jit(solution)/shard_map/ppermute | solution.py:203
  4.5 5.5 %collective-permute-start = (bf16[1,256,256]{2,1,0:T(8,128)(2,1)S(1)}, bf16[1,256,256]{2,1,0:T(8,128)(2,1)S(1)}, u32[]{:S(2)}, u32[]{:S(2)}) collective-permute-start(bf16[1,256,256]{2,1,0:T(8,128)(2,1)S(1)} %get-tuple-element.53), channel_id=1, source_target_pairs={{0,4},{4,0},{8,12},{12,8},{16,20},{20,16},{24,28},{28,24},{1,5},{5... | collective-permute-start | bytes 393224 | tf_op jit(solution)/shard_map/ppermute | solution.py:203
  8.3 6.4 %collective-permute-start.4 = (bf16[1,256,256]{2,1,0:T(8,128)(2,1)S(1)}, bf16[1,256,256]{2,1,0:T(8,128)(2,1)S(1)}, u32[]{:S(2)}, u32[]{:S(2)}) collective-permute-start(bf16[1,256,256]{2,1,0:T(8,128)(2,1)S(1)} %collective-permute-done.1.refs_3_), channel_id=1, source_target_pairs={{0,4},{4,0},{8,12},{12,8},{16,20},{20,16},{24,28},{28,24},{1,5},{5... | collective-permute-start | bytes 393224 | tf_op jit(solution)/shard_map/ppermute | solution.py:203
  9.0 5.7 %collective-permute-start.5 = (bf16[1,256,256]{2,1,0:T(8,128)(2,1)S(1)}, bf16[1,256,256]{2,1,0:T(8,128)(2,1)S(1)}, u32[]{:S(2)}, u32[]{:S(2)}) collective-permute-start(bf16[1,256,256]{2,1,0:T(8,128)(2,1)S(1)} %collective-permute-done.2.refs_4_), channel_id=1, source_target_pairs={{0,4},{4,0},{8,12},{12,8},{16,20},{20,16},{24,28},{28,24},{1,5},{5... | collective-permute-start | bytes 393224 | tf_op jit(solution)/shard_map/ppermute | solution.py:203
  9.9 4.7 %collective-permute-start.6 = (bf16[1,256,256]{2,1,0:T(8,128)(2,1)S(1)}, bf16[1,256,256]{2,1,0:T(8,128)(2,1)S(1)}, u32[]{:S(2)}, u32[]{:S(2)}) collective-permute-start(bf16[1,256,256]{2,1,0:T(8,128)(2,1)S(1)} %collective-permute-done.3.refs_5_), channel_id=1, source_target_pairs={{0,4},{4,0},{8,12},{12,8},{16,20},{20,16},{24,28},{28,24},{1,5},{5... | collective-permute-start | bytes 393224 | tf_op jit(solution)/shard_map/ppermute | solution.py:203
  9.9 1.0 %copy-start = (bf16[256,1024]{1,0:T(8,128)(2,1)S(1)}, bf16[256,1024]{1,0:T(8,128)(2,1)}, u32[]{:S(2)}) copy-start(bf16[256,1024]{1,0:T(8,128)(2,1)} %query_ref.1) | copy-start | bytes 1572868
  11.0 0.7 copy-start.1
  21.8 14.7 %collective-permute-start.7 = (bf16[256,512]{1,0:T(8,128)(2,1)S(1)}, bf16[256,512]{1,0:T(8,128)(2,1)S(1)}, u32[]{:S(2)}, u32[]{:S(2)}) collective-permute-start(bf16[256,512]{1,0:T(8,128)(2,1)S(1)} %project.8), channel_id=1, source_target_pairs={{0,1},{3,2},{4,5},{7,6},{8,9},{11,10},{12,13},{15,14},{16,17},{19,... | collective-permute-start | bytes 786440 | tf_op jit(solution)/shard_map/ppermute | solution.py:275
  24.8 13.6 %collective-permute-start.8 = (bf16[256,512]{1,0:T(8,128)(2,1)S(1)}, bf16[256,512]{1,0:T(8,128)(2,1)S(1)}, u32[]{:S(2)}, u32[]{:S(2)}) collective-permute-start(bf16[256,512]{1,0:T(8,128)(2,1)S(1)} %project.9), channel_id=1, source_target_pairs={{0,1},{3,2},{4,5},{7,6},{8,9},{11,10},{12,13},{15,14},{16,17},{19,... | collective-permute-start | bytes 786440 | tf_op jit(solution)/shard_map/ppermute | solution.py:275
  28.3 24.4 %collective-permute-start.9 = (bf16[256,1024]{1,0:T(8,128)(2,1)S(1)}, bf16[256,1024]{1,0:T(8,128)(2,1)S(1)}, u32[]{:S(2)}, u32[]{:S(2)}) collective-permute-start(bf16[256,1024]{1,0:T(8,128)(2,1)S(1)} %project.13), channel_id=1, source_target_pairs={{0,1},{3,2},{4,5},{7,6},{8,9},{11,10},{12,13},{15,14},{16,17},{19,... | collective-permute-start | bytes 1572872 | tf_op jit(solution)/shard_map/ppermute | solution.py:275
  31.8 29.1 %collective-permute-start.12 = (bf16[256,1024]{1,0:T(8,128)(2,1)S(1)}, bf16[256,1024]{1,0:T(8,128)(2,1)S(1)}, u32[]{:S(2)}, u32[]{:S(2)}) collective-permute-start(bf16[256,1024]{1,0:T(8,128)(2,1)S(1)} %project.14), channel_id=1, source_target_pairs={{0,1},{3,2},{4,5},{7,6},{8,9},{11,10},{12,13},{15,14},{16,17},{19,... | collective-permute-start | bytes 1572872 | tf_op jit(solution)/shard_map/ppermute | solution.py:275
  35.3 36.9 %collective-permute-start.15 = (bf16[256,1024]{1,0:T(8,128)(2,1)S(1)}, bf16[256,1024]{1,0:T(8,128)(2,1)S(1)}, u32[]{:S(2)}, u32[]{:S(2)}) collective-permute-start(bf16[256,1024]{1,0:T(8,128)(2,1)S(1)} %project.15), channel_id=1, source_target_pairs={{0,1},{3,2},{4,5},{7,6},{8,9},{11,10},{12,13},{15,14},{16,17},{19,... | collective-permute-start | bytes 1572872 | tf_op jit(solution)/shard_map/ppermute | solution.py:275
  38.5 14.5 %collective-permute-start.10 = (bf16[256,512]{1,0:T(8,128)(2,1)S(1)}, bf16[256,512]{1,0:T(8,128)(2,1)S(1)}, u32[]{:S(2)}, u32[]{:S(2)}) collective-permute-start(bf16[256,512]{1,0:T(8,128)(2,1)S(1)} %add_convert_fusion.10), channel_id=1, source_target_pairs={{1,2},{2,1},{5,6},{6,5},{9,10},{10,9},{13,14},{14,13},{17,18},{18,... | collective-permute-start | bytes 786440 | tf_op jit(solution)/shard_map/ppermute | solution.py:278
  42.0 11.6 %collective-permute-start.11 = (bf16[256,512]{1,0:T(8,128)(2,1)S(1)}, bf16[256,512]{1,0:T(8,128)(2,1)S(1)}, u32[]{:S(2)}, u32[]{:S(2)}) collective-permute-start(bf16[256,512]{1,0:T(8,128)(2,1)S(1)} %add_convert_fusion.9), channel_id=1, source_target_pairs={{1,2},{2,1},{5,6},{6,5},{9,10},{10,9},{13,14},{14,13},{17,18},{18,... | collective-permute-start | bytes 786440 | tf_op jit(solution)/shard_map/ppermute | solution.py:278
  53.7 10.9 %collective-permute-start.14 = (bf16[256,512]{1,0:T(8,128)(2,1)S(1)}, bf16[256,512]{1,0:T(8,128)(2,1)S(1)}, u32[]{:S(2)}, u32[]{:S(2)}) collective-permute-start(bf16[256,512]{1,0:T(8,128)(2,1)S(1)} %add_convert_fusion.7), channel_id=1, source_target_pairs={{1,0},{2,3},{5,4},{6,7},{9,8},{10,11},{13,12},{14,15},{17,16},{18,... | collective-permute-start | bytes 786440 | tf_op jit(solution)/shard_map/ppermute | solution.py:281
  55.0 10.9 %collective-permute-start.13 = (bf16[256,512]{1,0:T(8,128)(2,1)S(1)}, bf16[256,512]{1,0:T(8,128)(2,1)S(1)}, u32[]{:S(2)}, u32[]{:S(2)}) collective-permute-start(bf16[256,512]{1,0:T(8,128)(2,1)S(1)} %add_convert_fusion.8), channel_id=1, source_target_pairs={{1,0},{2,3},{5,4},{6,7},{9,8},{10,11},{13,12},{14,15},{17,16},{18,... | collective-permute-start | bytes 786440 | tf_op jit(solution)/shard_map/ppermute | solution.py:281
  56.3 20.8 %collective-permute-start.16 = (bf16[256,1024]{1,0:T(8,128)(2,1)S(1)}, bf16[256,1024]{1,0:T(8,128)(2,1)S(1)}, u32[]{:S(2)}, u32[]{:S(2)}) collective-permute-start(bf16[256,1024]{1,0:T(8,128)(2,1)S(1)} %add_convert_fusion.6), channel_id=1, source_target_pairs={{1,2},{2,1},{5,6},{6,5},{9,10},{10,9},{13,14},{14,13},{17,18},{18,... | collective-permute-start | bytes 1572872 | tf_op jit(solution)/shard_map/ppermute | solution.py:278
  61.1 23.2 %collective-permute-start.17 = (bf16[256,1024]{1,0:T(8,128)(2,1)S(1)}, bf16[256,1024]{1,0:T(8,128)(2,1)S(1)}, u32[]{:S(2)}, u32[]{:S(2)}) collective-permute-start(bf16[256,1024]{1,0:T(8,128)(2,1)S(1)} %add_convert_fusion.5), channel_id=1, source_target_pairs={{1,2},{2,1},{5,6},{6,5},{9,10},{10,9},{13,14},{14,13},{17,18},{18,... | collective-permute-start | bytes 1572872 | tf_op jit(solution)/shard_map/ppermute | solution.py:278
  64.6 18.8 %collective-permute-start.18 = (bf16[256,1024]{1,0:T(8,128)(2,1)S(1)}, bf16[256,1024]{1,0:T(8,128)(2,1)S(1)}, u32[]{:S(2)}, u32[]{:S(2)}) collective-permute-start(bf16[256,1024]{1,0:T(8,128)(2,1)S(1)} %project.10), channel_id=1, source_target_pairs={{0,1},{3,2},{4,5},{7,6},{8,9},{11,10},{12,13},{15,14},{16,17},{19,... | collective-permute-start | bytes 1572872 | tf_op jit(solution)/shard_map/ppermute | solution.py:275
  72.4 21.9 %collective-permute-start.20 = (bf16[256,1024]{1,0:T(8,128)(2,1)S(1)}, bf16[256,1024]{1,0:T(8,128)(2,1)S(1)}, u32[]{:S(2)}, u32[]{:S(2)}) collective-permute-start(bf16[256,1024]{1,0:T(8,128)(2,1)S(1)} %add_convert_fusion.3), channel_id=1, source_target_pairs={{1,2},{2,1},{5,6},{6,5},{9,10},{10,9},{13,14},{14,13},{17,18},{18,... | collective-permute-start | bytes 1572872 | tf_op jit(solution)/shard_map/ppermute | solution.py:278
  75.9 18.4 %collective-permute-start.21 = (bf16[256,1024]{1,0:T(8,128)(2,1)S(1)}, bf16[256,1024]{1,0:T(8,128)(2,1)S(1)}, u32[]{:S(2)}, u32[]{:S(2)}) collective-permute-start(bf16[256,1024]{1,0:T(8,128)(2,1)S(1)} %project.11), channel_id=1, source_target_pairs={{0,1},{3,2},{4,5},{7,6},{8,9},{11,10},{12,13},{15,14},{16,17},{19,... | collective-permute-start | bytes 1572872 | tf_op jit(solution)/shard_map/ppermute | solution.py:275
  77.4 16.9 %collective-permute-start.19 = (bf16[256,1024]{1,0:T(8,128)(2,1)S(1)}, bf16[256,1024]{1,0:T(8,128)(2,1)S(1)}, u32[]{:S(2)}, u32[]{:S(2)}) collective-permute-start(bf16[256,1024]{1,0:T(8,128)(2,1)S(1)} %add_convert_fusion.2), channel_id=1, source_target_pairs={{1,0},{2,3},{5,4},{6,7},{9,8},{10,11},{13,12},{14,15},{17,16},{18,... | collective-permute-start | bytes 1572872 | tf_op jit(solution)/shard_map/ppermute | solution.py:281

commit v4 on v3

--- a/solution.py
+++ b/solution.py
@@ -31,17 +31,11 @@
             found = found + here.astype(jnp.int32)
         return found
 
+    if not swaps:
+        return lax.fori_loop(0, owners, choose, jnp.int32(0))
     found = jnp.int32(0)
-    if swaps:
-        for slot in range(owners):
-            found = choose(slot, found)
-    else:
-        found = lax.fori_loop(0, owners, choose, found)
-
-    @pl.when(found % 2 == 1)
-    def _():
-        chosen[found] = chosen[found - 1]
-
+    for slot in range(owners):
+        found = choose(slot, found)
     return found
 
 
@@ -49,17 +43,25 @@
     if first:
         own_hbm, *refs = refs
         kv_refs = refs[:parts]
-        query_out, peaks_out, totals_out, sums_out, kv, scores, peak, chosen, arrived = refs[parts:]
+        query_out, peaks, totals, sums, kv, peak, scores, chosen, arrived = refs[parts:]
         loads = [pltpu.make_async_copy(query_ref, query_out, arrived.at[0])]
         if swaps:
             loads.append(pltpu.make_async_copy(own_hbm, kv.at[0], arrived.at[1]))
         for load in loads:
             load.start()
         at = len(loads) - 1
+        peaks[...] = jnp.full(peaks.shape, -1e30, jnp.float32)
+        totals[...] = jnp.zeros(totals.shape, jnp.float32)
+        sums[...] = jnp.zeros(sums.shape, jnp.float32)
     else:
-        peaks_in, totals_in, sums_in, *refs = refs
+        peaks, totals_in, sums_in, *refs = refs
         kv_refs = refs[:parts]
-        out_ref, kv, scores, peak, total, summed, chosen = refs[parts:]
+        weight_hbm, out_ref, partial_ref, kv, peak, scores, totals, sums, *refs = refs[parts:]
+        weight, chosen, arrived = refs
+        columns = weight.shape[1]
+        column = pl.multiple_of(place_ref[1] * columns, columns)
+        loads = [pltpu.make_async_copy(weight_hbm.at[:, pl.ds(column, columns)], weight, arrived)]
+        loads[0].start()
         at = 0
     for ref in kv_refs:
         count = ref.shape[0]
@@ -80,76 +82,83 @@
         found = choose_blocks(
             place, swaps, owners, place * per_device + block, per_device, mask_ref, chosen
         )
-        pairs = (found + 1) // 2
-
-        def tile(number):
-            index = chosen[number]
-            start = pl.multiple_of((index % per_device) * BLOCK, BLOCK)
-            return index // per_device, pl.ds(start, BLOCK)
-
-        if first:
-            total, summed = totals_out.at[block], sums_out.at[block]
-            peak[...] = jnp.full(peak.shape, -1e30, jnp.float32)
-            total[...] = jnp.zeros(total.shape, jnp.float32)
-            summed[...] = jnp.zeros(summed.shape, jnp.float32)
-        else:
-            peak[...] = peaks_in[block]
-
-        def score(pair, carry):
-            slot0, rows0 = tile(2 * pair)
-            slot1, rows1 = tile(2 * pair + 1)
-            keys = jnp.concatenate([kv[slot0, rows0, :HDIM], kv[slot1, rows1, :HDIM]], axis=0)
+
+        def tiles(start, count):
+            for number in range(count):
+                index = chosen[start + number]
+                here = pl.multiple_of((index % per_device) * BLOCK, BLOCK)
+                yield index // per_device, pl.ds(here, BLOCK)
+
+        def score(start, count):
+            keys = [kv[slot, here, :HDIM] for slot, here in tiles(start, count)]
+            keys = jnp.concatenate(keys, axis=0)
             for head in range(heads):
                 query = query_ref[top, head * HDIM : (head + 1) * HDIM]
-                here = lax.dot_general(
+                found_here = lax.dot_general(
                     query, keys, (((1,), (1,)), ((), ())), preferred_element_type=jnp.float32
                 )
-                scores[pair, head] = here
-                peak[head] = jnp.maximum(
-                    peak[head], jnp.maximum(here[:, :BLOCK], here[:, BLOCK:])
-                )
-            return carry
-
-        lax.fori_loop(0, pairs, score, 0)
-
-        @pl.when(found % 2 == 1)
-        def _():
-            scores[pairs - 1, :, :, BLOCK:] = jnp.full((heads, BLOCK, BLOCK), -1e30, jnp.float32)
-
+                highest = peak[head]
+                for number in range(count):
+                    part = found_here[:, number * BLOCK : (number + 1) * BLOCK]
+                    scores[start + number, head] = part
+                    highest = jnp.maximum(highest, part)
+                peak[head] = highest
+
+        def weigh(start, count):
+            values = [kv[slot, here, HDIM:] for slot, here in tiles(start, count)]
+            values = jnp.concatenate(values, axis=0)
+            for head in range(heads):
+                weights = [
+                    jnp.exp2((scores[start + number, head] - peak[head]) * EXPONENT)
+                    for number in range(count)
+                ]
+                totals[block, head] += sum(weights[1:], weights[0])
+                weights = jnp.concatenate([w.astype(jnp.bfloat16) for w in weights], axis=1)
+                sums[block, head] += jnp.dot(weights, values, preferred_element_type=jnp.float32)
+
+        def over_blocks(work):
+            def four(number, carry):
+                work(4 * number, 4)
+                return carry
+
+            lax.fori_loop(0, found // 4, four, 0)
+
+            @pl.when((found & 2) == 2)
+            def _():
+                work(found // 4 * 4, 2)
+
+            @pl.when((found & 1) == 1)
+            def _():
+                work(found - 1, 1)
+
+        peak[...] = peaks[block]
+        over_blocks(score)
         for head in range(heads):
             highest = jnp.max(peak[head], axis=1, keepdims=True)
             peak[head] = jnp.broadcast_to(highest, (BLOCK, BLOCK))
-            if not first:
-                factor = jnp.exp2((peaks_in[block, head] - peak[head]) * EXPONENT)
-                total[head] = totals_in[block, head] * factor
-                summed[head] = sums_in[block, head] * factor
-
-        def weigh(pair, carry):
-            slot0, rows0 = tile(2 * pair)
-            slot1, rows1 = tile(2 * pair + 1)
-            values = jnp.concatenate([kv[slot0, rows0, HDIM:], kv[slot1, rows1, HDIM:]], axis=0)
+            if first:
+                peaks[block, head] = peak[head]
+            else:
+                factor = jnp.exp2((peaks[block, head] - peak[head]) * EXPONENT)
+                totals[block, head] = totals_in[block, head] * factor
+                sums[block, head] = sums_in[block, head] * factor
+        over_blocks(weigh)
+
+        if not first:
             for head in range(heads):
-                highest = peak[head]
-                left = jnp.exp2((scores[pair, head, :, :BLOCK] - highest) * EXPONENT)
-                right = jnp.exp2((scores[pair, head, :, BLOCK:] - highest) * EXPONENT)
-                total[head] += left + right
-                weights = jnp.concatenate([left, right], axis=1).astype(jnp.bfloat16)
-                summed[head] += jnp.dot(weights, values, preferred_element_type=jnp.float32)
-            return carry
-
-        lax.fori_loop(0, pairs, weigh, 0)
-
-        if first:
-            peaks_out[block] = peak[...]
-        else:
-            for head in range(heads):
-                norm = jnp.sum(total[head], axis=1, keepdims=True)
-                out_ref[top, head * HDIM : (head + 1) * HDIM] = (summed[head] / norm).astype(
+                norm = jnp.sum(totals[block, head], axis=1, keepdims=True)
+                out_ref[top, head * HDIM : (head + 1) * HDIM] = (sums[block, head] / norm).astype(
                     jnp.bfloat16
                 )
 
-
-def attention_part(first, swaps, count, place, storm_mask, query, state, parts):
+    if not first:
+        loads[0].wait()
+        partial_ref[...] = jnp.dot(
+            out_ref[...], weight[...], preferred_element_type=jnp.float32
+        ).astype(jnp.bfloat16)
+
+
+def attention_part(first, swaps, count, place, storm_mask, query, state, parts, *projection):
     rows, width = query.shape
     heads = width // HDIM
     blocks = count * (rows // BLOCK)
@@ -159,35 +168,38 @@
     taken = jax.ShapeDtypeStruct((rows, width), jnp.bfloat16)
     scratch = [
         pltpu.VMEM((count, rows, 2 * HDIM), jnp.bfloat16),
-        pltpu.VMEM(((blocks + 1) // 2, heads, BLOCK, 2 * BLOCK), jnp.float32),
         pltpu.VMEM((heads, BLOCK, BLOCK), jnp.float32),
+        pltpu.VMEM((blocks, heads, BLOCK, BLOCK), jnp.float32),
     ]
     if first:
         specs = [hbm, hbm] + [vmem] * len(parts)
         out_shape = [taken] + [jax.ShapeDtypeStruct(running, jnp.float32)] * 3
     else:
-        specs = [vmem] * (4 + len(parts))
-        out_shape = taken
-        scratch += [pltpu.VMEM((heads, BLOCK, BLOCK), jnp.float32)] * 2
-    scratch += [pltpu.SMEM((blocks + 2,), jnp.int32)]
-    if first:
-        scratch += [pltpu.SemaphoreType.DMA((2,))]
+        weight, column, columns = projection
+        place = jnp.stack([place, column // columns])
+        parts = [*parts, weight]
+        specs = [vmem] * (3 + len(parts)) + [hbm]
+        out_shape = [taken, jax.ShapeDtypeStruct((rows, columns), jnp.bfloat16)]
+        scratch += [pltpu.VMEM(running, jnp.float32)] * 2
+        scratch += [pltpu.VMEM((weight.shape[0], columns), jnp.bfloat16)]
+    scratch += [pltpu.SMEM((blocks + 1,), jnp.int32)]
+    scratch += [pltpu.SemaphoreType.DMA((2,)) if first else pltpu.SemaphoreType.DMA]
     return pl.pallas_call(
-        functools.partial(attention_kernel, len(parts), swaps, first),
+        functools.partial(attention_kernel, len(parts) - len(projection[:1]), swaps, first),
         grid_spec=pltpu.PrefetchScalarGridSpec(
             num_scalar_prefetch=2,
             grid=(1,),
             in_specs=specs,
-            out_specs=[vmem] * 4 if first else vmem,
+            out_specs=[vmem] * len(out_shape),
             scratch_shapes=scratch,
         ),
         out_shape=out_shape,
         compiler_params=pltpu.CompilerParams(vmem_limit_bytes=VMEM_LIMIT),
         name="attend_first" if first else "attend_rest",
-    )(place.astype(jnp.int32).reshape(1), storm_mask, query, *state, *parts)
-
-
-def attend(queries, packed, place, devices, storm_mask):
+    )(place.astype(jnp.int32).reshape(-1), storm_mask, query, *state, *parts)
+
+
+def attend(queries, packed, place, devices, storm_mask, *projection):
     if devices != 8:
         everyone = lax.all_gather(packed, "ctx", axis=0, tiled=False)
         state = attention_part(
@@ -196,7 +208,7 @@
         query, *state = state
         nothing = jnp.zeros_like(storm_mask)
         return attention_part(
-            False, (), 1, place, nothing, query, state, [everyone[:1]]
+            False, (), 1, place, nothing, query, state, [everyone[:1]], *projection
         )
 
     def swap(array, bits):
@@ -208,7 +220,7 @@
     )
     other = [swap(array, 1) for array in near]
     return attention_part(
-        False, (6, 2, 4, 7, 3, 5), 6, place, storm_mask, query, state, near + other
+        False, (6, 2, 4, 7, 3, 5), 6, place, storm_mask, query, state, near + other, *projection
     )
 
 
@@ -247,7 +259,7 @@
     return functools.reduce(lambda a, b: a + b, wide).astype(jnp.bfloat16)
 
 
-def line_sum(attended, out_weight):
+def line_sum(attend_now, out_weight):
     place = lax.axis_index("tp")
     quarter = out_weight.shape[1] // 4
     upper = place >= 2
@@ -259,7 +271,8 @@
     fourth = quarter // 4
     pieces = ((0, fourth), (fourth, fourth), (half, half))
     halves = ((0, half), (half, half))
-    projected, chain = [], []
+    attended, partial = attend_now(far_outer, fourth)
+    projected, chain = [partial], []
 
     def part(first, columns):
         source = after(attended, projected[-1]) if projected else attended
@@ -280,7 +293,7 @@
     def outward(array):
         return lax.ppermute(array, "tp", [(1, 0), (2, 3)])
 
-    outer_parts = [part(far_outer + at, size) for at, size in pieces]
+    outer_parts = [partial] + [part(far_outer + at, size) for at, size in pieces[1:]]
     outer_sums = [inward(array) for array in outer_parts]
     inner_parts = [part(far_inner + at, size) for at, size in halves]
     inner_sums = [inward(array) for array in inner_parts]
@@ -319,10 +332,15 @@
     heads = queries.shape[1] // HDIM
     shared_head = lax.axis_index("tp") * heads // GQ
     packed = pack_head(keys, values, shared_head)
-    attended = attend(queries, packed, place, mesh.shape["ctx"], storm_mask)
+
+    def attend_now(first, columns):
+        return attend(
+            queries, packed, place, mesh.shape["ctx"], storm_mask, out_weight, first, columns
+        )
+
     if mesh.shape["tp"] == 4:
-        return line_sum(attended, out_weight)
-    partial = project(attended, out_weight, jnp.int32(0), out_weight.shape[1])
+        return line_sum(attend_now, out_weight)
+    _, partial = attend_now(jnp.int32(0), out_weight.shape[1])
     return lax.psum_scatter(partial, "tp", scatter_dimension=1, tiled=True)
 
 

time: 97.1 us -> 94.7 us (0.975)
  the two profiles are of different devices: /device:TPU:14 before, /device:TPU:0 now
where the time goes in v4:
time: 94.7 us; the launch traced here: 93.5 us
  waiting for transfers between devices  33.7 us (36%)
  starting transfers between devices  32.2 us (34%)
  Pallas kernels  21.5 us (23%)
  other arithmetic  2.97 us (3%)
  local copies, waits for them, and re-layouts  2.73 us (3%)
    ppermute x7, waiting for transfers between devices, inward(): return lax.ppermute(array, 'tp', [(0, 1), (3, 2)])  22.3 us
    ppermute x7, starting transfers between devices, inward(): return lax.ppermute(array, 'tp', [(0, 1), (3, 2)])  19.6 us
    pallas_call x7, Pallas kernels, project(): pl.pallas_call(project_kernel, grid_spec=pltpu.PrefetchScalarGridSpec(num...  16.4 us
    ppermute x7, waiting for transfers between devices, swap(): return lax.ppermute(array, 'ctx', [(i, i ^ bits) for i in range(devices)])  5.92 us
    ppermute x3, waiting for transfers between devices, outward(): return lax.ppermute(array, 'tp', [(1, 0), (2, 3)])  5.44 us
    pallas_call x2, Pallas kernels, attention_part(): pl.pallas_call(functools.partial(attention_kernel, len(parts) - len(proje...  5.17 us
    ppermute x7, starting transfers between devices, swap(): return lax.ppermute(array, 'ctx', [(i, i ^ bits) for i in range(devices)])  5.12 us
    ppermute x3, starting transfers between devices, outward(): return lax.ppermute(array, 'tp', [(1, 0), (2, 3)])  3.88 us
  transfers between devices with their start and end apart: 22, of which 9 were waited for; matrix products, arithmetic and copies ran while one was open for 2% of the time, Pallas kernels for 21%

profile of v4, /device:TPU:0, one launch (start us, length us, event | category | flops | bytes accessed | tf_op | source)
XLA Modules:
  0.0 93.5 jit_solution(12914547396880182168)
XLA Ops:
  0.0 0.9 constant_dynamic-slice_fusion
  0.9 4.0 %collective-permute-start.1 = (bf16[1,256,256]{2,1,0:T(8,128)(2,1)S(1)}, bf16[1,256,256]{2,1,0:T(8,128)(2,1)S(1)}, u32[]{:S(2)}, u32[]{:S(2)}) collective-permute-start(bf16[1,256,256]{2,1,0:T(8,128)(2,1)S(1)} %get-tuple-element.56), channel_id=1, source_target_pairs={{0,24},{4,28},{8,16},{12,20},{16,8},{20,12},{24,0},{28,4},{1,25},{... | collective-permute-start | bytes 393224 | tf_op jit(solution)/shard_map/ppermute | solution.py:215
  4.9 0.5 collective-permute-start.2
  5.4 0.1 collective-permute-start.3
  5.5 3.7 %collective-permute-done.1.refs_3_ = bf16[1,256,256]{2,1,0:T(8,128)(2,1)S(1)} collective-permute-done((bf16[1,256,256]{2,1,0:T(8,128)(2,1)S(1)}, bf16[1,256,256]{2,1,0:T(8,128)(2,1)S(1)}, u32[]{:S(2)}, u32[]{:S(2)}) %collective-permute-start.1) | collective-permute-done | bytes 131104 | tf_op jit(solution)/shard_map/ppermute | solution.py:215
  9.2 0.0 collective-permute-start.4
  9.2 2.2 %collective-permute-done.2.refs_4_ = bf16[1,256,256]{2,1,0:T(8,128)(2,1)S(1)} collective-permute-done((bf16[1,256,256]{2,1,0:T(8,128)(2,1)S(1)}, bf16[1,256,256]{2,1,0:T(8,128)(2,1)S(1)}, u32[]{:S(2)}, u32[]{:S(2)}) %collective-permute-start.2) | collective-permute-done | bytes 131104 | tf_op jit(solution)/shard_map/ppermute | solution.py:215
  11.4 0.0 collective-permute-start.5
  11.4 0.5 collective-permute-start.6
  11.9 0.1 pad_add_fusion.place_ref
  12.0 0.0 collective-permute-done.refs_1_
  12.0 1.0 %copy-done = bf16[256,1024]{1,0:T(8,128)(2,1)S(1)} copy-done((bf16[256,1024]{1,0:T(8,128)(2,1)S(1)}, bf16[256,1024]{1,0:T(8,128)(2,1)}, u32[]{:S(2)}) %copy-start) | copy-done | bytes 524312
  13.1 0.7 copy-done.1
  13.8 2.8 %attend_first.1 = (bf16[256,1024]{1,0:T(8,128)(2,1)S(1)}, f32[2,8,128,128]{3,2,1,0:T(8,128)S(1)}, f32[2,8,128,128]{3,2,1,0:T(8,128)S(1)}, f32[2,8,128,128]{3,2,1,0:T(8,128)S(1)}) custom-call(s32[1]{0:T(128)} %bitcast.1.place_ref, s32[16,16]{1,0:T(8,128)S(1)} %copy-done.1, bf16[256,1024]{1,0:T(8,128)(2,1)S(1)} %copy-done, ...), custom_call_target="tpu_custom_call" | custom-call | tf_op jit(solution)/shard_map/attend_first/pallas_call | solution.py:187
  16.6 0.0 collective-permute-done.5.refs_7_
  16.6 0.0 collective-permute-done.6.refs_8_
  16.6 2.3 %attend_rest.1 = (bf16[256,1024]{1,0:T(8,128)(2,1)S(1)}, bf16[256,512]{1,0:T(8,128)(2,1)S(1)}) custom-call(s32[2]{0:T(128)S(1)} %pad_add_fusion.place_ref, s32[16,16]{1,0:T(8,128)S(1)} %copy-done.1, bf16[256,1024]{1,0:T(8,128)(2,1)S(1)} %get-tuple-element.29.query_ref, f32[2,8,128,128]{3,2,1,0:T(8,128)S(1)} %get-tuple-element.30.refs_0_, ...), custom_call_target="tpu_custom_call" | custom-call | tf_op jit(solution)/shard_map/attend_rest/pallas_call | solution.py:187
  19.0 3.5 %collective-permute-start.7 = (bf16[256,512]{1,0:T(8,128)(2,1)S(1)}, bf16[256,512]{1,0:T(8,128)(2,1)S(1)}, u32[]{:S(2)}, u32[]{:S(2)}) collective-permute-start(bf16[256,512]{1,0:T(8,128)(2,1)S(1)} %get-tuple-element.34), channel_id=1, source_target_pairs={{0,1},{3,2},{4,5},{7,6},{8,9},{11,10},{12,13},{15,14},{16,17},{19,... | collective-permute-start | bytes 786440 | tf_op jit(solution)/shard_map/ppermute | solution.py:288
  22.5 1.7 %project.7 = bf16[256,512]{1,0:T(8,128)(2,1)S(1)} custom-call(s32[1]{0:T(128)} %bitcast.6.first_ref, bf16[256,1024]{1,0:T(8,128)(2,1)S(1)} %get-tuple-element.38.attended_ref, bf16[1024,8192]{1,0:T(8,128)(2,1)} %weight_ref.13), custom_call_target="tpu_custom_call" | custom-call | tf_op jit(solution)/shard_map/project/pallas_call | solution.py:236
  24.2 1.3 %collective-permute-start.8 = (bf16[256,512]{1,0:T(8,128)(2,1)S(1)}, bf16[256,512]{1,0:T(8,128)(2,1)S(1)}, u32[]{:S(2)}, u32[]{:S(2)}) collective-permute-start(bf16[256,512]{1,0:T(8,128)(2,1)S(1)} %project.7), channel_id=1, source_target_pairs={{0,1},{3,2},{4,5},{7,6},{8,9},{11,10},{12,13},{15,14},{16,17},{19,... | collective-permute-start | bytes 786440 | tf_op jit(solution)/shard_map/ppermute | solution.py:288
  25.5 2.2 %project.11 = bf16[256,1024]{1,0:T(8,128)(2,1)S(1)} custom-call(s32[1]{0:T(128)} %bitcast.8.first_ref, bf16[256,1024]{1,0:T(8,128)(2,1)S(1)} %get-tuple-element.38.attended_ref, bf16[1024,8192]{1,0:T(8,128)(2,1)} %weight_ref.13), custom_call_target="tpu_custom_call" | custom-call | tf_op jit(solution)/shard_map/project/pallas_call | solution.py:236
  27.7 1.3 %collective-permute-start.9 = (bf16[256,1024]{1,0:T(8,128)(2,1)S(1)}, bf16[256,1024]{1,0:T(8,128)(2,1)S(1)}, u32[]{:S(2)}, u32[]{:S(2)}) collective-permute-start(bf16[256,1024]{1,0:T(8,128)(2,1)S(1)} %project.11), channel_id=1, source_target_pairs={{0,1},{3,2},{4,5},{7,6},{8,9},{11,10},{12,13},{15,14},{16,17},{19,... | collective-permute-start | bytes 1572872 | tf_op jit(solution)/shard_map/ppermute | solution.py:288
  29.0 2.2 %project.12 = bf16[256,1024]{1,0:T(8,128)(2,1)S(1)} custom-call(s32[1]{0:T(128)} %bitcast.7.first_ref, bf16[256,1024]{1,0:T(8,128)(2,1)S(1)} %get-tuple-element.38.attended_ref, bf16[1024,8192]{1,0:T(8,128)(2,1)} %weight_ref.13), custom_call_target="tpu_custom_call" | custom-call | tf_op jit(solution)/shard_map/project/pallas_call | solution.py:236
  31.2 1.3 %collective-permute-start.12 = (bf16[256,1024]{1,0:T(8,128)(2,1)S(1)}, bf16[256,1024]{1,0:T(8,128)(2,1)S(1)}, u32[]{:S(2)}, u32[]{:S(2)}) collective-permute-start(bf16[256,1024]{1,0:T(8,128)(2,1)S(1)} %project.12), channel_id=1, source_target_pairs={{0,1},{3,2},{4,5},{7,6},{8,9},{11,10},{12,13},{15,14},{16,17},{19,... | collective-permute-start | bytes 1572872 | tf_op jit(solution)/shard_map/ppermute | solution.py:288
  32.5 2.2 %project.13 = bf16[256,1024]{1,0:T(8,128)(2,1)S(1)} custom-call(s32[1]{0:T(128)} %bitcast.9.first_ref, bf16[256,1024]{1,0:T(8,128)(2,1)S(1)} %get-tuple-element.38.attended_ref, bf16[1024,8192]{1,0:T(8,128)(2,1)} %weight_ref.13), custom_call_target="tpu_custom_call" | custom-call | tf_op jit(solution)/shard_map/project/pallas_call | solution.py:236
  34.7 1.3 %collective-permute-start.15 = (bf16[256,1024]{1,0:T(8,128)(2,1)S(1)}, bf16[256,1024]{1,0:T(8,128)(2,1)S(1)}, u32[]{:S(2)}, u32[]{:S(2)}) collective-permute-start(bf16[256,1024]{1,0:T(8,128)(2,1)S(1)} %project.13), channel_id=1, source_target_pairs={{0,1},{3,2},{4,5},{7,6},{8,9},{11,10},{12,13},{15,14},{16,17},{19,... | collective-permute-start | bytes 1572872 | tf_op jit(solution)/shard_map/ppermute | solution.py:288
  36.0 0.0 collective-permute-done.7
  36.0 0.1 add_convert_fusion.10
  36.1 0.0 collective-permute-done.8
  36.1 0.1 add_convert_fusion.9
  36.2 0.7 collective-permute-start.10
  36.9 0.9 collective-permute-start.11
  37.8 2.2 %project.8 = bf16[256,1024]{1,0:T(8,128)(2,1)S(1)} custom-call(s32[1]{0:T(128)} %bitcast.5.first_ref, bf16[256,1024]{1,0:T(8,128)(2,1)S(1)} %get-tuple-element.38.attended_ref, bf16[1024,8192]{1,0:T(8,128)(2,1)} %weight_ref.13), custom_call_target="tpu_custom_call" | custom-call | tf_op jit(solution)/shard_map/project/pallas_call | solution.py:236
  39.9 2.2 %project.9 = bf16[256,1024]{1,0:T(8,128)(2,1)S(1)} custom-call(s32[1]{0:T(128)} %bitcast.4.first_ref, bf16[256,1024]{1,0:T(8,128)(2,1)S(1)} %get-tuple-element.38.attended_ref, bf16[1024,8192]{1,0:T(8,128)(2,1)} %weight_ref.13), custom_call_target="tpu_custom_call" | custom-call | tf_op jit(solution)/shard_map/project/pallas_call | solution.py:236
  42.1 3.9 %project.10 = bf16[256,2048]{1,0:T(8,128)(2,1)S(1)} custom-call(s32[1]{0:T(128)} %bitcast.first_ref, bf16[256,1024]{1,0:T(8,128)(2,1)S(1)} %get-tuple-element.38.attended_ref, bf16[1024,8192]{1,0:T(8,128)(2,1)} %weight_ref.13), custom_call_target="tpu_custom_call" | custom-call | tf_op jit(solution)/shard_map/project/pallas_call | solution.py:236
  46.1 0.1 fusion.1
  46.1 0.2 add_convert_fusion.6
  46.4 0.1 add_convert_fusion.8
  46.4 0.0 collective-permute-done.11
  46.4 0.1 add_convert_fusion.7
  46.5 1.3 %collective-permute-start.14 = (bf16[256,512]{1,0:T(8,128)(2,1)S(1)}, bf16[256,512]{1,0:T(8,128)(2,1)S(1)}, u32[]{:S(2)}, u32[]{:S(2)}) collective-permute-start(bf16[256,512]{1,0:T(8,128)(2,1)S(1)} %add_convert_fusion.7), channel_id=1, source_target_pairs={{1,0},{2,3},{5,4},{6,7},{9,8},{10,11},{13,12},{14,15},{17,16},{18,... | collective-permute-start | bytes 786440 | tf_op jit(solution)/shard_map/ppermute | solution.py:294
  47.8 1.3 %collective-permute-start.13 = (bf16[256,512]{1,0:T(8,128)(2,1)S(1)}, bf16[256,512]{1,0:T(8,128)(2,1)S(1)}, u32[]{:S(2)}, u32[]{:S(2)}) collective-permute-start(bf16[256,512]{1,0:T(8,128)(2,1)S(1)} %add_convert_fusion.8), channel_id=1, source_target_pairs={{1,0},{2,3},{5,4},{6,7},{9,8},{10,11},{13,12},{14,15},{17,16},{18,... | collective-permute-start | bytes 786440 | tf_op jit(solution)/shard_map/ppermute | solution.py:294
  49.1 0.7 collective-permute-start.16
  49.8 7.4 %collective-permute-done.12 = bf16[256,1024]{1,0:T(8,128)(2,1)S(1)} collective-permute-done((bf16[256,1024]{1,0:T(8,128)(2,1)S(1)}, bf16[256,1024]{1,0:T(8,128)(2,1)S(1)}, u32[]{:S(2)}, u32[]{:S(2)}) %collective-permute-start.12) | collective-permute-done | bytes 524320 | tf_op jit(solution)/shard_map/ppermute | solution.py:288
  57.2 0.2 add_convert_fusion.5
  57.4 0.7 collective-permute-start.17
  58.1 3.6 %collective-permute-done.14 = bf16[256,512]{1,0:T(8,128)(2,1)S(1)} collective-permute-done((bf16[256,512]{1,0:T(8,128)(2,1)S(1)}, bf16[256,512]{1,0:T(8,128)(2,1)S(1)}, u32[]{:S(2)}, u32[]{:S(2)}) %collective-permute-start.14) | collective-permute-done | bytes 262176 | tf_op jit(solution)/shard_map/ppermute | solution.py:294
  61.7 3.6 %collective-permute-start.18 = (bf16[256,1024]{1,0:T(8,128)(2,1)S(1)}, bf16[256,1024]{1,0:T(8,128)(2,1)S(1)}, u32[]{:S(2)}, u32[]{:S(2)}) collective-permute-start(bf16[256,1024]{1,0:T(8,128)(2,1)S(1)} %project.8), channel_id=1, source_target_pairs={{0,1},{3,2},{4,5},{7,6},{8,9},{11,10},{12,13},{15,14},{16,17},{19,... | collective-permute-start | bytes 1572872 | tf_op jit(solution)/shard_map/ppermute | solution.py:288
  65.3 0.6 collective-permute-done.13
  66.0 0.2 add_convert_fusion.4
  66.1 2.3 %collective-permute-done.15 = bf16[256,1024]{1,0:T(8,128)(2,1)S(1)} collective-permute-done((bf16[256,1024]{1,0:T(8,128)(2,1)S(1)}, bf16[256,1024]{1,0:T(8,128)(2,1)S(1)}, u32[]{:S(2)}, u32[]{:S(2)}) %collective-permute-start.15) | collective-permute-done | bytes 524320 | tf_op jit(solution)/shard_map/ppermute | solution.py:288
  68.5 0.2 add_convert_fusion.3
  68.7 0.7 collective-permute-start.20
  69.4 7.2 %collective-permute-start.21 = (bf16[256,1024]{1,0:T(8,128)(2,1)S(1)}, bf16[256,1024]{1,0:T(8,128)(2,1)S(1)}, u32[]{:S(2)}, u32[]{:S(2)}) collective-permute-start(bf16[256,1024]{1,0:T(8,128)(2,1)S(1)} %project.9), channel_id=1, source_target_pairs={{0,1},{3,2},{4,5},{7,6},{8,9},{11,10},{12,13},{15,14},{16,17},{19,... | collective-permute-start | bytes 1572872 | tf_op jit(solution)/shard_map/ppermute | solution.py:288
  76.6 0.2 add_convert_fusion.2
  76.8 1.3 %collective-permute-start.19 = (bf16[256,1024]{1,0:T(8,128)(2,1)S(1)}, bf16[256,1024]{1,0:T(8,128)(2,1)S(1)}, u32[]{:S(2)}, u32[]{:S(2)}) collective-permute-start(bf16[256,1024]{1,0:T(8,128)(2,1)S(1)} %add_convert_fusion.2), channel_id=1, source_target_pairs={{1,0},{2,3},{5,4},{6,7},{9,8},{10,11},{13,12},{14,15},{17,16},{18,... | collective-permute-start | bytes 1572872 | tf_op jit(solution)/shard_map/ppermute | solution.py:294
  78.1 1.6 %collective-permute-done.18 = bf16[256,1024]{1,0:T(8,128)(2,1)S(1)} collective-permute-done((bf16[256,1024]{1,0:T(8,128)(2,1)S(1)}, bf16[256,1024]{1,0:T(8,128)(2,1)S(1)}, u32[]{:S(2)}, u32[]{:S(2)}) %collective-permute-start.18) | collective-permute-done | bytes 524320 | tf_op jit(solution)/shard_map/ppermute | solution.py:288
  79.7 0.0 collective-permute-done.17
  79.7 0.3 add_convert_fusion.1
  80.0 11.0 %collective-permute-done.21 = bf16[256,1024]{1,0:T(8,128)(2,1)S(1)} collective-permute-done((bf16[256,1024]{1,0:T(8,128)(2,1)S(1)}, bf16[256,1024]{1,0:T(8,128)(2,1)S(1)}, u32[]{:S(2)}, u32[]{:S(2)}) %collective-permute-start.21) | collective-permute-done | bytes 524320 | tf_op jit(solution)/shard_map/ppermute | solution.py:288
  90.9 0.0 collective-permute-done.20
  90.9 1.2 %collective-permute-done.19 = bf16[256,1024]{1,0:T(8,128)(2,1)S(1)} collective-permute-done((bf16[256,1024]{1,0:T(8,128)(2,1)S(1)}, bf16[256,1024]{1,0:T(8,128)(2,1)S(1)}, u32[]{:S(2)}, u32[]{:S(2)}) %collective-permute-start.19) | collective-permute-done | bytes 524320 | tf_op jit(solution)/shard_map/ppermute | solution.py:294
  92.1 0.4 add_convert_fusion
  92.5 1.1 %pad_maximum_fusion = bf16[256,2048]{1,0:T(8,128)(2,1)} fusion(bf16[256,1024]{1,0:T(8,128)(2,1)S(1)} %add_convert_fusion, bf16[256,1024]{1,0:T(8,128)(2,1)S(1)} %add_convert_fusion.1), kind=kLoop, calls=%fused_computation | loop fusion | flops 2097152 | bytes 2097152 | tf_op jit(solution)/shard_map/concatenate | solution.py:327
  (10 shorter events, 0.1 us)
Async XLA Ops:
  0.9 8.3 %collective-permute-start.1 = (bf16[1,256,256]{2,1,0:T(8,128)(2,1)S(1)}, bf16[1,256,256]{2,1,0:T(8,128)(2,1)S(1)}, u32[]{:S(2)}, u32[]{:S(2)}) collective-permute-start(bf16[1,256,256]{2,1,0:T(8,128)(2,1)S(1)} %get-tuple-element.56), channel_id=1, source_target_pairs={{0,24},{4,28},{8,16},{12,20},{16,8},{20,12},{24,0},{28,4},{1,25},{... | collective-permute-start | bytes 393224 | tf_op jit(solution)/shard_map/ppermute | solution.py:215
  4.9 6.6 %collective-permute-start.2 = (bf16[1,256,256]{2,1,0:T(8,128)(2,1)S(1)}, bf16[1,256,256]{2,1,0:T(8,128)(2,1)S(1)}, u32[]{:S(2)}, u32[]{:S(2)}) collective-permute-start(bf16[1,256,256]{2,1,0:T(8,128)(2,1)S(1)} %get-tuple-element.56), channel_id=1, source_target_pairs={{0,8},{4,12},{8,0},{12,4},{16,24},{20,28},{24,16},{28,20},{1,9},{5... | collective-permute-start | bytes 393224 | tf_op jit(solution)/shard_map/ppermute | solution.py:215
  5.4 6.0 %collective-permute-start.3 = (bf16[1,256,256]{2,1,0:T(8,128)(2,1)S(1)}, bf16[1,256,256]{2,1,0:T(8,128)(2,1)S(1)}, u32[]{:S(2)}, u32[]{:S(2)}) collective-permute-start(bf16[1,256,256]{2,1,0:T(8,128)(2,1)S(1)} %get-tuple-element.56), channel_id=1, source_target_pairs={{0,16},{4,20},{8,24},{12,28},{16,0},{20,4},{24,8},{28,12},{1,17},{... | collective-permute-start | bytes 393224 | tf_op jit(solution)/shard_map/ppermute | solution.py:215
  5.5 6.5 %collective-permute-start = (bf16[1,256,256]{2,1,0:T(8,128)(2,1)S(1)}, bf16[1,256,256]{2,1,0:T(8,128)(2,1)S(1)}, u32[]{:S(2)}, u32[]{:S(2)}) collective-permute-start(bf16[1,256,256]{2,1,0:T(8,128)(2,1)S(1)} %get-tuple-element.56), channel_id=1, source_target_pairs={{0,4},{4,0},{8,12},{12,8},{16,20},{20,16},{24,28},{28,24},{1,5},{5... | collective-permute-start | bytes 393224 | tf_op jit(solution)/shard_map/ppermute | solution.py:215
  9.2 7.4 %collective-permute-start.4 = (bf16[1,256,256]{2,1,0:T(8,128)(2,1)S(1)}, bf16[1,256,256]{2,1,0:T(8,128)(2,1)S(1)}, u32[]{:S(2)}, u32[]{:S(2)}) collective-permute-start(bf16[1,256,256]{2,1,0:T(8,128)(2,1)S(1)} %collective-permute-done.1.refs_3_), channel_id=1, source_target_pairs={{0,4},{4,0},{8,12},{12,8},{16,20},{20,16},{24,28},{28,24},{1,5},{5... | collective-permute-start | bytes 393224 | tf_op jit(solution)/shard_map/ppermute | solution.py:215
  11.4 5.2 %collective-permute-start.5 = (bf16[1,256,256]{2,1,0:T(8,128)(2,1)S(1)}, bf16[1,256,256]{2,1,0:T(8,128)(2,1)S(1)}, u32[]{:S(2)}, u32[]{:S(2)}) collective-permute-start(bf16[1,256,256]{2,1,0:T(8,128)(2,1)S(1)} %collective-permute-done.2.refs_4_), channel_id=1, source_target_pairs={{0,4},{4,0},{8,12},{12,8},{16,20},{20,16},{24,28},{28,24},{1,5},{5... | collective-permute-start | bytes 393224 | tf_op jit(solution)/shard_map/ppermute | solution.py:215
  11.4 5.2 %collective-permute-start.6 = (bf16[1,256,256]{2,1,0:T(8,128)(2,1)S(1)}, bf16[1,256,256]{2,1,0:T(8,128)(2,1)S(1)}, u32[]{:S(2)}, u32[]{:S(2)}) collective-permute-start(bf16[1,256,256]{2,1,0:T(8,128)(2,1)S(1)} %collective-permute-done.3.refs_5_), channel_id=1, source_target_pairs={{0,4},{4,0},{8,12},{12,8},{16,20},{20,16},{24,28},{28,24},{1,5},{5... | collective-permute-start | bytes 393224 | tf_op jit(solution)/shard_map/ppermute | solution.py:215
  12.0 1.0 %copy-start = (bf16[256,1024]{1,0:T(8,128)(2,1)S(1)}, bf16[256,1024]{1,0:T(8,128)(2,1)}, u32[]{:S(2)}) copy-start(bf16[256,1024]{1,0:T(8,128)(2,1)} %query_ref.1) | copy-start | bytes 1572868
  13.1 0.7 copy-start.1
  19.0 17.1 %collective-permute-start.7 = (bf16[256,512]{1,0:T(8,128)(2,1)S(1)}, bf16[256,512]{1,0:T(8,128)(2,1)S(1)}, u32[]{:S(2)}, u32[]{:S(2)}) collective-permute-start(bf16[256,512]{1,0:T(8,128)(2,1)S(1)} %get-tuple-element.34), channel_id=1, source_target_pairs={{0,1},{3,2},{4,5},{7,6},{8,9},{11,10},{12,13},{15,14},{16,17},{19,... | collective-permute-start | bytes 786440 | tf_op jit(solution)/shard_map/ppermute | solution.py:288
  24.2 12.0 %collective-permute-start.8 = (bf16[256,512]{1,0:T(8,128)(2,1)S(1)}, bf16[256,512]{1,0:T(8,128)(2,1)S(1)}, u32[]{:S(2)}, u32[]{:S(2)}) collective-permute-start(bf16[256,512]{1,0:T(8,128)(2,1)S(1)} %project.7), channel_id=1, source_target_pairs={{0,1},{3,2},{4,5},{7,6},{8,9},{11,10},{12,13},{15,14},{16,17},{19,... | collective-permute-start | bytes 786440 | tf_op jit(solution)/shard_map/ppermute | solution.py:288
  27.7 18.4 %collective-permute-start.9 = (bf16[256,1024]{1,0:T(8,128)(2,1)S(1)}, bf16[256,1024]{1,0:T(8,128)(2,1)S(1)}, u32[]{:S(2)}, u32[]{:S(2)}) collective-permute-start(bf16[256,1024]{1,0:T(8,128)(2,1)S(1)} %project.11), channel_id=1, source_target_pairs={{0,1},{3,2},{4,5},{7,6},{8,9},{11,10},{12,13},{15,14},{16,17},{19,... | collective-permute-start | bytes 1572872 | tf_op jit(solution)/shard_map/ppermute | solution.py:288
  31.2 26.0 %collective-permute-start.12 = (bf16[256,1024]{1,0:T(8,128)(2,1)S(1)}, bf16[256,1024]{1,0:T(8,128)(2,1)S(1)}, u32[]{:S(2)}, u32[]{:S(2)}) collective-permute-start(bf16[256,1024]{1,0:T(8,128)(2,1)S(1)} %project.12), channel_id=1, source_target_pairs={{0,1},{3,2},{4,5},{7,6},{8,9},{11,10},{12,13},{15,14},{16,17},{19,... | collective-permute-start | bytes 1572872 | tf_op jit(solution)/shard_map/ppermute | solution.py:288
  34.7 33.7 %collective-permute-start.15 = (bf16[256,1024]{1,0:T(8,128)(2,1)S(1)}, bf16[256,1024]{1,0:T(8,128)(2,1)S(1)}, u32[]{:S(2)}, u32[]{:S(2)}) collective-permute-start(bf16[256,1024]{1,0:T(8,128)(2,1)S(1)} %project.13), channel_id=1, source_target_pairs={{0,1},{3,2},{4,5},{7,6},{8,9},{11,10},{12,13},{15,14},{16,17},{19,... | collective-permute-start | bytes 1572872 | tf_op jit(solution)/shard_map/ppermute | solution.py:288
  36.2 10.1 %collective-permute-start.10 = (bf16[256,512]{1,0:T(8,128)(2,1)S(1)}, bf16[256,512]{1,0:T(8,128)(2,1)S(1)}, u32[]{:S(2)}, u32[]{:S(2)}) collective-permute-start(bf16[256,512]{1,0:T(8,128)(2,1)S(1)} %add_convert_fusion.10), channel_id=1, source_target_pairs={{1,2},{2,1},{5,6},{6,5},{9,10},{10,9},{13,14},{14,13},{17,18},{18,... | collective-permute-start | bytes 786440 | tf_op jit(solution)/shard_map/ppermute | solution.py:291
  36.9 9.5 %collective-permute-start.11 = (bf16[256,512]{1,0:T(8,128)(2,1)S(1)}, bf16[256,512]{1,0:T(8,128)(2,1)S(1)}, u32[]{:S(2)}, u32[]{:S(2)}) collective-permute-start(bf16[256,512]{1,0:T(8,128)(2,1)S(1)} %add_convert_fusion.9), channel_id=1, source_target_pairs={{1,2},{2,1},{5,6},{6,5},{9,10},{10,9},{13,14},{14,13},{17,18},{18,... | collective-permute-start | bytes 786440 | tf_op jit(solution)/shard_map/ppermute | solution.py:291
  46.5 15.2 %collective-permute-start.14 = (bf16[256,512]{1,0:T(8,128)(2,1)S(1)}, bf16[256,512]{1,0:T(8,128)(2,1)S(1)}, u32[]{:S(2)}, u32[]{:S(2)}) collective-permute-start(bf16[256,512]{1,0:T(8,128)(2,1)S(1)} %add_convert_fusion.7), channel_id=1, source_target_pairs={{1,0},{2,3},{5,4},{6,7},{9,8},{10,11},{13,12},{14,15},{17,16},{18,... | collective-permute-start | bytes 786440 | tf_op jit(solution)/shard_map/ppermute | solution.py:294
  47.8 18.1 %collective-permute-start.13 = (bf16[256,512]{1,0:T(8,128)(2,1)S(1)}, bf16[256,512]{1,0:T(8,128)(2,1)S(1)}, u32[]{:S(2)}, u32[]{:S(2)}) collective-permute-start(bf16[256,512]{1,0:T(8,128)(2,1)S(1)} %add_convert_fusion.8), channel_id=1, source_target_pairs={{1,0},{2,3},{5,4},{6,7},{9,8},{10,11},{13,12},{14,15},{17,16},{18,... | collective-permute-start | bytes 786440 | tf_op jit(solution)/shard_map/ppermute | solution.py:294
  49.1 27.4 %collective-permute-start.16 = (bf16[256,1024]{1,0:T(8,128)(2,1)S(1)}, bf16[256,1024]{1,0:T(8,128)(2,1)S(1)}, u32[]{:S(2)}, u32[]{:S(2)}) collective-permute-start(bf16[256,1024]{1,0:T(8,128)(2,1)S(1)} %add_convert_fusion.6), channel_id=1, source_target_pairs={{1,2},{2,1},{5,6},{6,5},{9,10},{10,9},{13,14},{14,13},{17,18},{18,... | collective-permute-start | bytes 1572872 | tf_op jit(solution)/shard_map/ppermute | solution.py:291
  57.4 22.3 %collective-permute-start.17 = (bf16[256,1024]{1,0:T(8,128)(2,1)S(1)}, bf16[256,1024]{1,0:T(8,128)(2,1)S(1)}, u32[]{:S(2)}, u32[]{:S(2)}) collective-permute-start(bf16[256,1024]{1,0:T(8,128)(2,1)S(1)} %add_convert_fusion.5), channel_id=1, source_target_pairs={{1,2},{2,1},{5,6},{6,5},{9,10},{10,9},{13,14},{14,13},{17,18},{18,... | collective-permute-start | bytes 1572872 | tf_op jit(solution)/shard_map/ppermute | solution.py:291
  61.7 18.0 %collective-permute-start.18 = (bf16[256,1024]{1,0:T(8,128)(2,1)S(1)}, bf16[256,1024]{1,0:T(8,128)(2,1)S(1)}, u32[]{:S(2)}, u32[]{:S(2)}) collective-permute-start(bf16[256,1024]{1,0:T(8,128)(2,1)S(1)} %project.8), channel_id=1, source_target_pairs={{0,1},{3,2},{4,5},{7,6},{8,9},{11,10},{12,13},{15,14},{16,17},{19,... | collective-permute-start | bytes 1572872 | tf_op jit(solution)/shard_map/ppermute | solution.py:288
  68.7 22.3 %collective-permute-start.20 = (bf16[256,1024]{1,0:T(8,128)(2,1)S(1)}, bf16[256,1024]{1,0:T(8,128)(2,1)S(1)}, u32[]{:S(2)}, u32[]{:S(2)}) collective-permute-start(bf16[256,1024]{1,0:T(8,128)(2,1)S(1)} %add_convert_fusion.3), channel_id=1, source_target_pairs={{1,2},{2,1},{5,6},{6,5},{9,10},{10,9},{13,14},{14,13},{17,18},{18,... | collective-permute-start | bytes 1572872 | tf_op jit(solution)/shard_map/ppermute | solution.py:291
  69.4 21.6 %collective-permute-start.21 = (bf16[256,1024]{1,0:T(8,128)(2,1)S(1)}, bf16[256,1024]{1,0:T(8,128)(2,1)S(1)}, u32[]{:S(2)}, u32[]{:S(2)}) collective-permute-start(bf16[256,1024]{1,0:T(8,128)(2,1)S(1)} %project.9), channel_id=1, source_target_pairs={{0,1},{3,2},{4,5},{7,6},{8,9},{11,10},{12,13},{15,14},{16,17},{19,... | collective-permute-start | bytes 1572872 | tf_op jit(solution)/shard_map/ppermute | solution.py:288
  76.8 15.4 %collective-permute-start.19 = (bf16[256,1024]{1,0:T(8,128)(2,1)S(1)}, bf16[256,1024]{1,0:T(8,128)(2,1)S(1)}, u32[]{:S(2)}, u32[]{:S(2)}) collective-permute-start(bf16[256,1024]{1,0:T(8,128)(2,1)S(1)} %add_convert_fusion.2), channel_id=1, source_target_pairs={{1,0},{2,3},{5,4},{6,7},{9,8},{10,11},{13,12},{14,15},{17,16},{18,... | collective-permute-start | bytes 1572872 | tf_op jit(solution)/shard_map/ppermute | solution.py:294

commit v5 on v4

--- a/solution.py
+++ b/solution.py
@@ -304,6 +304,8 @@
 
     def send_inner(at):
         to_own[at] = across(step(inner_parts[at], inner_sums[at]))
+
+    def send_direct(at):
         direct[at] = inward(after(near_parts[at], chain[-1]))
 
     def send_back(at):
@@ -319,12 +321,19 @@
     send_back(1)
     mine = part(own, quarter)
     send_inner(0)
+    send_direct(0)
     left = step(mine[:, :half], jnp.concatenate(returned[:2], axis=1))
     send_inner(1)
     send_back(2)
+    ends = (slice(0, fourth), slice(fourth, half))
+    last = [inward(after(near_parts[1], chain[-1])[:, end]) for end in ends]
     left = step(left, to_own[0], direct[0])
-    right = step(mine[:, half:], returned[2], to_own[1], direct[1])
-    return jnp.concatenate([left, right], axis=1)
+    result = jnp.concatenate([left, mine[:, half:]], axis=1)
+    for end, arrived in zip(ends, last):
+        rest = after(result, left)[:, half + end.start : half + end.stop]
+        final = added(rest, returned[2][:, end], to_own[1][:, end], arrived)
+        result = lax.dynamic_update_slice(result, final, (0, half + end.start))
+    return result
 
 
 def body(mesh, queries, keys, values, out_weight, storm_mask):

time: 94.7 us -> 95 us (level)
  the two profiles are of different devices: /device:TPU:0 before, /device:TPU:14 now
where the time goes in v5:
time: 95 us; the launch traced here: 93.1 us
  starting transfers between devices  34.3 us (36%)
  waiting for transfers between devices  27.5 us (29%)
  Pallas kernels  24.4 us (26%)
  local copies, waits for them, and re-layouts  3.81 us (4%)
  other arithmetic  2.69 us (3%)
    ppermute x5, starting transfers between devices, across(): return lax.ppermute(array, 'tp', [(1, 2), (2, 1)])  16.4 us
    pallas_call x7, Pallas kernels, project(): pl.pallas_call(project_kernel, grid_spec=pltpu.PrefetchScalarGridSpec(num...  16.4 us
    ppermute x8, waiting for transfers between devices, inward(): return lax.ppermute(array, 'tp', [(0, 1), (3, 2)])  13.7 us
    ppermute x8, starting transfers between devices, inward(): return lax.ppermute(array, 'tp', [(0, 1), (3, 2)])  10.3 us
    ppermute x5, waiting for transfers between devices, across(): return lax.ppermute(array, 'tp', [(1, 2), (2, 1)])  8.32 us
    pallas_call x2, Pallas kernels, attention_part(): pl.pallas_call(functools.partial(attention_kernel, len(parts) - len(proje...  8.03 us
    ppermute x7, waiting for transfers between devices, swap(): return lax.ppermute(array, 'ctx', [(i, i ^ bits) for i in range(devices)])  5.46 us
    ppermute x3, starting transfers between devices, outward(): return lax.ppermute(array, 'tp', [(1, 0), (2, 3)])  3.93 us
  transfers between devices with their start and end apart: 23, of which 10 were waited for; matrix products, arithmetic and copies ran while one was open for 3% of the time, Pallas kernels for 21%

profile of v5, /device:TPU:14, one launch (start us, length us, event | category | flops | bytes accessed | tf_op | source)
XLA Modules:
  0.0 93.1 jit_solution(5225618767823229219)
XLA Ops:
  0.0 0.9 constant_dynamic-slice_fusion
  0.9 0.5 collective-permute-start.1
  1.5 1.5 %collective-permute-start.2 = (bf16[1,256,256]{2,1,0:T(8,128)(2,1)S(1)}, bf16[1,256,256]{2,1,0:T(8,128)(2,1)S(1)}, u32[]{:S(2)}, u32[]{:S(2)}) collective-permute-start(bf16[1,256,256]{2,1,0:T(8,128)(2,1)S(1)} %get-tuple-element.62), channel_id=1, source_target_pairs={{0,8},{4,12},{8,0},{12,4},{16,24},{20,28},{24,16},{28,20},{1,9},{5... | collective-permute-start | bytes 393224 | tf_op jit(solution)/shard_map/ppermute | solution.py:215
  3.0 1.5 %collective-permute-start.3 = (bf16[1,256,256]{2,1,0:T(8,128)(2,1)S(1)}, bf16[1,256,256]{2,1,0:T(8,128)(2,1)S(1)}, u32[]{:S(2)}, u32[]{:S(2)}) collective-permute-start(bf16[1,256,256]{2,1,0:T(8,128)(2,1)S(1)} %get-tuple-element.62), channel_id=1, source_target_pairs={{0,16},{4,20},{8,24},{12,28},{16,0},{20,4},{24,8},{28,12},{1,17},{... | collective-permute-start | bytes 393224 | tf_op jit(solution)/shard_map/ppermute | solution.py:215
  4.5 3.8 %collective-permute-done.1.refs_3_ = bf16[1,256,256]{2,1,0:T(8,128)(2,1)S(1)} collective-permute-done((bf16[1,256,256]{2,1,0:T(8,128)(2,1)S(1)}, bf16[1,256,256]{2,1,0:T(8,128)(2,1)S(1)}, u32[]{:S(2)}, u32[]{:S(2)}) %collective-permute-start.1) | collective-permute-done | bytes 131104 | tf_op jit(solution)/shard_map/ppermute | solution.py:215
  8.3 0.0 collective-permute-start.4
  8.3 0.7 collective-permute-done.2.refs_4_
  9.0 1.0 %collective-permute-done.3.refs_5_ = bf16[1,256,256]{2,1,0:T(8,128)(2,1)S(1)} collective-permute-done((bf16[1,256,256]{2,1,0:T(8,128)(2,1)S(1)}, bf16[1,256,256]{2,1,0:T(8,128)(2,1)S(1)}, u32[]{:S(2)}, u32[]{:S(2)}) %collective-permute-start.3) | collective-permute-done | bytes 131104 | tf_op jit(solution)/shard_map/ppermute | solution.py:215
  9.9 0.0 collective-permute-start.6
  9.9 0.1 pad_add_fusion.place_ref
  10.0 0.0 collective-permute-done.refs_1_
  10.0 1.0 %copy-done = bf16[256,1024]{1,0:T(8,128)(2,1)S(1)} copy-done((bf16[256,1024]{1,0:T(8,128)(2,1)S(1)}, bf16[256,1024]{1,0:T(8,128)(2,1)}, u32[]{:S(2)}) %copy-start) | copy-done | bytes 524312
  11.1 0.7 copy-done.1
  11.7 2.8 %attend_first.1 = (bf16[256,1024]{1,0:T(8,128)(2,1)S(1)}, f32[2,8,128,128]{3,2,1,0:T(8,128)S(1)}, f32[2,8,128,128]{3,2,1,0:T(8,128)S(1)}, f32[2,8,128,128]{3,2,1,0:T(8,128)S(1)}) custom-call(s32[1]{0:T(128)} %bitcast.1.place_ref, s32[16,16]{1,0:T(8,128)S(1)} %copy-done.1, bf16[256,1024]{1,0:T(8,128)(2,1)S(1)} %copy-done, ...), custom_call_target="tpu_custom_call" | custom-call | tf_op jit(solution)/shard_map/attend_first/pallas_call | solution.py:187
  14.6 0.0 collective-permute-done.5.refs_7_
  14.6 0.0 collective-permute-done.6.refs_8_
  14.6 5.2 %attend_rest.1 = (bf16[256,1024]{1,0:T(8,128)(2,1)S(1)}, bf16[256,512]{1,0:T(8,128)(2,1)S(1)}) custom-call(s32[2]{0:T(128)S(1)} %pad_add_fusion.place_ref, s32[16,16]{1,0:T(8,128)S(1)} %copy-done.1, bf16[256,1024]{1,0:T(8,128)(2,1)S(1)} %get-tuple-element.31.query_ref, f32[2,8,128,128]{3,2,1,0:T(8,128)S(1)} %get-tuple-element.32.refs_0_, ...), custom_call_target="tpu_custom_call" | custom-call | tf_op jit(solution)/shard_map/attend_rest/pallas_call | solution.py:187
  19.8 1.3 %collective-permute-start.7 = (bf16[256,512]{1,0:T(8,128)(2,1)S(1)}, bf16[256,512]{1,0:T(8,128)(2,1)S(1)}, u32[]{:S(2)}, u32[]{:S(2)}) collective-permute-start(bf16[256,512]{1,0:T(8,128)(2,1)S(1)} %get-tuple-element.36), channel_id=1, source_target_pairs={{0,1},{3,2},{4,5},{7,6},{8,9},{11,10},{12,13},{15,14},{16,17},{19,... | collective-permute-start | bytes 786440 | tf_op jit(solution)/shard_map/ppermute | solution.py:288
  21.1 1.7 %project.7 = bf16[256,512]{1,0:T(8,128)(2,1)S(1)} custom-call(s32[1]{0:T(128)} %bitcast.6.first_ref, bf16[256,1024]{1,0:T(8,128)(2,1)S(1)} %get-tuple-element.48.attended_ref, bf16[1024,8192]{1,0:T(8,128)(2,1)} %weight_ref.13), custom_call_target="tpu_custom_call" | custom-call | tf_op jit(solution)/shard_map/project/pallas_call | solution.py:236
  22.8 1.3 %collective-permute-start.8 = (bf16[256,512]{1,0:T(8,128)(2,1)S(1)}, bf16[256,512]{1,0:T(8,128)(2,1)S(1)}, u32[]{:S(2)}, u32[]{:S(2)}) collective-permute-start(bf16[256,512]{1,0:T(8,128)(2,1)S(1)} %project.7), channel_id=1, source_target_pairs={{0,1},{3,2},{4,5},{7,6},{8,9},{11,10},{12,13},{15,14},{16,17},{19,... | collective-permute-start | bytes 786440 | tf_op jit(solution)/shard_map/ppermute | solution.py:288
  24.2 2.2 %project.11 = bf16[256,1024]{1,0:T(8,128)(2,1)S(1)} custom-call(s32[1]{0:T(128)} %bitcast.8.first_ref, bf16[256,1024]{1,0:T(8,128)(2,1)S(1)} %get-tuple-element.48.attended_ref, bf16[1024,8192]{1,0:T(8,128)(2,1)} %weight_ref.13), custom_call_target="tpu_custom_call" | custom-call | tf_op jit(solution)/shard_map/project/pallas_call | solution.py:236
  26.3 1.3 %collective-permute-start.9 = (bf16[256,1024]{1,0:T(8,128)(2,1)S(1)}, bf16[256,1024]{1,0:T(8,128)(2,1)S(1)}, u32[]{:S(2)}, u32[]{:S(2)}) collective-permute-start(bf16[256,1024]{1,0:T(8,128)(2,1)S(1)} %project.11), channel_id=1, source_target_pairs={{0,1},{3,2},{4,5},{7,6},{8,9},{11,10},{12,13},{15,14},{16,17},{19,... | collective-permute-start | bytes 1572872 | tf_op jit(solution)/shard_map/ppermute | solution.py:288
  27.6 2.2 %project.12 = bf16[256,1024]{1,0:T(8,128)(2,1)S(1)} custom-call(s32[1]{0:T(128)} %bitcast.7.first_ref, bf16[256,1024]{1,0:T(8,128)(2,1)S(1)} %get-tuple-element.48.attended_ref, bf16[1024,8192]{1,0:T(8,128)(2,1)} %weight_ref.13), custom_call_target="tpu_custom_call" | custom-call | tf_op jit(solution)/shard_map/project/pallas_call | solution.py:236
  29.8 1.3 %collective-permute-start.12 = (bf16[256,1024]{1,0:T(8,128)(2,1)S(1)}, bf16[256,1024]{1,0:T(8,128)(2,1)S(1)}, u32[]{:S(2)}, u32[]{:S(2)}) collective-permute-start(bf16[256,1024]{1,0:T(8,128)(2,1)S(1)} %project.12), channel_id=1, source_target_pairs={{0,1},{3,2},{4,5},{7,6},{8,9},{11,10},{12,13},{15,14},{16,17},{19,... | collective-permute-start | bytes 1572872 | tf_op jit(solution)/shard_map/ppermute | solution.py:288
  31.1 2.2 %project.13 = bf16[256,1024]{1,0:T(8,128)(2,1)S(1)} custom-call(s32[1]{0:T(128)} %bitcast.9.first_ref, bf16[256,1024]{1,0:T(8,128)(2,1)S(1)} %get-tuple-element.48.attended_ref, bf16[1024,8192]{1,0:T(8,128)(2,1)} %weight_ref.13), custom_call_target="tpu_custom_call" | custom-call | tf_op jit(solution)/shard_map/project/pallas_call | solution.py:236
  33.3 1.3 %collective-permute-start.15 = (bf16[256,1024]{1,0:T(8,128)(2,1)S(1)}, bf16[256,1024]{1,0:T(8,128)(2,1)S(1)}, u32[]{:S(2)}, u32[]{:S(2)}) collective-permute-start(bf16[256,1024]{1,0:T(8,128)(2,1)S(1)} %project.13), channel_id=1, source_target_pairs={{0,1},{3,2},{4,5},{7,6},{8,9},{11,10},{12,13},{15,14},{16,17},{19,... | collective-permute-start | bytes 1572872 | tf_op jit(solution)/shard_map/ppermute | solution.py:288
  34.6 0.0 collective-permute-done.7
  34.6 0.1 add_convert_fusion.11
  34.7 1.8 %collective-permute-done.8 = bf16[256,512]{1,0:T(8,128)(2,1)S(1)} collective-permute-done((bf16[256,512]{1,0:T(8,128)(2,1)S(1)}, bf16[256,512]{1,0:T(8,128)(2,1)S(1)}, u32[]{:S(2)}, u32[]{:S(2)}) %collective-permute-start.8) | collective-permute-done | bytes 262176 | tf_op jit(solution)/shard_map/ppermute | solution.py:288
  36.4 0.1 add_convert_fusion.10
  36.5 3.5 %collective-permute-start.10 = (bf16[256,512]{1,0:T(8,128)(2,1)S(1)}, bf16[256,512]{1,0:T(8,128)(2,1)S(1)}, u32[]{:S(2)}, u32[]{:S(2)}) collective-permute-start(bf16[256,512]{1,0:T(8,128)(2,1)S(1)} %add_convert_fusion.11), channel_id=1, source_target_pairs={{1,2},{2,1},{5,6},{6,5},{9,10},{10,9},{13,14},{14,13},{17,18},{18,... | collective-permute-start | bytes 786440 | tf_op jit(solution)/shard_map/ppermute | solution.py:291
  40.0 2.6 %collective-permute-start.11 = (bf16[256,512]{1,0:T(8,128)(2,1)S(1)}, bf16[256,512]{1,0:T(8,128)(2,1)S(1)}, u32[]{:S(2)}, u32[]{:S(2)}) collective-permute-start(bf16[256,512]{1,0:T(8,128)(2,1)S(1)} %add_convert_fusion.10), channel_id=1, source_target_pairs={{1,2},{2,1},{5,6},{6,5},{9,10},{10,9},{13,14},{14,13},{17,18},{18,... | collective-permute-start | bytes 786440 | tf_op jit(solution)/shard_map/ppermute | solution.py:291
  42.5 2.2 %project.8 = bf16[256,1024]{1,0:T(8,128)(2,1)S(1)} custom-call(s32[1]{0:T(128)} %bitcast.5.first_ref, bf16[256,1024]{1,0:T(8,128)(2,1)S(1)} %get-tuple-element.48.attended_ref, bf16[1024,8192]{1,0:T(8,128)(2,1)} %weight_ref.13), custom_call_target="tpu_custom_call" | custom-call | tf_op jit(solution)/shard_map/project/pallas_call | solution.py:236
  44.7 2.2 %project.9 = bf16[256,1024]{1,0:T(8,128)(2,1)S(1)} custom-call(s32[1]{0:T(128)} %bitcast.4.first_ref, bf16[256,1024]{1,0:T(8,128)(2,1)S(1)} %get-tuple-element.48.attended_ref, bf16[1024,8192]{1,0:T(8,128)(2,1)} %weight_ref.13), custom_call_target="tpu_custom_call" | custom-call | tf_op jit(solution)/shard_map/project/pallas_call | solution.py:236
  46.9 3.9 %project.10 = bf16[256,2048]{1,0:T(8,128)(2,1)S(1)} custom-call(s32[1]{0:T(128)} %bitcast.first_ref, bf16[256,1024]{1,0:T(8,128)(2,1)S(1)} %get-tuple-element.48.attended_ref, bf16[1024,8192]{1,0:T(8,128)(2,1)} %weight_ref.13), custom_call_target="tpu_custom_call" | custom-call | tf_op jit(solution)/shard_map/project/pallas_call | solution.py:236
  50.8 0.1 fusion.3
  50.9 0.2 add_convert_fusion.5
  51.1 0.1 add_convert_fusion.9
  51.2 0.4 collective-permute-done.11
  51.6 0.1 add_convert_fusion.8
  51.7 1.3 %collective-permute-start.14 = (bf16[256,512]{1,0:T(8,128)(2,1)S(1)}, bf16[256,512]{1,0:T(8,128)(2,1)S(1)}, u32[]{:S(2)}, u32[]{:S(2)}) collective-permute-start(bf16[256,512]{1,0:T(8,128)(2,1)S(1)} %add_convert_fusion.8), channel_id=1, source_target_pairs={{1,0},{2,3},{5,4},{6,7},{9,8},{10,11},{13,12},{14,15},{17,16},{18,... | collective-permute-start | bytes 786440 | tf_op jit(solution)/shard_map/ppermute | solution.py:294
  53.0 1.3 %collective-permute-start.13 = (bf16[256,512]{1,0:T(8,128)(2,1)S(1)}, bf16[256,512]{1,0:T(8,128)(2,1)S(1)}, u32[]{:S(2)}, u32[]{:S(2)}) collective-permute-start(bf16[256,512]{1,0:T(8,128)(2,1)S(1)} %add_convert_fusion.9), channel_id=1, source_target_pairs={{1,0},{2,3},{5,4},{6,7},{9,8},{10,11},{13,12},{14,15},{17,16},{18,... | collective-permute-start | bytes 786440 | tf_op jit(solution)/shard_map/ppermute | solution.py:294
  54.3 3.5 %collective-permute-start.16 = (bf16[256,1024]{1,0:T(8,128)(2,1)S(1)}, bf16[256,1024]{1,0:T(8,128)(2,1)S(1)}, u32[]{:S(2)}, u32[]{:S(2)}) collective-permute-start(bf16[256,1024]{1,0:T(8,128)(2,1)S(1)} %add_convert_fusion.5), channel_id=1, source_target_pairs={{1,2},{2,1},{5,6},{6,5},{9,10},{10,9},{13,14},{14,13},{17,18},{18,... | collective-permute-start | bytes 1572872 | tf_op jit(solution)/shard_map/ppermute | solution.py:291
  57.8 1.1 %collective-permute-done.12 = bf16[256,1024]{1,0:T(8,128)(2,1)S(1)} collective-permute-done((bf16[256,1024]{1,0:T(8,128)(2,1)S(1)}, bf16[256,1024]{1,0:T(8,128)(2,1)S(1)}, u32[]{:S(2)}, u32[]{:S(2)}) %collective-permute-start.12) | collective-permute-done | bytes 524320 | tf_op jit(solution)/shard_map/ppermute | solution.py:288
  58.9 0.2 add_convert_fusion.4
  59.1 3.5 %collective-permute-start.17 = (bf16[256,1024]{1,0:T(8,128)(2,1)S(1)}, bf16[256,1024]{1,0:T(8,128)(2,1)S(1)}, u32[]{:S(2)}, u32[]{:S(2)}) collective-permute-start(bf16[256,1024]{1,0:T(8,128)(2,1)S(1)} %add_convert_fusion.4), channel_id=1, source_target_pairs={{1,2},{2,1},{5,6},{6,5},{9,10},{10,9},{13,14},{14,13},{17,18},{18,... | collective-permute-start | bytes 1572872 | tf_op jit(solution)/shard_map/ppermute | solution.py:291
  62.6 1.3 %collective-permute-start.18 = (bf16[256,1024]{1,0:T(8,128)(2,1)S(1)}, bf16[256,1024]{1,0:T(8,128)(2,1)S(1)}, u32[]{:S(2)}, u32[]{:S(2)}) collective-permute-start(bf16[256,1024]{1,0:T(8,128)(2,1)S(1)} %project.8), channel_id=1, source_target_pairs={{0,1},{3,2},{4,5},{7,6},{8,9},{11,10},{12,13},{15,14},{16,17},{19,... | collective-permute-start | bytes 1572872 | tf_op jit(solution)/shard_map/ppermute | solution.py:288
  63.9 0.2 add_convert_fusion.3
  64.1 6.1 %collective-permute-done.15 = bf16[256,1024]{1,0:T(8,128)(2,1)S(1)} collective-permute-done((bf16[256,1024]{1,0:T(8,128)(2,1)S(1)}, bf16[256,1024]{1,0:T(8,128)(2,1)S(1)}, u32[]{:S(2)}, u32[]{:S(2)}) %collective-permute-start.15) | collective-permute-done | bytes 524320 | tf_op jit(solution)/shard_map/ppermute | solution.py:288
  70.1 0.2 add_convert_fusion.2
  70.3 3.5 %collective-permute-start.20 = (bf16[256,1024]{1,0:T(8,128)(2,1)S(1)}, bf16[256,1024]{1,0:T(8,128)(2,1)S(1)}, u32[]{:S(2)}, u32[]{:S(2)}) collective-permute-start(bf16[256,1024]{1,0:T(8,128)(2,1)S(1)} %add_convert_fusion.2), channel_id=1, source_target_pairs={{1,2},{2,1},{5,6},{6,5},{9,10},{10,9},{13,14},{14,13},{17,18},{18,... | collective-permute-start | bytes 1572872 | tf_op jit(solution)/shard_map/ppermute | solution.py:291
  73.8 0.2 add_convert_fusion.1
  74.0 1.3 %collective-permute-start.19 = (bf16[256,1024]{1,0:T(8,128)(2,1)S(1)}, bf16[256,1024]{1,0:T(8,128)(2,1)S(1)}, u32[]{:S(2)}, u32[]{:S(2)}) collective-permute-start(bf16[256,1024]{1,0:T(8,128)(2,1)S(1)} %add_convert_fusion.1), channel_id=1, source_target_pairs={{1,0},{2,3},{5,4},{6,7},{9,8},{10,11},{13,12},{14,15},{17,16},{18,... | collective-permute-start | bytes 1572872 | tf_op jit(solution)/shard_map/ppermute | solution.py:294
  75.4 1.3 %collective-permute-start.21 = (bf16[256,512]{1,0:T(8,128)(2,1)S(1)}, bf16[256,512]{1,0:T(8,128)(2,1)S(1)}, u32[]{:S(2)}, u32[]{:S(2)}) collective-permute-start(bf16[256,512]{1,0:T(8,128)(2,1)S(1)} %get-tuple-element.59), channel_id=1, source_target_pairs={{0,1},{3,2},{4,5},{7,6},{8,9},{11,10},{12,13},{15,14},{16,17},{19,... | collective-permute-start | bytes 786440 | tf_op jit(solution)/shard_map/ppermute | solution.py:288
  76.7 4.7 %collective-permute-done.18 = bf16[256,1024]{1,0:T(8,128)(2,1)S(1)} collective-permute-done((bf16[256,1024]{1,0:T(8,128)(2,1)S(1)}, bf16[256,1024]{1,0:T(8,128)(2,1)S(1)}, u32[]{:S(2)}, u32[]{:S(2)}) %collective-permute-start.18) | collective-permute-done | bytes 524320 | tf_op jit(solution)/shard_map/ppermute | solution.py:288
  81.4 1.3 %collective-permute-start.22 = (bf16[256,512]{1,0:T(8,128)(2,1)S(1)}, bf16[256,512]{1,0:T(8,128)(2,1)S(1)}, u32[]{:S(2)}, u32[]{:S(2)}) collective-permute-start(bf16[256,512]{1,0:T(8,128)(2,1)S(1)} %get-tuple-element.58), channel_id=1, source_target_pairs={{0,1},{3,2},{4,5},{7,6},{8,9},{11,10},{12,13},{15,14},{16,17},{19,... | collective-permute-start | bytes 786440 | tf_op jit(solution)/shard_map/ppermute | solution.py:288
  82.7 0.3 add_convert_fusion
  83.0 0.1 pad_maximum_fusion
  83.0 0.1 copy.6
  83.1 7.9 %collective-permute-done.20 = bf16[256,1024]{1,0:T(8,128)(2,1)S(1)} collective-permute-done((bf16[256,1024]{1,0:T(8,128)(2,1)S(1)}, bf16[256,1024]{1,0:T(8,128)(2,1)S(1)}, u32[]{:S(2)}, u32[]{:S(2)}) %collective-permute-start.20) | collective-permute-done | bytes 524320 | tf_op jit(solution)/shard_map/ppermute | solution.py:291
  91.0 0.2 fusion
  91.2 1.0 %copy.7 = bf16[256,2048]{1,0:T(8,128)(2,1)} copy(bf16[256,2048]{1,0:T(8,128)(2,1)S(1)} %fusion) | data formatting | bytes 2097152
  92.2 0.1 collective-permute-done.22
  92.3 0.9 fusion.1
  (16 shorter events, 0.1 us)
Async XLA Ops:
  0.9 7.3 %collective-permute-start.1 = (bf16[1,256,256]{2,1,0:T(8,128)(2,1)S(1)}, bf16[1,256,256]{2,1,0:T(8,128)(2,1)S(1)}, u32[]{:S(2)}, u32[]{:S(2)}) collective-permute-start(bf16[1,256,256]{2,1,0:T(8,128)(2,1)S(1)} %get-tuple-element.62), channel_id=1, source_target_pairs={{0,24},{4,28},{8,16},{12,20},{16,8},{20,12},{24,0},{28,4},{1,25},{... | collective-permute-start | bytes 393224 | tf_op jit(solution)/shard_map/ppermute | solution.py:215
  1.5 7.5 %collective-permute-start.2 = (bf16[1,256,256]{2,1,0:T(8,128)(2,1)S(1)}, bf16[1,256,256]{2,1,0:T(8,128)(2,1)S(1)}, u32[]{:S(2)}, u32[]{:S(2)}) collective-permute-start(bf16[1,256,256]{2,1,0:T(8,128)(2,1)S(1)} %get-tuple-element.62), channel_id=1, source_target_pairs={{0,8},{4,12},{8,0},{12,4},{16,24},{20,28},{24,16},{28,20},{1,9},{5... | collective-permute-start | bytes 393224 | tf_op jit(solution)/shard_map/ppermute | solution.py:215
  3.0 7.0 %collective-permute-start.3 = (bf16[1,256,256]{2,1,0:T(8,128)(2,1)S(1)}, bf16[1,256,256]{2,1,0:T(8,128)(2,1)S(1)}, u32[]{:S(2)}, u32[]{:S(2)}) collective-permute-start(bf16[1,256,256]{2,1,0:T(8,128)(2,1)S(1)} %get-tuple-element.62), channel_id=1, source_target_pairs={{0,16},{4,20},{8,24},{12,28},{16,0},{20,4},{24,8},{28,12},{1,17},{... | collective-permute-start | bytes 393224 | tf_op jit(solution)/shard_map/ppermute | solution.py:215
  4.5 5.5 %collective-permute-start = (bf16[1,256,256]{2,1,0:T(8,128)(2,1)S(1)}, bf16[1,256,256]{2,1,0:T(8,128)(2,1)S(1)}, u32[]{:S(2)}, u32[]{:S(2)}) collective-permute-start(bf16[1,256,256]{2,1,0:T(8,128)(2,1)S(1)} %get-tuple-element.62), channel_id=1, source_target_pairs={{0,4},{4,0},{8,12},{12,8},{16,20},{20,16},{24,28},{28,24},{1,5},{5... | collective-permute-start | bytes 393224 | tf_op jit(solution)/shard_map/ppermute | solution.py:215
  8.3 6.3 %collective-permute-start.4 = (bf16[1,256,256]{2,1,0:T(8,128)(2,1)S(1)}, bf16[1,256,256]{2,1,0:T(8,128)(2,1)S(1)}, u32[]{:S(2)}, u32[]{:S(2)}) collective-permute-start(bf16[1,256,256]{2,1,0:T(8,128)(2,1)S(1)} %collective-permute-done.1.refs_3_), channel_id=1, source_target_pairs={{0,4},{4,0},{8,12},{12,8},{16,20},{20,16},{24,28},{28,24},{1,5},{5... | collective-permute-start | bytes 393224 | tf_op jit(solution)/shard_map/ppermute | solution.py:215
  9.0 5.6 %collective-permute-start.5 = (bf16[1,256,256]{2,1,0:T(8,128)(2,1)S(1)}, bf16[1,256,256]{2,1,0:T(8,128)(2,1)S(1)}, u32[]{:S(2)}, u32[]{:S(2)}) collective-permute-start(bf16[1,256,256]{2,1,0:T(8,128)(2,1)S(1)} %collective-permute-done.2.refs_4_), channel_id=1, source_target_pairs={{0,4},{4,0},{8,12},{12,8},{16,20},{20,16},{24,28},{28,24},{1,5},{5... | collective-permute-start | bytes 393224 | tf_op jit(solution)/shard_map/ppermute | solution.py:215
  9.9 4.7 %collective-permute-start.6 = (bf16[1,256,256]{2,1,0:T(8,128)(2,1)S(1)}, bf16[1,256,256]{2,1,0:T(8,128)(2,1)S(1)}, u32[]{:S(2)}, u32[]{:S(2)}) collective-permute-start(bf16[1,256,256]{2,1,0:T(8,128)(2,1)S(1)} %collective-permute-done.3.refs_5_), channel_id=1, source_target_pairs={{0,4},{4,0},{8,12},{12,8},{16,20},{20,16},{24,28},{28,24},{1,5},{5... | collective-permute-start | bytes 393224 | tf_op jit(solution)/shard_map/ppermute | solution.py:215
  10.0 1.0 %copy-start = (bf16[256,1024]{1,0:T(8,128)(2,1)S(1)}, bf16[256,1024]{1,0:T(8,128)(2,1)}, u32[]{:S(2)}) copy-start(bf16[256,1024]{1,0:T(8,128)(2,1)} %query_ref.1) | copy-start | bytes 1572868
  11.1 0.7 copy-start.1
  19.8 14.7 %collective-permute-start.7 = (bf16[256,512]{1,0:T(8,128)(2,1)S(1)}, bf16[256,512]{1,0:T(8,128)(2,1)S(1)}, u32[]{:S(2)}, u32[]{:S(2)}) collective-permute-start(bf16[256,512]{1,0:T(8,128)(2,1)S(1)} %get-tuple-element.36), channel_id=1, source_target_pairs={{0,1},{3,2},{4,5},{7,6},{8,9},{11,10},{12,13},{15,14},{16,17},{19,... | collective-permute-start | bytes 786440 | tf_op jit(solution)/shard_map/ppermute | solution.py:288
  22.8 13.6 %collective-permute-start.8 = (bf16[256,512]{1,0:T(8,128)(2,1)S(1)}, bf16[256,512]{1,0:T(8,128)(2,1)S(1)}, u32[]{:S(2)}, u32[]{:S(2)}) collective-permute-start(bf16[256,512]{1,0:T(8,128)(2,1)S(1)} %project.7), channel_id=1, source_target_pairs={{0,1},{3,2},{4,5},{7,6},{8,9},{11,10},{12,13},{15,14},{16,17},{19,... | collective-permute-start | bytes 786440 | tf_op jit(solution)/shard_map/ppermute | solution.py:288
  26.3 24.6 %collective-permute-start.9 = (bf16[256,1024]{1,0:T(8,128)(2,1)S(1)}, bf16[256,1024]{1,0:T(8,128)(2,1)S(1)}, u32[]{:S(2)}, u32[]{:S(2)}) collective-permute-start(bf16[256,1024]{1,0:T(8,128)(2,1)S(1)} %project.11), channel_id=1, source_target_pairs={{0,1},{3,2},{4,5},{7,6},{8,9},{11,10},{12,13},{15,14},{16,17},{19,... | collective-permute-start | bytes 1572872 | tf_op jit(solution)/shard_map/ppermute | solution.py:288
  29.8 29.1 %collective-permute-start.12 = (bf16[256,1024]{1,0:T(8,128)(2,1)S(1)}, bf16[256,1024]{1,0:T(8,128)(2,1)S(1)}, u32[]{:S(2)}, u32[]{:S(2)}) collective-permute-start(bf16[256,1024]{1,0:T(8,128)(2,1)S(1)} %project.12), channel_id=1, source_target_pairs={{0,1},{3,2},{4,5},{7,6},{8,9},{11,10},{12,13},{15,14},{16,17},{19,... | collective-permute-start | bytes 1572872 | tf_op jit(solution)/shard_map/ppermute | solution.py:288
  33.3 36.9 %collective-permute-start.15 = (bf16[256,1024]{1,0:T(8,128)(2,1)S(1)}, bf16[256,1024]{1,0:T(8,128)(2,1)S(1)}, u32[]{:S(2)}, u32[]{:S(2)}) collective-permute-start(bf16[256,1024]{1,0:T(8,128)(2,1)S(1)} %project.13), channel_id=1, source_target_pairs={{0,1},{3,2},{4,5},{7,6},{8,9},{11,10},{12,13},{15,14},{16,17},{19,... | collective-permute-start | bytes 1572872 | tf_op jit(solution)/shard_map/ppermute | solution.py:288
  36.5 14.6 %collective-permute-start.10 = (bf16[256,512]{1,0:T(8,128)(2,1)S(1)}, bf16[256,512]{1,0:T(8,128)(2,1)S(1)}, u32[]{:S(2)}, u32[]{:S(2)}) collective-permute-start(bf16[256,512]{1,0:T(8,128)(2,1)S(1)} %add_convert_fusion.11), channel_id=1, source_target_pairs={{1,2},{2,1},{5,6},{6,5},{9,10},{10,9},{13,14},{14,13},{17,18},{18,... | collective-permute-start | bytes 786440 | tf_op jit(solution)/shard_map/ppermute | solution.py:291
  40.0 11.7 %collective-permute-start.11 = (bf16[256,512]{1,0:T(8,128)(2,1)S(1)}, bf16[256,512]{1,0:T(8,128)(2,1)S(1)}, u32[]{:S(2)}, u32[]{:S(2)}) collective-permute-start(bf16[256,512]{1,0:T(8,128)(2,1)S(1)} %add_convert_fusion.10), channel_id=1, source_target_pairs={{1,2},{2,1},{5,6},{6,5},{9,10},{10,9},{13,14},{14,13},{17,18},{18,... | collective-permute-start | bytes 786440 | tf_op jit(solution)/shard_map/ppermute | solution.py:291
  51.7 10.9 %collective-permute-start.14 = (bf16[256,512]{1,0:T(8,128)(2,1)S(1)}, bf16[256,512]{1,0:T(8,128)(2,1)S(1)}, u32[]{:S(2)}, u32[]{:S(2)}) collective-permute-start(bf16[256,512]{1,0:T(8,128)(2,1)S(1)} %add_convert_fusion.8), channel_id=1, source_target_pairs={{1,0},{2,3},{5,4},{6,7},{9,8},{10,11},{13,12},{14,15},{17,16},{18,... | collective-permute-start | bytes 786440 | tf_op jit(solution)/shard_map/ppermute | solution.py:294
  53.0 10.9 %collective-permute-start.13 = (bf16[256,512]{1,0:T(8,128)(2,1)S(1)}, bf16[256,512]{1,0:T(8,128)(2,1)S(1)}, u32[]{:S(2)}, u32[]{:S(2)}) collective-permute-start(bf16[256,512]{1,0:T(8,128)(2,1)S(1)} %add_convert_fusion.9), channel_id=1, source_target_pairs={{1,0},{2,3},{5,4},{6,7},{9,8},{10,11},{13,12},{14,15},{17,16},{18,... | collective-permute-start | bytes 786440 | tf_op jit(solution)/shard_map/ppermute | solution.py:294
  54.3 19.5 %collective-permute-start.16 = (bf16[256,1024]{1,0:T(8,128)(2,1)S(1)}, bf16[256,1024]{1,0:T(8,128)(2,1)S(1)}, u32[]{:S(2)}, u32[]{:S(2)}) collective-permute-start(bf16[256,1024]{1,0:T(8,128)(2,1)S(1)} %add_convert_fusion.5), channel_id=1, source_target_pairs={{1,2},{2,1},{5,6},{6,5},{9,10},{10,9},{13,14},{14,13},{17,18},{18,... | collective-permute-start | bytes 1572872 | tf_op jit(solution)/shard_map/ppermute | solution.py:291
  59.1 23.6 %collective-permute-start.17 = (bf16[256,1024]{1,0:T(8,128)(2,1)S(1)}, bf16[256,1024]{1,0:T(8,128)(2,1)S(1)}, u32[]{:S(2)}, u32[]{:S(2)}) collective-permute-start(bf16[256,1024]{1,0:T(8,128)(2,1)S(1)} %add_convert_fusion.4), channel_id=1, source_target_pairs={{1,2},{2,1},{5,6},{6,5},{9,10},{10,9},{13,14},{14,13},{17,18},{18,... | collective-permute-start | bytes 1572872 | tf_op jit(solution)/shard_map/ppermute | solution.py:291
  62.6 18.8 %collective-permute-start.18 = (bf16[256,1024]{1,0:T(8,128)(2,1)S(1)}, bf16[256,1024]{1,0:T(8,128)(2,1)S(1)}, u32[]{:S(2)}, u32[]{:S(2)}) collective-permute-start(bf16[256,1024]{1,0:T(8,128)(2,1)S(1)} %project.8), channel_id=1, source_target_pairs={{0,1},{3,2},{4,5},{7,6},{8,9},{11,10},{12,13},{15,14},{16,17},{19,... | collective-permute-start | bytes 1572872 | tf_op jit(solution)/shard_map/ppermute | solution.py:288
  70.3 20.7 %collective-permute-start.20 = (bf16[256,1024]{1,0:T(8,128)(2,1)S(1)}, bf16[256,1024]{1,0:T(8,128)(2,1)S(1)}, u32[]{:S(2)}, u32[]{:S(2)}) collective-permute-start(bf16[256,1024]{1,0:T(8,128)(2,1)S(1)} %add_convert_fusion.2), channel_id=1, source_target_pairs={{1,2},{2,1},{5,6},{6,5},{9,10},{10,9},{13,14},{14,13},{17,18},{18,... | collective-permute-start | bytes 1572872 | tf_op jit(solution)/shard_map/ppermute | solution.py:291
  74.0 17.0 %collective-permute-start.19 = (bf16[256,1024]{1,0:T(8,128)(2,1)S(1)}, bf16[256,1024]{1,0:T(8,128)(2,1)S(1)}, u32[]{:S(2)}, u32[]{:S(2)}) collective-permute-start(bf16[256,1024]{1,0:T(8,128)(2,1)S(1)} %add_convert_fusion.1), channel_id=1, source_target_pairs={{1,0},{2,3},{5,4},{6,7},{9,8},{10,11},{13,12},{14,15},{17,16},{18,... | collective-permute-start | bytes 1572872 | tf_op jit(solution)/shard_map/ppermute | solution.py:294
  75.4 15.6 %collective-permute-start.21 = (bf16[256,512]{1,0:T(8,128)(2,1)S(1)}, bf16[256,512]{1,0:T(8,128)(2,1)S(1)}, u32[]{:S(2)}, u32[]{:S(2)}) collective-permute-start(bf16[256,512]{1,0:T(8,128)(2,1)S(1)} %get-tuple-element.59), channel_id=1, source_target_pairs={{0,1},{3,2},{4,5},{7,6},{8,9},{11,10},{12,13},{15,14},{16,17},{19,... | collective-permute-start | bytes 786440 | tf_op jit(solution)/shard_map/ppermute | solution.py:288
  81.4 10.9 %collective-permute-start.22 = (bf16[256,512]{1,0:T(8,128)(2,1)S(1)}, bf16[256,512]{1,0:T(8,128)(2,1)S(1)}, u32[]{:S(2)}, u32[]{:S(2)}) collective-permute-start(bf16[256,512]{1,0:T(8,128)(2,1)S(1)} %get-tuple-element.58), channel_id=1, source_target_pairs={{0,1},{3,2},{4,5},{7,6},{8,9},{11,10},{12,13},{15,14},{16,17},{19,... | collective-permute-start | bytes 786440 | tf_op jit(solution)/shard_map/ppermute | solution.py:288

commit v6 on v4

--- a/solution.py
+++ b/solution.py
@@ -39,7 +39,7 @@
     return found
 
 
-def attention_kernel(parts, swaps, first, place_ref, mask_ref, query_ref, *refs):
+def attention_kernel(parts, swaps, first, chosen_rows, place_ref, mask_ref, query_ref, *refs):
     if first:
         own_hbm, *refs = refs
         kv_refs = refs[:parts]
@@ -77,7 +77,7 @@
     place = place_ref[0]
     owners = kv.shape[0]
 
-    for block in range(per_device):
+    for block in chosen_rows:
         top = slice(block * BLOCK, (block + 1) * BLOCK)
         found = choose_blocks(
             place, swaps, owners, place * per_device + block, per_device, mask_ref, chosen
@@ -147,7 +147,7 @@
         if not first:
             for head in range(heads):
                 norm = jnp.sum(totals[block, head], axis=1, keepdims=True)
-                out_ref[top, head * HDIM : (head + 1) * HDIM] = (sums[block, head] / norm).astype(
+                out_ref[:, head * HDIM : (head + 1) * HDIM] = (sums[block, head] / norm).astype(
                     jnp.bfloat16
                 )
 
@@ -158,7 +158,7 @@
         ).astype(jnp.bfloat16)
 
 
-def attention_part(first, swaps, count, place, storm_mask, query, state, parts, *projection):
+def attention_part(first, chosen_rows, swaps, count, place, storm_mask, query, state, parts, *projection):
     rows, width = query.shape
     heads = width // HDIM
     blocks = count * (rows // BLOCK)
@@ -179,13 +179,15 @@
         place = jnp.stack([place, column // columns])
         parts = [*parts, weight]
         specs = [vmem] * (3 + len(parts)) + [hbm]
-        out_shape = [taken, jax.ShapeDtypeStruct((rows, columns), jnp.bfloat16)]
+        out_shape = [
+            jax.ShapeDtypeStruct((BLOCK, wide), jnp.bfloat16) for wide in (width, columns)
+        ]
         scratch += [pltpu.VMEM(running, jnp.float32)] * 2
         scratch += [pltpu.VMEM((weight.shape[0], columns), jnp.bfloat16)]
     scratch += [pltpu.SMEM((blocks + 1,), jnp.int32)]
     scratch += [pltpu.SemaphoreType.DMA((2,)) if first else pltpu.SemaphoreType.DMA]
     return pl.pallas_call(
-        functools.partial(attention_kernel, len(parts) - len(projection[:1]), swaps, first),
+        functools.partial(attention_kernel, len(parts) - len(projection[:1]), swaps, first, chosen_rows),
         grid_spec=pltpu.PrefetchScalarGridSpec(
             num_scalar_prefetch=2,
             grid=(1,),
@@ -200,54 +202,65 @@
 
 
 def attend(queries, packed, place, devices, storm_mask, *projection):
+    every = tuple(range(queries.shape[0] // BLOCK))
     if devices != 8:
         everyone = lax.all_gather(packed, "ctx", axis=0, tiled=False)
         state = attention_part(
-            True, (), devices, place, storm_mask, queries, [packed], [everyone]
+            True, every, (), devices, place, storm_mask, queries, [packed], [everyone]
         )
         query, *state = state
         nothing = jnp.zeros_like(storm_mask)
-        return attention_part(
-            False, (), 1, place, nothing, query, state, [everyone[:1]], *projection
-        )
-
-    def swap(array, bits):
-        return lax.ppermute(array, "ctx", [(i, i ^ bits) for i in range(devices)])
-
-    near = [swap(packed[None], bits) for bits in (6, 2, 4)]
-    query, *state = attention_part(
-        True, (0, 1), 2, place, storm_mask, queries, [packed], [swap(packed[None], 1)]
-    )
-    other = [swap(array, 1) for array in near]
-    return attention_part(
-        False, (6, 2, 4, 7, 3, 5), 6, place, storm_mask, query, state, near + other, *projection
-    )
-
-
-def project_kernel(first_ref, attended_ref, weight_ref, out_ref):
-    out_ref[...] = jnp.dot(
-        attended_ref[...], weight_ref[...], preferred_element_type=jnp.float32
-    ).astype(jnp.bfloat16)
+        swaps, parts, storm_mask = (), [everyone[:1]], nothing
+    else:
+
+        def swap(array, bits):
+            return lax.ppermute(array, "ctx", [(i, i ^ bits) for i in range(devices)])
+
+        near = [swap(packed[None], bits) for bits in (6, 2, 4)]
+        query, *state = attention_part(
+            True, every, (0, 1), 2, place, storm_mask, queries, [packed], [swap(packed[None], 1)]
+        )
+        swaps, parts = (6, 2, 4, 7, 3, 5), near + [swap(array, 1) for array in near]
+    attended, partials = [], []
+    for block in every:
+        if partials:
+            query = after(query, partials[-1])
+        rows, partial = attention_part(
+            False, (block,), swaps, len(swaps) or 1, place, storm_mask, query, state, parts, *projection
+        )
+        attended.append(rows)
+        partials.append(partial)
+    return attended, partials
+
+
+def project_kernel(first_ref, *refs):
+    *attended_refs, weight_ref, out_ref = refs
+    at = 0
+    for ref in attended_refs:
+        rows = ref.shape[0]
+        out_ref[at : at + rows] = jnp.dot(
+            ref[...], weight_ref[...], preferred_element_type=jnp.float32
+        ).astype(jnp.bfloat16)
+        at += rows
 
 
 def project(attended, out_weight, first, columns):
-    rows, depth = attended.shape
+    depth = out_weight.shape[0]
+    rows = sum(array.shape[0] for array in attended)
     tile = min(TILE, columns)
     return pl.pallas_call(
         project_kernel,
         grid_spec=pltpu.PrefetchScalarGridSpec(
             num_scalar_prefetch=1,
             grid=(columns // tile,),
-            in_specs=[
-                pl.BlockSpec((rows, depth), lambda i, first: (0, 0)),
-                pl.BlockSpec((depth, tile), lambda i, first: (0, first[0] + i)),
-            ],
+            in_specs=[pl.BlockSpec(array.shape, lambda i, first: (0, 0)) for array in attended]
+            + [pl.BlockSpec((depth, tile), lambda i, first: (0, first[0] + i))],
             out_specs=pl.BlockSpec((rows, tile), lambda i, first: (0, i)),
         ),
         out_shape=jax.ShapeDtypeStruct((rows, columns), jnp.bfloat16),
         compiler_params=pltpu.CompilerParams(vmem_limit_bytes=VMEM_LIMIT),
         name="project",
-    )((first // tile).astype(jnp.int32).reshape(1), attended, out_weight)
+    )((first // tile).astype(jnp.int32).reshape(1), *attended, out_weight)
 
 
 def after(array, *earlier):
@@ -269,13 +282,13 @@
     own = place * quarter
     half = quarter // 2
     fourth = quarter // 4
-    pieces = ((0, fourth), (fourth, fourth), (half, half))
     halves = ((0, half), (half, half))
-    attended, partial = attend_now(far_outer, fourth)
-    projected, chain = [partial], []
+    attended, partials = attend_now(far_outer, half)
+    projected, chain = [partials[-1]], []
+    ahead = partials[0].shape[0]
 
     def part(first, columns):
-        source = after(attended, projected[-1]) if projected else attended
+        source = [after(attended[0], projected[-1]), *attended[1:]]
         projected.append(project(source, out_weight, first, columns))
         return projected[-1]
 
@@ -293,7 +306,7 @@
     def outward(array):
         return lax.ppermute(array, "tp", [(1, 0), (2, 3)])
 
-    outer_parts = [partial] + [part(far_outer + at, size) for at, size in pieces[1:]]
+    outer_parts = [*partials, part(far_outer + half, half)]
     outer_sums = [inward(array) for array in outer_parts]
     inner_parts = [part(far_inner + at, size) for at, size in halves]
     inner_sums = [inward(array) for array in inner_parts]
@@ -313,13 +326,13 @@
     send_outer(1)
     projected.append(chain[-1])
     near_parts = [part(near + at, size) for at, size in halves]
-    near_pieces = [near_parts[0][:, :fourth], near_parts[0][:, fourth:], near_parts[1]]
+    near_pieces = [near_parts[0][:ahead], near_parts[0][ahead:], near_parts[1]]
     send_outer(2)
     send_back(0)
     send_back(1)
     mine = part(own, quarter)
     send_inner(0)
-    left = step(mine[:, :half], jnp.concatenate(returned[:2], axis=1))
+    left = step(mine[:, :half], jnp.concatenate(returned[:2], axis=0))
     send_inner(1)
     send_back(2)
     left = step(left, to_own[0], direct[0])
@@ -340,7 +353,8 @@
 
     if mesh.shape["tp"] == 4:
         return line_sum(attend_now, out_weight)
-    _, partial = attend_now(jnp.int32(0), out_weight.shape[1])
+    _, partials = attend_now(jnp.int32(0), out_weight.shape[1])
+    partial = jnp.concatenate(partials, axis=0)
     return lax.psum_scatter(partial, "tp", scatter_dimension=1, tiled=True)
 
 

time: 94.7 us -> 94.7 us (level)
  Pallas kernels: 21.5 us -> 23.2 us
  waiting for transfers between devices: 33.7 us -> 32.5 us
    pallas_call x2 -> x3, Pallas kernels: 5.17 us -> 8.29 us  [attention_part(): pl.pallas_call(functools.partial(attention_kernel, len(parts) - len(proje...]
    ppermute x7, waiting for transfers between devices: 22.3 us -> 20.6 us  [inward(): return lax.ppermute(array, 'tp', [(0, 1), (3, 2)])]
    pallas_call x7 -> x6, Pallas kernels: 16.4 us -> 14.9 us  [project(): pl.pallas_call(project_kernel, grid_spec=pltpu.PrefetchScalarGridSpec(num...]
  transfers between devices with their start and end apart: 22 -> 22, of which waited for: 9 -> 9; matrix products, arithmetic and copies ran while one was open for 2% -> 2% of each run, Pallas kernels for 21% -> 22%
where the time goes in v6:
time: 94.7 us; the launch traced here: 93.9 us
  waiting for transfers between devices  32.5 us (34%)
  starting transfers between devices  32 us (34%)
  Pallas kernels  23.2 us (24%)
  other arithmetic  3.01 us (3%)
  local copies, waits for them, and re-layouts  2.73 us (3%)
    ppermute x7, waiting for transfers between devices, inward(): return lax.ppermute(array, 'tp', [(0, 1), (3, 2)])  20.6 us
    ppermute x7, starting transfers between devices, inward(): return lax.ppermute(array, 'tp', [(0, 1), (3, 2)])  19.4 us
    pallas_call x6, Pallas kernels, project(): pl.pallas_call(project_kernel, grid_spec=pltpu.PrefetchScalarGridSpec(num...  14.9 us
    pallas_call x3, Pallas kernels, attention_part(): pl.pallas_call(functools.partial(attention_kernel, len(parts) - len(proje...  8.29 us
    ppermute x3, waiting for transfers between devices, outward(): return lax.ppermute(array, 'tp', [(1, 0), (2, 3)])  5.96 us
    ppermute x7, waiting for transfers between devices, swap(): return lax.ppermute(array, 'ctx', [(i, i ^ bits) for i in range(devices)])  5.92 us
    ppermute x7, starting transfers between devices, swap(): return lax.ppermute(array, 'ctx', [(i, i ^ bits) for i in range(devices)])  5.12 us
    ppermute x3, starting transfers between devices, outward(): return lax.ppermute(array, 'tp', [(1, 0), (2, 3)])  3.88 us
  transfers between devices with their start and end apart: 22, of which 9 were waited for; matrix products, arithmetic and copies ran while one was open for 2% of the time, Pallas kernels for 22%

profile of v6, /device:TPU:0, one launch (start us, length us, event | category | flops | bytes accessed | tf_op | source)
XLA Modules:
  0.0 93.9 jit_solution(14128728216146854023)
XLA Ops:
  0.0 0.9 constant_dynamic-slice_fusion
  0.9 4.0 %collective-permute-start.1 = (bf16[1,256,256]{2,1,0:T(8,128)(2,1)S(1)}, bf16[1,256,256]{2,1,0:T(8,128)(2,1)S(1)}, u32[]{:S(2)}, u32[]{:S(2)}) collective-permute-start(bf16[1,256,256]{2,1,0:T(8,128)(2,1)S(1)} %get-tuple-element.61), channel_id=1, source_target_pairs={{0,24},{4,28},{8,16},{12,20},{16,8},{20,12},{24,0},{28,4},{1,25},{... | collective-permute-start | bytes 393224 | tf_op jit(solution)/shard_map/ppermute | solution.py:217
  4.9 0.5 collective-permute-start.2
  5.4 0.1 collective-permute-start.3
  5.5 0.0 collective-permute-start
  5.5 3.7 %collective-permute-done.1.refs_3_ = bf16[1,256,256]{2,1,0:T(8,128)(2,1)S(1)} collective-permute-done((bf16[1,256,256]{2,1,0:T(8,128)(2,1)S(1)}, bf16[1,256,256]{2,1,0:T(8,128)(2,1)S(1)}, u32[]{:S(2)}, u32[]{:S(2)}) %collective-permute-start.1) | collective-permute-done | bytes 131104 | tf_op jit(solution)/shard_map/ppermute | solution.py:217
  9.2 0.0 collective-permute-start.4
  9.2 2.2 %collective-permute-done.2.refs_4_ = bf16[1,256,256]{2,1,0:T(8,128)(2,1)S(1)} collective-permute-done((bf16[1,256,256]{2,1,0:T(8,128)(2,1)S(1)}, bf16[1,256,256]{2,1,0:T(8,128)(2,1)S(1)}, u32[]{:S(2)}, u32[]{:S(2)}) %collective-permute-start.2) | collective-permute-done | bytes 131104 | tf_op jit(solution)/shard_map/ppermute | solution.py:217
  11.4 0.0 collective-permute-start.5
  11.4 0.5 collective-permute-start.6
  11.9 0.1 pad_add_fusion.place_ref
  12.0 1.0 %copy-done = bf16[256,1024]{1,0:T(8,128)(2,1)S(1)} copy-done((bf16[256,1024]{1,0:T(8,128)(2,1)S(1)}, bf16[256,1024]{1,0:T(8,128)(2,1)}, u32[]{:S(2)}) %copy-start) | copy-done | bytes 524312
  13.1 0.7 copy-done.1
  13.8 2.8 %attend_first.1 = (bf16[256,1024]{1,0:T(8,128)(2,1)S(1)}, f32[2,8,128,128]{3,2,1,0:T(8,128)S(1)}, f32[2,8,128,128]{3,2,1,0:T(8,128)S(1)}, f32[2,8,128,128]{3,2,1,0:T(8,128)S(1)}) custom-call(s32[1]{0:T(128)} %bitcast.1.place_ref, s32[16,16]{1,0:T(8,128)S(1)} %copy-done.1, bf16[256,1024]{1,0:T(8,128)(2,1)S(1)} %copy-done, ...), custom_call_target="tpu_custom_call" | custom-call | tf_op jit(solution)/shard_map/attend_first/pallas_call | solution.py:189
  16.6 0.0 collective-permute-done.4.refs_6_
  16.6 0.0 collective-permute-done.6.refs_8_
  16.6 2.7 %attend_rest.2 = (bf16[128,1024]{1,0:T(8,128)(2,1)S(1)}, bf16[128,1024]{1,0:T(8,128)(2,1)S(1)}) custom-call(s32[2]{0:T(128)S(1)} %pad_add_fusion.place_ref, s32[16,16]{1,0:T(8,128)S(1)} %copy-done.1, bf16[256,1024]{1,0:T(8,128)(2,1)S(1)} %get-tuple-element.37.query_ref, f32[2,8,128,128]{3,2,1,0:T(8,128)S(1)} %get-tuple-element.32.refs_0_, ...), custom_call_target="tpu_custom_call" | custom-call | tf_op jit(solution)/shard_map/attend_rest/pallas_call | solution.py:189
  19.4 3.5 %collective-permute-start.7 = (bf16[128,1024]{1,0:T(8,128)(2,1)S(1)}, bf16[128,1024]{1,0:T(8,128)(2,1)S(1)}, u32[]{:S(2)}, u32[]{:S(2)}) collective-permute-start(bf16[128,1024]{1,0:T(8,128)(2,1)S(1)} %get-tuple-element.36), channel_id=1, source_target_pairs={{0,1},{3,2},{4,5},{7,6},{8,9},{11,10},{12,13},{15,14},{16,17},{19,... | collective-permute-start | bytes 786440 | tf_op jit(solution)/shard_map/ppermute | solution.py:301
  22.9 2.7 %attend_rest.3 = (bf16[128,1024]{1,0:T(8,128)(2,1)S(1)}, bf16[128,1024]{1,0:T(8,128)(2,1)S(1)}) custom-call(s32[2]{0:T(128)S(1)} %pad_add_fusion.place_ref, s32[16,16]{1,0:T(8,128)S(1)} %copy-done.1, bf16[256,1024]{1,0:T(8,128)(2,1)S(1)} %get-tuple-element.37.query_ref, f32[2,8,128,128]{3,2,1,0:T(8,128)S(1)} %get-tuple-element.32.refs_0_, ...), custom_call_target="tpu_custom_call" | custom-call | tf_op jit(solution)/shard_map/attend_rest/pallas_call | solution.py:189
  25.6 1.3 %collective-permute-start.8 = (bf16[128,1024]{1,0:T(8,128)(2,1)S(1)}, bf16[128,1024]{1,0:T(8,128)(2,1)S(1)}, u32[]{:S(2)}, u32[]{:S(2)}) collective-permute-start(bf16[128,1024]{1,0:T(8,128)(2,1)S(1)} %get-tuple-element.39), channel_id=1, source_target_pairs={{0,1},{3,2},{4,5},{7,6},{8,9},{11,10},{12,13},{15,14},{16,17},{19,... | collective-permute-start | bytes 786440 | tf_op jit(solution)/shard_map/ppermute | solution.py:301
  27.0 2.2 %project.9 = bf16[256,1024]{1,0:T(8,128)(2,1)S(1)} custom-call(s32[1]{0:T(128)} %bitcast.7.first_ref, bf16[128,1024]{1,0:T(8,128)(2,1)S(1)} %get-tuple-element.43.refs_0_, bf16[128,1024]{1,0:T(8,128)(2,1)S(1)} %get-tuple-element.41.refs_1_, bf16[1024,8192]{1,0:T(8,128)(2,1)} %refs_2_.11), custom_call_target="tpu_custom_call" | custom-call | tf_op jit(solution)/shard_map/project/pallas_call | solution.py:251
  29.2 1.3 %collective-permute-start.9 = (bf16[256,1024]{1,0:T(8,128)(2,1)S(1)}, bf16[256,1024]{1,0:T(8,128)(2,1)S(1)}, u32[]{:S(2)}, u32[]{:S(2)}) collective-permute-start(bf16[256,1024]{1,0:T(8,128)(2,1)S(1)} %project.9), channel_id=1, source_target_pairs={{0,1},{3,2},{4,5},{7,6},{8,9},{11,10},{12,13},{15,14},{16,17},{19,... | collective-permute-start | bytes 1572872 | tf_op jit(solution)/shard_map/ppermute | solution.py:301
  30.5 2.2 %project.10 = bf16[256,1024]{1,0:T(8,128)(2,1)S(1)} custom-call(s32[1]{0:T(128)} %bitcast.6.first_ref, bf16[128,1024]{1,0:T(8,128)(2,1)S(1)} %get-tuple-element.43.refs_0_, bf16[128,1024]{1,0:T(8,128)(2,1)S(1)} %get-tuple-element.41.refs_1_, bf16[1024,8192]{1,0:T(8,128)(2,1)} %refs_2_.11), custom_call_target="tpu_custom_call" | custom-call | tf_op jit(solution)/shard_map/project/pallas_call | solution.py:251
  32.7 1.3 %collective-permute-start.12 = (bf16[256,1024]{1,0:T(8,128)(2,1)S(1)}, bf16[256,1024]{1,0:T(8,128)(2,1)S(1)}, u32[]{:S(2)}, u32[]{:S(2)}) collective-permute-start(bf16[256,1024]{1,0:T(8,128)(2,1)S(1)} %project.10), channel_id=1, source_target_pairs={{0,1},{3,2},{4,5},{7,6},{8,9},{11,10},{12,13},{15,14},{16,17},{19,... | collective-permute-start | bytes 1572872 | tf_op jit(solution)/shard_map/ppermute | solution.py:301
  34.1 2.2 %project.11 = bf16[256,1024]{1,0:T(8,128)(2,1)S(1)} custom-call(s32[1]{0:T(128)} %bitcast.8.first_ref, bf16[128,1024]{1,0:T(8,128)(2,1)S(1)} %get-tuple-element.43.refs_0_, bf16[128,1024]{1,0:T(8,128)(2,1)S(1)} %get-tuple-element.41.refs_1_, bf16[1024,8192]{1,0:T(8,128)(2,1)} %refs_2_.11), custom_call_target="tpu_custom_call" | custom-call | tf_op jit(solution)/shard_map/project/pallas_call | solution.py:251
  36.3 1.3 %collective-permute-start.15 = (bf16[256,1024]{1,0:T(8,128)(2,1)S(1)}, bf16[256,1024]{1,0:T(8,128)(2,1)S(1)}, u32[]{:S(2)}, u32[]{:S(2)}) collective-permute-start(bf16[256,1024]{1,0:T(8,128)(2,1)S(1)} %project.11), channel_id=1, source_target_pairs={{0,1},{3,2},{4,5},{7,6},{8,9},{11,10},{12,13},{15,14},{16,17},{19,... | collective-permute-start | bytes 1572872 | tf_op jit(solution)/shard_map/ppermute | solution.py:301
  37.6 0.1 add_convert_fusion.10
  37.7 0.0 collective-permute-done.8
  37.7 0.1 add_convert_fusion.9
  37.8 0.7 collective-permute-start.10
  38.4 0.9 collective-permute-start.11
  39.3 2.2 %project.6 = bf16[256,1024]{1,0:T(8,128)(2,1)S(1)} custom-call(s32[1]{0:T(128)} %bitcast.5.first_ref, bf16[128,1024]{1,0:T(8,128)(2,1)S(1)} %get-tuple-element.43.refs_0_, bf16[128,1024]{1,0:T(8,128)(2,1)S(1)} %get-tuple-element.41.refs_1_, bf16[1024,8192]{1,0:T(8,128)(2,1)} %refs_2_.11), custom_call_target="tpu_custom_call" | custom-call | tf_op jit(solution)/shard_map/project/pallas_call | solution.py:251
  41.5 2.2 %project.7 = bf16[256,1024]{1,0:T(8,128)(2,1)S(1)} custom-call(s32[1]{0:T(128)} %bitcast.4.first_ref, bf16[128,1024]{1,0:T(8,128)(2,1)S(1)} %get-tuple-element.43.refs_0_, bf16[128,1024]{1,0:T(8,128)(2,1)S(1)} %get-tuple-element.41.refs_1_, bf16[1024,8192]{1,0:T(8,128)(2,1)} %refs_2_.11), custom_call_target="tpu_custom_call" | custom-call | tf_op jit(solution)/shard_map/project/pallas_call | solution.py:251
  43.7 4.0 %project.8 = bf16[256,2048]{1,0:T(8,128)(2,1)S(1)} custom-call(s32[1]{0:T(128)} %bitcast.first_ref, bf16[128,1024]{1,0:T(8,128)(2,1)S(1)} %get-tuple-element.43.refs_0_, bf16[128,1024]{1,0:T(8,128)(2,1)S(1)} %get-tuple-element.41.refs_1_, bf16[1024,8192]{1,0:T(8,128)(2,1)} %refs_2_.11), custom_call_target="tpu_custom_call" | custom-call | tf_op jit(solution)/shard_map/project/pallas_call | solution.py:251
  47.7 0.1 fusion.1
  47.8 0.0 collective-permute-done.9
  47.8 0.2 add_convert_fusion.6
  48.0 0.0 collective-permute-done.10
  48.0 0.1 add_convert_fusion.8
  48.1 0.1 add_convert_fusion.7
  48.2 1.3 %collective-permute-start.14 = (bf16[128,1024]{1,0:T(8,128)(2,1)S(1)}, bf16[128,1024]{1,0:T(8,128)(2,1)S(1)}, u32[]{:S(2)}, u32[]{:S(2)}) collective-permute-start(bf16[128,1024]{1,0:T(8,128)(2,1)S(1)} %add_convert_fusion.7), channel_id=1, source_target_pairs={{1,0},{2,3},{5,4},{6,7},{9,8},{10,11},{13,12},{14,15},{17,16},{18,... | collective-permute-start | bytes 786440 | tf_op jit(solution)/shard_map/ppermute | solution.py:307
  49.5 1.3 %collective-permute-start.13 = (bf16[128,1024]{1,0:T(8,128)(2,1)S(1)}, bf16[128,1024]{1,0:T(8,128)(2,1)S(1)}, u32[]{:S(2)}, u32[]{:S(2)}) collective-permute-start(bf16[128,1024]{1,0:T(8,128)(2,1)S(1)} %add_convert_fusion.8), channel_id=1, source_target_pairs={{1,0},{2,3},{5,4},{6,7},{9,8},{10,11},{13,12},{14,15},{17,16},{18,... | collective-permute-start | bytes 786440 | tf_op jit(solution)/shard_map/ppermute | solution.py:307
  50.8 0.7 collective-permute-start.16
  51.5 6.1 %collective-permute-done.12 = bf16[256,1024]{1,0:T(8,128)(2,1)S(1)} collective-permute-done((bf16[256,1024]{1,0:T(8,128)(2,1)S(1)}, bf16[256,1024]{1,0:T(8,128)(2,1)S(1)}, u32[]{:S(2)}, u32[]{:S(2)}) %collective-permute-start.12) | collective-permute-done | bytes 524320 | tf_op jit(solution)/shard_map/ppermute | solution.py:301
  57.6 0.2 add_convert_fusion.5
  57.8 0.7 collective-permute-start.17
  58.5 3.8 %collective-permute-done.14 = bf16[128,1024]{1,0:T(8,128)(2,1)S(1)} collective-permute-done((bf16[128,1024]{1,0:T(8,128)(2,1)S(1)}, bf16[128,1024]{1,0:T(8,128)(2,1)S(1)}, u32[]{:S(2)}, u32[]{:S(2)}) %collective-permute-start.14) | collective-permute-done | bytes 262176 | tf_op jit(solution)/shard_map/ppermute | solution.py:307
  62.3 3.4 %collective-permute-start.18 = (bf16[256,1024]{1,0:T(8,128)(2,1)S(1)}, bf16[256,1024]{1,0:T(8,128)(2,1)S(1)}, u32[]{:S(2)}, u32[]{:S(2)}) collective-permute-start(bf16[256,1024]{1,0:T(8,128)(2,1)S(1)} %project.6), channel_id=1, source_target_pairs={{0,1},{3,2},{4,5},{7,6},{8,9},{11,10},{12,13},{15,14},{16,17},{19,... | collective-permute-start | bytes 1572872 | tf_op jit(solution)/shard_map/ppermute | solution.py:301
  65.7 1.0 %collective-permute-done.13 = bf16[128,1024]{1,0:T(8,128)(2,1)S(1)} collective-permute-done((bf16[128,1024]{1,0:T(8,128)(2,1)S(1)}, bf16[128,1024]{1,0:T(8,128)(2,1)S(1)}, u32[]{:S(2)}, u32[]{:S(2)}) %collective-permute-start.13) | collective-permute-done | bytes 262176 | tf_op jit(solution)/shard_map/ppermute | solution.py:307
  66.7 0.2 add_convert_fusion.4
  66.9 1.9 %collective-permute-done.15 = bf16[256,1024]{1,0:T(8,128)(2,1)S(1)} collective-permute-done((bf16[256,1024]{1,0:T(8,128)(2,1)S(1)}, bf16[256,1024]{1,0:T(8,128)(2,1)S(1)}, u32[]{:S(2)}, u32[]{:S(2)}) %collective-permute-start.15) | collective-permute-done | bytes 524320 | tf_op jit(solution)/shard_map/ppermute | solution.py:301
  68.8 0.2 add_convert_fusion.3
  69.0 0.7 collective-permute-start.20
  69.7 7.2 %collective-permute-start.21 = (bf16[256,1024]{1,0:T(8,128)(2,1)S(1)}, bf16[256,1024]{1,0:T(8,128)(2,1)S(1)}, u32[]{:S(2)}, u32[]{:S(2)}) collective-permute-start(bf16[256,1024]{1,0:T(8,128)(2,1)S(1)} %project.7), channel_id=1, source_target_pairs={{0,1},{3,2},{4,5},{7,6},{8,9},{11,10},{12,13},{15,14},{16,17},{19,... | collective-permute-start | bytes 1572872 | tf_op jit(solution)/shard_map/ppermute | solution.py:301
  76.9 0.2 add_convert_fusion.2
  77.1 1.3 %collective-permute-start.19 = (bf16[256,1024]{1,0:T(8,128)(2,1)S(1)}, bf16[256,1024]{1,0:T(8,128)(2,1)S(1)}, u32[]{:S(2)}, u32[]{:S(2)}) collective-permute-start(bf16[256,1024]{1,0:T(8,128)(2,1)S(1)} %add_convert_fusion.2), channel_id=1, source_target_pairs={{1,0},{2,3},{5,4},{6,7},{9,8},{10,11},{13,12},{14,15},{17,16},{18,... | collective-permute-start | bytes 1572872 | tf_op jit(solution)/shard_map/ppermute | solution.py:307
  78.4 1.6 %collective-permute-done.18 = bf16[256,1024]{1,0:T(8,128)(2,1)S(1)} collective-permute-done((bf16[256,1024]{1,0:T(8,128)(2,1)S(1)}, bf16[256,1024]{1,0:T(8,128)(2,1)S(1)}, u32[]{:S(2)}, u32[]{:S(2)}) %collective-permute-start.18) | collective-permute-done | bytes 524320 | tf_op jit(solution)/shard_map/ppermute | solution.py:301
  80.1 0.0 collective-permute-done.17
  80.1 0.3 add_convert_fusion.1
  80.3 11.0 %collective-permute-done.21 = bf16[256,1024]{1,0:T(8,128)(2,1)S(1)} collective-permute-done((bf16[256,1024]{1,0:T(8,128)(2,1)S(1)}, bf16[256,1024]{1,0:T(8,128)(2,1)S(1)}, u32[]{:S(2)}, u32[]{:S(2)}) %collective-permute-start.21) | collective-permute-done | bytes 524320 | tf_op jit(solution)/shard_map/ppermute | solution.py:301
  91.3 0.0 collective-permute-done.20
  91.3 1.2 %collective-permute-done.19 = bf16[256,1024]{1,0:T(8,128)(2,1)S(1)} collective-permute-done((bf16[256,1024]{1,0:T(8,128)(2,1)S(1)}, bf16[256,1024]{1,0:T(8,128)(2,1)S(1)}, u32[]{:S(2)}, u32[]{:S(2)}) %collective-permute-start.19) | collective-permute-done | bytes 524320 | tf_op jit(solution)/shard_map/ppermute | solution.py:307
  92.5 0.4 add_convert_fusion
  92.9 1.1 %pad_maximum_fusion = bf16[256,2048]{1,0:T(8,128)(2,1)} fusion(bf16[256,1024]{1,0:T(8,128)(2,1)S(1)} %add_convert_fusion, bf16[256,1024]{1,0:T(8,128)(2,1)S(1)} %add_convert_fusion.1), kind=kLoop, calls=%fused_computation | loop fusion | flops 2097152 | bytes 2097152 | tf_op jit(solution)/shard_map/concatenate | solution.py:340
  (10 shorter events, 0.1 us)
Async XLA Ops:
  0.9 8.3 %collective-permute-start.1 = (bf16[1,256,256]{2,1,0:T(8,128)(2,1)S(1)}, bf16[1,256,256]{2,1,0:T(8,128)(2,1)S(1)}, u32[]{:S(2)}, u32[]{:S(2)}) collective-permute-start(bf16[1,256,256]{2,1,0:T(8,128)(2,1)S(1)} %get-tuple-element.61), channel_id=1, source_target_pairs={{0,24},{4,28},{8,16},{12,20},{16,8},{20,12},{24,0},{28,4},{1,25},{... | collective-permute-start | bytes 393224 | tf_op jit(solution)/shard_map/ppermute | solution.py:217
  4.9 6.6 %collective-permute-start.2 = (bf16[1,256,256]{2,1,0:T(8,128)(2,1)S(1)}, bf16[1,256,256]{2,1,0:T(8,128)(2,1)S(1)}, u32[]{:S(2)}, u32[]{:S(2)}) collective-permute-start(bf16[1,256,256]{2,1,0:T(8,128)(2,1)S(1)} %get-tuple-element.61), channel_id=1, source_target_pairs={{0,8},{4,12},{8,0},{12,4},{16,24},{20,28},{24,16},{28,20},{1,9},{5... | collective-permute-start | bytes 393224 | tf_op jit(solution)/shard_map/ppermute | solution.py:217
  5.4 6.0 %collective-permute-start.3 = (bf16[1,256,256]{2,1,0:T(8,128)(2,1)S(1)}, bf16[1,256,256]{2,1,0:T(8,128)(2,1)S(1)}, u32[]{:S(2)}, u32[]{:S(2)}) collective-permute-start(bf16[1,256,256]{2,1,0:T(8,128)(2,1)S(1)} %get-tuple-element.61), channel_id=1, source_target_pairs={{0,16},{4,20},{8,24},{12,28},{16,0},{20,4},{24,8},{28,12},{1,17},{... | collective-permute-start | bytes 393224 | tf_op jit(solution)/shard_map/ppermute | solution.py:217
  5.5 6.5 %collective-permute-start = (bf16[1,256,256]{2,1,0:T(8,128)(2,1)S(1)}, bf16[1,256,256]{2,1,0:T(8,128)(2,1)S(1)}, u32[]{:S(2)}, u32[]{:S(2)}) collective-permute-start(bf16[1,256,256]{2,1,0:T(8,128)(2,1)S(1)} %get-tuple-element.61), channel_id=1, source_target_pairs={{0,4},{4,0},{8,12},{12,8},{16,20},{20,16},{24,28},{28,24},{1,5},{5... | collective-permute-start | bytes 393224 | tf_op jit(solution)/shard_map/ppermute | solution.py:217
  9.2 7.4 %collective-permute-start.4 = (bf16[1,256,256]{2,1,0:T(8,128)(2,1)S(1)}, bf16[1,256,256]{2,1,0:T(8,128)(2,1)S(1)}, u32[]{:S(2)}, u32[]{:S(2)}) collective-permute-start(bf16[1,256,256]{2,1,0:T(8,128)(2,1)S(1)} %collective-permute-done.1.refs_3_), channel_id=1, source_target_pairs={{0,4},{4,0},{8,12},{12,8},{16,20},{20,16},{24,28},{28,24},{1,5},{5... | collective-permute-start | bytes 393224 | tf_op jit(solution)/shard_map/ppermute | solution.py:217
  11.4 5.2 %collective-permute-start.5 = (bf16[1,256,256]{2,1,0:T(8,128)(2,1)S(1)}, bf16[1,256,256]{2,1,0:T(8,128)(2,1)S(1)}, u32[]{:S(2)}, u32[]{:S(2)}) collective-permute-start(bf16[1,256,256]{2,1,0:T(8,128)(2,1)S(1)} %collective-permute-done.2.refs_4_), channel_id=1, source_target_pairs={{0,4},{4,0},{8,12},{12,8},{16,20},{20,16},{24,28},{28,24},{1,5},{5... | collective-permute-start | bytes 393224 | tf_op jit(solution)/shard_map/ppermute | solution.py:217
  11.4 5.2 %collective-permute-start.6 = (bf16[1,256,256]{2,1,0:T(8,128)(2,1)S(1)}, bf16[1,256,256]{2,1,0:T(8,128)(2,1)S(1)}, u32[]{:S(2)}, u32[]{:S(2)}) collective-permute-start(bf16[1,256,256]{2,1,0:T(8,128)(2,1)S(1)} %collective-permute-done.3.refs_5_), channel_id=1, source_target_pairs={{0,4},{4,0},{8,12},{12,8},{16,20},{20,16},{24,28},{28,24},{1,5},{5... | collective-permute-start | bytes 393224 | tf_op jit(solution)/shard_map/ppermute | solution.py:217
  12.0 1.0 %copy-start = (bf16[256,1024]{1,0:T(8,128)(2,1)S(1)}, bf16[256,1024]{1,0:T(8,128)(2,1)}, u32[]{:S(2)}) copy-start(bf16[256,1024]{1,0:T(8,128)(2,1)} %query_ref.1) | copy-start | bytes 1572868
  13.1 0.7 copy-start.1
  19.4 18.2 %collective-permute-start.7 = (bf16[128,1024]{1,0:T(8,128)(2,1)S(1)}, bf16[128,1024]{1,0:T(8,128)(2,1)S(1)}, u32[]{:S(2)}, u32[]{:S(2)}) collective-permute-start(bf16[128,1024]{1,0:T(8,128)(2,1)S(1)} %get-tuple-element.36), channel_id=1, source_target_pairs={{0,1},{3,2},{4,5},{7,6},{8,9},{11,10},{12,13},{15,14},{16,17},{19,... | collective-permute-start | bytes 786440 | tf_op jit(solution)/shard_map/ppermute | solution.py:301
  25.6 12.1 %collective-permute-start.8 = (bf16[128,1024]{1,0:T(8,128)(2,1)S(1)}, bf16[128,1024]{1,0:T(8,128)(2,1)S(1)}, u32[]{:S(2)}, u32[]{:S(2)}) collective-permute-start(bf16[128,1024]{1,0:T(8,128)(2,1)S(1)} %get-tuple-element.39), channel_id=1, source_target_pairs={{0,1},{3,2},{4,5},{7,6},{8,9},{11,10},{12,13},{15,14},{16,17},{19,... | collective-permute-start | bytes 786440 | tf_op jit(solution)/shard_map/ppermute | solution.py:301
  29.2 18.6 %collective-permute-start.9 = (bf16[256,1024]{1,0:T(8,128)(2,1)S(1)}, bf16[256,1024]{1,0:T(8,128)(2,1)S(1)}, u32[]{:S(2)}, u32[]{:S(2)}) collective-permute-start(bf16[256,1024]{1,0:T(8,128)(2,1)S(1)} %project.9), channel_id=1, source_target_pairs={{0,1},{3,2},{4,5},{7,6},{8,9},{11,10},{12,13},{15,14},{16,17},{19,... | collective-permute-start | bytes 1572872 | tf_op jit(solution)/shard_map/ppermute | solution.py:301
  32.7 24.9 %collective-permute-start.12 = (bf16[256,1024]{1,0:T(8,128)(2,1)S(1)}, bf16[256,1024]{1,0:T(8,128)(2,1)S(1)}, u32[]{:S(2)}, u32[]{:S(2)}) collective-permute-start(bf16[256,1024]{1,0:T(8,128)(2,1)S(1)} %project.10), channel_id=1, source_target_pairs={{0,1},{3,2},{4,5},{7,6},{8,9},{11,10},{12,13},{15,14},{16,17},{19,... | collective-permute-start | bytes 1572872 | tf_op jit(solution)/shard_map/ppermute | solution.py:301
  36.3 32.6 %collective-permute-start.15 = (bf16[256,1024]{1,0:T(8,128)(2,1)S(1)}, bf16[256,1024]{1,0:T(8,128)(2,1)S(1)}, u32[]{:S(2)}, u32[]{:S(2)}) collective-permute-start(bf16[256,1024]{1,0:T(8,128)(2,1)S(1)} %project.11), channel_id=1, source_target_pairs={{0,1},{3,2},{4,5},{7,6},{8,9},{11,10},{12,13},{15,14},{16,17},{19,... | collective-permute-start | bytes 1572872 | tf_op jit(solution)/shard_map/ppermute | solution.py:301
  37.8 10.3 %collective-permute-start.10 = (bf16[128,1024]{1,0:T(8,128)(2,1)S(1)}, bf16[128,1024]{1,0:T(8,128)(2,1)S(1)}, u32[]{:S(2)}, u32[]{:S(2)}) collective-permute-start(bf16[128,1024]{1,0:T(8,128)(2,1)S(1)} %add_convert_fusion.10), channel_id=1, source_target_pairs={{1,2},{2,1},{5,6},{6,5},{9,10},{10,9},{13,14},{14,13},{17,18},{18,... | collective-permute-start | bytes 786440 | tf_op jit(solution)/shard_map/ppermute | solution.py:304
  38.4 9.7 %collective-permute-start.11 = (bf16[128,1024]{1,0:T(8,128)(2,1)S(1)}, bf16[128,1024]{1,0:T(8,128)(2,1)S(1)}, u32[]{:S(2)}, u32[]{:S(2)}) collective-permute-start(bf16[128,1024]{1,0:T(8,128)(2,1)S(1)} %add_convert_fusion.9), channel_id=1, source_target_pairs={{1,2},{2,1},{5,6},{6,5},{9,10},{10,9},{13,14},{14,13},{17,18},{18,... | collective-permute-start | bytes 786440 | tf_op jit(solution)/shard_map/ppermute | solution.py:304
  48.2 14.1 %collective-permute-start.14 = (bf16[128,1024]{1,0:T(8,128)(2,1)S(1)}, bf16[128,1024]{1,0:T(8,128)(2,1)S(1)}, u32[]{:S(2)}, u32[]{:S(2)}) collective-permute-start(bf16[128,1024]{1,0:T(8,128)(2,1)S(1)} %add_convert_fusion.7), channel_id=1, source_target_pairs={{1,0},{2,3},{5,4},{6,7},{9,8},{10,11},{13,12},{14,15},{17,16},{18,... | collective-permute-start | bytes 786440 | tf_op jit(solution)/shard_map/ppermute | solution.py:307
  49.5 17.2 %collective-permute-start.13 = (bf16[128,1024]{1,0:T(8,128)(2,1)S(1)}, bf16[128,1024]{1,0:T(8,128)(2,1)S(1)}, u32[]{:S(2)}, u32[]{:S(2)}) collective-permute-start(bf16[128,1024]{1,0:T(8,128)(2,1)S(1)} %add_convert_fusion.8), channel_id=1, source_target_pairs={{1,0},{2,3},{5,4},{6,7},{9,8},{10,11},{13,12},{14,15},{17,16},{18,... | collective-permute-start | bytes 786440 | tf_op jit(solution)/shard_map/ppermute | solution.py:307
  50.8 26.2 %collective-permute-start.16 = (bf16[256,1024]{1,0:T(8,128)(2,1)S(1)}, bf16[256,1024]{1,0:T(8,128)(2,1)S(1)}, u32[]{:S(2)}, u32[]{:S(2)}) collective-permute-start(bf16[256,1024]{1,0:T(8,128)(2,1)S(1)} %add_convert_fusion.6), channel_id=1, source_target_pairs={{1,2},{2,1},{5,6},{6,5},{9,10},{10,9},{13,14},{14,13},{17,18},{18,... | collective-permute-start | bytes 1572872 | tf_op jit(solution)/shard_map/ppermute | solution.py:304
  57.8 22.3 %collective-permute-start.17 = (bf16[256,1024]{1,0:T(8,128)(2,1)S(1)}, bf16[256,1024]{1,0:T(8,128)(2,1)S(1)}, u32[]{:S(2)}, u32[]{:S(2)}) collective-permute-start(bf16[256,1024]{1,0:T(8,128)(2,1)S(1)} %add_convert_fusion.5), channel_id=1, source_target_pairs={{1,2},{2,1},{5,6},{6,5},{9,10},{10,9},{13,14},{14,13},{17,18},{18,... | collective-permute-start | bytes 1572872 | tf_op jit(solution)/shard_map/ppermute | solution.py:304
  62.3 17.8 %collective-permute-start.18 = (bf16[256,1024]{1,0:T(8,128)(2,1)S(1)}, bf16[256,1024]{1,0:T(8,128)(2,1)S(1)}, u32[]{:S(2)}, u32[]{:S(2)}) collective-permute-start(bf16[256,1024]{1,0:T(8,128)(2,1)S(1)} %project.6), channel_id=1, source_target_pairs={{0,1},{3,2},{4,5},{7,6},{8,9},{11,10},{12,13},{15,14},{16,17},{19,... | collective-permute-start | bytes 1572872 | tf_op jit(solution)/shard_map/ppermute | solution.py:301
  69.0 22.3 %collective-permute-start.20 = (bf16[256,1024]{1,0:T(8,128)(2,1)S(1)}, bf16[256,1024]{1,0:T(8,128)(2,1)S(1)}, u32[]{:S(2)}, u32[]{:S(2)}) collective-permute-start(bf16[256,1024]{1,0:T(8,128)(2,1)S(1)} %add_convert_fusion.3), channel_id=1, source_target_pairs={{1,2},{2,1},{5,6},{6,5},{9,10},{10,9},{13,14},{14,13},{17,18},{18,... | collective-permute-start | bytes 1572872 | tf_op jit(solution)/shard_map/ppermute | solution.py:304
  69.7 21.6 %collective-permute-start.21 = (bf16[256,1024]{1,0:T(8,128)(2,1)S(1)}, bf16[256,1024]{1,0:T(8,128)(2,1)S(1)}, u32[]{:S(2)}, u32[]{:S(2)}) collective-permute-start(bf16[256,1024]{1,0:T(8,128)(2,1)S(1)} %project.7), channel_id=1, source_target_pairs={{0,1},{3,2},{4,5},{7,6},{8,9},{11,10},{12,13},{15,14},{16,17},{19,... | collective-permute-start | bytes 1572872 | tf_op jit(solution)/shard_map/ppermute | solution.py:301
  77.1 15.4 %collective-permute-start.19 = (bf16[256,1024]{1,0:T(8,128)(2,1)S(1)}, bf16[256,1024]{1,0:T(8,128)(2,1)S(1)}, u32[]{:S(2)}, u32[]{:S(2)}) collective-permute-start(bf16[256,1024]{1,0:T(8,128)(2,1)S(1)} %add_convert_fusion.2), channel_id=1, source_target_pairs={{1,0},{2,3},{5,4},{6,7},{9,8},{10,11},{13,12},{14,15},{17,16},{18,... | collective-permute-start | bytes 1572872 | tf_op jit(solution)/shard_map/ppermute | solution.py:307

commit v7 on v6

--- a/solution.py
+++ b/solution.py
@@ -328,10 +328,10 @@
     near_parts = [part(near + at, size) for at, size in halves]
     near_pieces = [near_parts[0][:ahead], near_parts[0][ahead:], near_parts[1]]
     send_outer(2)
+    send_inner(0)
     send_back(0)
     send_back(1)
     mine = part(own, quarter)
-    send_inner(0)
     left = step(mine[:, :half], jnp.concatenate(returned[:2], axis=0))
     send_inner(1)
     send_back(2)

time: 94.7 us -> 99.7 us (1.053)
  waiting for transfers between devices: 32.5 us -> 42.6 us
  starting transfers between devices: 32 us -> 27 us
    ppermute x3, waiting for transfers between devices: 5.96 us -> 12.5 us  [outward(): return lax.ppermute(array, 'tp', [(1, 0), (2, 3)])]
    ppermute x7, starting transfers between devices: 19.4 us -> 14.3 us  [inward(): return lax.ppermute(array, 'tp', [(0, 1), (3, 2)])]
    ppermute x7, waiting for transfers between devices: 20.6 us -> 24.1 us  [inward(): return lax.ppermute(array, 'tp', [(0, 1), (3, 2)])]
  transfers between devices with their start and end apart: 22 -> 22, of which waited for: 9 -> 6; matrix products, arithmetic and copies ran while one was open for 2% -> 2% of each run, Pallas kernels for 22% -> 21%
where the time goes in v7:
time: 99.7 us; the launch traced here: 98.9 us
  waiting for transfers between devices  42.6 us (43%)
  starting transfers between devices  27 us (27%)
  Pallas kernels  23.2 us (23%)
  other arithmetic  3.02 us (3%)
  local copies, waits for them, and re-layouts  2.73 us (3%)
    ppermute x7, waiting for transfers between devices, inward(): return lax.ppermute(array, 'tp', [(0, 1), (3, 2)])  24.1 us
    pallas_call x6, Pallas kernels, project(): pl.pallas_call(project_kernel, grid_spec=pltpu.PrefetchScalarGridSpec(num...  14.9 us
    ppermute x7, starting transfers between devices, inward(): return lax.ppermute(array, 'tp', [(0, 1), (3, 2)])  14.3 us
    ppermute x3, waiting for transfers between devices, outward(): return lax.ppermute(array, 'tp', [(1, 0), (2, 3)])  12.5 us
    pallas_call x3, Pallas kernels, attention_part(): pl.pallas_call(functools.partial(attention_kernel, len(parts) - len(proje...  8.29 us
    ppermute x7, waiting for transfers between devices, swap(): return lax.ppermute(array, 'ctx', [(i, i ^ bits) for i in range(devices)])  5.92 us
    ppermute x7, starting transfers between devices, swap(): return lax.ppermute(array, 'ctx', [(i, i ^ bits) for i in range(devices)])  5.12 us
    ppermute x3, starting transfers between devices, outward(): return lax.ppermute(array, 'tp', [(1, 0), (2, 3)])  3.88 us
  transfers between devices with their start and end apart: 22, of which 6 were waited for; matrix products, arithmetic and copies ran while one was open for 2% of the time, Pallas kernels for 21%

profile of v7, /device:TPU:0, one launch (start us, length us, event | category | flops | bytes accessed | tf_op | source)
XLA Modules:
  0.0 98.9 jit_solution(13452265231761909207)
XLA Ops:
  0.0 0.9 constant_dynamic-slice_fusion
  0.9 4.0 %collective-permute-start.1 = (bf16[1,256,256]{2,1,0:T(8,128)(2,1)S(1)}, bf16[1,256,256]{2,1,0:T(8,128)(2,1)S(1)}, u32[]{:S(2)}, u32[]{:S(2)}) collective-permute-start(bf16[1,256,256]{2,1,0:T(8,128)(2,1)S(1)} %get-tuple-element.61), channel_id=1, source_target_pairs={{0,24},{4,28},{8,16},{12,20},{16,8},{20,12},{24,0},{28,4},{1,25},{... | collective-permute-start | bytes 393224 | tf_op jit(solution)/shard_map/ppermute | solution.py:217
  4.9 0.5 collective-permute-start.2
  5.4 0.1 collective-permute-start.3
  5.5 0.0 collective-permute-start
  5.5 3.7 %collective-permute-done.1.refs_3_ = bf16[1,256,256]{2,1,0:T(8,128)(2,1)S(1)} collective-permute-done((bf16[1,256,256]{2,1,0:T(8,128)(2,1)S(1)}, bf16[1,256,256]{2,1,0:T(8,128)(2,1)S(1)}, u32[]{:S(2)}, u32[]{:S(2)}) %collective-permute-start.1) | collective-permute-done | bytes 131104 | tf_op jit(solution)/shard_map/ppermute | solution.py:217
  9.2 0.0 collective-permute-start.4
  9.2 2.2 %collective-permute-done.2.refs_4_ = bf16[1,256,256]{2,1,0:T(8,128)(2,1)S(1)} collective-permute-done((bf16[1,256,256]{2,1,0:T(8,128)(2,1)S(1)}, bf16[1,256,256]{2,1,0:T(8,128)(2,1)S(1)}, u32[]{:S(2)}, u32[]{:S(2)}) %collective-permute-start.2) | collective-permute-done | bytes 131104 | tf_op jit(solution)/shard_map/ppermute | solution.py:217
  11.4 0.0 collective-permute-start.5
  11.4 0.0 collective-permute-done.3.refs_5_
  11.4 0.5 collective-permute-start.6
  11.9 0.1 pad_add_fusion.place_ref
  12.0 0.0 collective-permute-done.refs_1_
  12.0 1.0 %copy-done = bf16[256,1024]{1,0:T(8,128)(2,1)S(1)} copy-done((bf16[256,1024]{1,0:T(8,128)(2,1)S(1)}, bf16[256,1024]{1,0:T(8,128)(2,1)}, u32[]{:S(2)}) %copy-start) | copy-done | bytes 524312
  13.1 0.7 copy-done.1
  13.8 2.8 %attend_first.1 = (bf16[256,1024]{1,0:T(8,128)(2,1)S(1)}, f32[2,8,128,128]{3,2,1,0:T(8,128)S(1)}, f32[2,8,128,128]{3,2,1,0:T(8,128)S(1)}, f32[2,8,128,128]{3,2,1,0:T(8,128)S(1)}) custom-call(s32[1]{0:T(128)} %bitcast.1.place_ref, s32[16,16]{1,0:T(8,128)S(1)} %copy-done.1, bf16[256,1024]{1,0:T(8,128)(2,1)S(1)} %copy-done, ...), custom_call_target="tpu_custom_call" | custom-call | tf_op jit(solution)/shard_map/attend_first/pallas_call | solution.py:189
  16.6 0.0 collective-permute-done.6.refs_8_
  16.6 2.7 %attend_rest.2 = (bf16[128,1024]{1,0:T(8,128)(2,1)S(1)}, bf16[128,1024]{1,0:T(8,128)(2,1)S(1)}) custom-call(s32[2]{0:T(128)S(1)} %pad_add_fusion.place_ref, s32[16,16]{1,0:T(8,128)S(1)} %copy-done.1, bf16[256,1024]{1,0:T(8,128)(2,1)S(1)} %get-tuple-element.37.query_ref, f32[2,8,128,128]{3,2,1,0:T(8,128)S(1)} %get-tuple-element.32.refs_0_, ...), custom_call_target="tpu_custom_call" | custom-call | tf_op jit(solution)/shard_map/attend_rest/pallas_call | solution.py:189
  19.4 3.5 %collective-permute-start.7 = (bf16[128,1024]{1,0:T(8,128)(2,1)S(1)}, bf16[128,1024]{1,0:T(8,128)(2,1)S(1)}, u32[]{:S(2)}, u32[]{:S(2)}) collective-permute-start(bf16[128,1024]{1,0:T(8,128)(2,1)S(1)} %get-tuple-element.36), channel_id=1, source_target_pairs={{0,1},{3,2},{4,5},{7,6},{8,9},{11,10},{12,13},{15,14},{16,17},{19,... | collective-permute-start | bytes 786440 | tf_op jit(solution)/shard_map/ppermute | solution.py:301
  22.9 2.7 %attend_rest.3 = (bf16[128,1024]{1,0:T(8,128)(2,1)S(1)}, bf16[128,1024]{1,0:T(8,128)(2,1)S(1)}) custom-call(s32[2]{0:T(128)S(1)} %pad_add_fusion.place_ref, s32[16,16]{1,0:T(8,128)S(1)} %copy-done.1, bf16[256,1024]{1,0:T(8,128)(2,1)S(1)} %get-tuple-element.37.query_ref, f32[2,8,128,128]{3,2,1,0:T(8,128)S(1)} %get-tuple-element.32.refs_0_, ...), custom_call_target="tpu_custom_call" | custom-call | tf_op jit(solution)/shard_map/attend_rest/pallas_call | solution.py:189
  25.6 1.3 %collective-permute-start.8 = (bf16[128,1024]{1,0:T(8,128)(2,1)S(1)}, bf16[128,1024]{1,0:T(8,128)(2,1)S(1)}, u32[]{:S(2)}, u32[]{:S(2)}) collective-permute-start(bf16[128,1024]{1,0:T(8,128)(2,1)S(1)} %get-tuple-element.39), channel_id=1, source_target_pairs={{0,1},{3,2},{4,5},{7,6},{8,9},{11,10},{12,13},{15,14},{16,17},{19,... | collective-permute-start | bytes 786440 | tf_op jit(solution)/shard_map/ppermute | solution.py:301
  27.0 2.2 %project.9 = bf16[256,1024]{1,0:T(8,128)(2,1)S(1)} custom-call(s32[1]{0:T(128)} %bitcast.7.first_ref, bf16[128,1024]{1,0:T(8,128)(2,1)S(1)} %get-tuple-element.43.refs_0_, bf16[128,1024]{1,0:T(8,128)(2,1)S(1)} %get-tuple-element.41.refs_1_, bf16[1024,8192]{1,0:T(8,128)(2,1)} %refs_2_.11), custom_call_target="tpu_custom_call" | custom-call | tf_op jit(solution)/shard_map/project/pallas_call | solution.py:251
  29.2 1.3 %collective-permute-start.9 = (bf16[256,1024]{1,0:T(8,128)(2,1)S(1)}, bf16[256,1024]{1,0:T(8,128)(2,1)S(1)}, u32[]{:S(2)}, u32[]{:S(2)}) collective-permute-start(bf16[256,1024]{1,0:T(8,128)(2,1)S(1)} %project.9), channel_id=1, source_target_pairs={{0,1},{3,2},{4,5},{7,6},{8,9},{11,10},{12,13},{15,14},{16,17},{19,... | collective-permute-start | bytes 1572872 | tf_op jit(solution)/shard_map/ppermute | solution.py:301
  30.5 2.2 %project.10 = bf16[256,1024]{1,0:T(8,128)(2,1)S(1)} custom-call(s32[1]{0:T(128)} %bitcast.6.first_ref, bf16[128,1024]{1,0:T(8,128)(2,1)S(1)} %get-tuple-element.43.refs_0_, bf16[128,1024]{1,0:T(8,128)(2,1)S(1)} %get-tuple-element.41.refs_1_, bf16[1024,8192]{1,0:T(8,128)(2,1)} %refs_2_.11), custom_call_target="tpu_custom_call" | custom-call | tf_op jit(solution)/shard_map/project/pallas_call | solution.py:251
  32.7 1.3 %collective-permute-start.10 = (bf16[256,1024]{1,0:T(8,128)(2,1)S(1)}, bf16[256,1024]{1,0:T(8,128)(2,1)S(1)}, u32[]{:S(2)}, u32[]{:S(2)}) collective-permute-start(bf16[256,1024]{1,0:T(8,128)(2,1)S(1)} %project.10), channel_id=1, source_target_pairs={{0,1},{3,2},{4,5},{7,6},{8,9},{11,10},{12,13},{15,14},{16,17},{19,... | collective-permute-start | bytes 1572872 | tf_op jit(solution)/shard_map/ppermute | solution.py:301
  34.1 2.2 %project.11 = bf16[256,1024]{1,0:T(8,128)(2,1)S(1)} custom-call(s32[1]{0:T(128)} %bitcast.8.first_ref, bf16[128,1024]{1,0:T(8,128)(2,1)S(1)} %get-tuple-element.43.refs_0_, bf16[128,1024]{1,0:T(8,128)(2,1)S(1)} %get-tuple-element.41.refs_1_, bf16[1024,8192]{1,0:T(8,128)(2,1)} %refs_2_.11), custom_call_target="tpu_custom_call" | custom-call | tf_op jit(solution)/shard_map/project/pallas_call | solution.py:251
  36.3 1.3 %collective-permute-start.15 = (bf16[256,1024]{1,0:T(8,128)(2,1)S(1)}, bf16[256,1024]{1,0:T(8,128)(2,1)S(1)}, u32[]{:S(2)}, u32[]{:S(2)}) collective-permute-start(bf16[256,1024]{1,0:T(8,128)(2,1)S(1)} %project.11), channel_id=1, source_target_pairs={{0,1},{3,2},{4,5},{7,6},{8,9},{11,10},{12,13},{15,14},{16,17},{19,... | collective-permute-start | bytes 1572872 | tf_op jit(solution)/shard_map/ppermute | solution.py:301
  37.6 0.0 collective-permute-done.7
  37.6 0.1 add_convert_fusion.10
  37.7 0.0 collective-permute-done.8
  37.7 0.1 add_convert_fusion.9
  37.8 0.7 collective-permute-start.11
  38.4 0.9 collective-permute-start.12
  39.3 2.2 %project.6 = bf16[256,1024]{1,0:T(8,128)(2,1)S(1)} custom-call(s32[1]{0:T(128)} %bitcast.5.first_ref, bf16[128,1024]{1,0:T(8,128)(2,1)S(1)} %get-tuple-element.43.refs_0_, bf16[128,1024]{1,0:T(8,128)(2,1)S(1)} %get-tuple-element.41.refs_1_, bf16[1024,8192]{1,0:T(8,128)(2,1)} %refs_2_.11), custom_call_target="tpu_custom_call" | custom-call | tf_op jit(solution)/shard_map/project/pallas_call | solution.py:251
  41.5 2.2 %project.7 = bf16[256,1024]{1,0:T(8,128)(2,1)S(1)} custom-call(s32[1]{0:T(128)} %bitcast.4.first_ref, bf16[128,1024]{1,0:T(8,128)(2,1)S(1)} %get-tuple-element.43.refs_0_, bf16[128,1024]{1,0:T(8,128)(2,1)S(1)} %get-tuple-element.41.refs_1_, bf16[1024,8192]{1,0:T(8,128)(2,1)} %refs_2_.11), custom_call_target="tpu_custom_call" | custom-call | tf_op jit(solution)/shard_map/project/pallas_call | solution.py:251
  43.7 4.0 %project.8 = bf16[256,2048]{1,0:T(8,128)(2,1)S(1)} custom-call(s32[1]{0:T(128)} %bitcast.first_ref, bf16[128,1024]{1,0:T(8,128)(2,1)S(1)} %get-tuple-element.43.refs_0_, bf16[128,1024]{1,0:T(8,128)(2,1)S(1)} %get-tuple-element.41.refs_1_, bf16[1024,8192]{1,0:T(8,128)(2,1)} %refs_2_.11), custom_call_target="tpu_custom_call" | custom-call | tf_op jit(solution)/shard_map/project/pallas_call | solution.py:251
  47.7 0.0 collective-permute-done.9
  47.7 0.2 add_convert_fusion.6
  47.9 0.7 collective-permute-start.16
  48.6 9.0 %collective-permute-done.10 = bf16[256,1024]{1,0:T(8,128)(2,1)S(1)} collective-permute-done((bf16[256,1024]{1,0:T(8,128)(2,1)S(1)}, bf16[256,1024]{1,0:T(8,128)(2,1)S(1)}, u32[]{:S(2)}, u32[]{:S(2)}) %collective-permute-start.10) | collective-permute-done | bytes 524320 | tf_op jit(solution)/shard_map/ppermute | solution.py:301
  57.6 0.2 add_convert_fusion.5
  57.8 0.1 add_convert_fusion.8
  57.9 1.3 %collective-permute-start.13 = (bf16[128,1024]{1,0:T(8,128)(2,1)S(1)}, bf16[128,1024]{1,0:T(8,128)(2,1)S(1)}, u32[]{:S(2)}, u32[]{:S(2)}) collective-permute-start(bf16[128,1024]{1,0:T(8,128)(2,1)S(1)} %add_convert_fusion.8), channel_id=1, source_target_pairs={{1,0},{2,3},{5,4},{6,7},{9,8},{10,11},{13,12},{14,15},{17,16},{18,... | collective-permute-start | bytes 786440 | tf_op jit(solution)/shard_map/ppermute | solution.py:307
  59.2 0.0 collective-permute-done.12
  59.2 0.1 add_convert_fusion.7
  59.3 1.3 %collective-permute-start.14 = (bf16[128,1024]{1,0:T(8,128)(2,1)S(1)}, bf16[128,1024]{1,0:T(8,128)(2,1)S(1)}, u32[]{:S(2)}, u32[]{:S(2)}) collective-permute-start(bf16[128,1024]{1,0:T(8,128)(2,1)S(1)} %add_convert_fusion.7), channel_id=1, source_target_pairs={{1,0},{2,3},{5,4},{6,7},{9,8},{10,11},{13,12},{14,15},{17,16},{18,... | collective-permute-start | bytes 786440 | tf_op jit(solution)/shard_map/ppermute | solution.py:307
  60.6 0.1 fusion.1
  60.7 0.7 collective-permute-start.17
  61.4 12.5 %collective-permute-done.14 = bf16[128,1024]{1,0:T(8,128)(2,1)S(1)} collective-permute-done((bf16[128,1024]{1,0:T(8,128)(2,1)S(1)}, bf16[128,1024]{1,0:T(8,128)(2,1)S(1)}, u32[]{:S(2)}, u32[]{:S(2)}) %collective-permute-start.14) | collective-permute-done | bytes 262176 | tf_op jit(solution)/shard_map/ppermute | solution.py:307
  73.9 1.5 %collective-permute-start.18 = (bf16[256,1024]{1,0:T(8,128)(2,1)S(1)}, bf16[256,1024]{1,0:T(8,128)(2,1)S(1)}, u32[]{:S(2)}, u32[]{:S(2)}) collective-permute-start(bf16[256,1024]{1,0:T(8,128)(2,1)S(1)} %project.6), channel_id=1, source_target_pairs={{0,1},{3,2},{4,5},{7,6},{8,9},{11,10},{12,13},{15,14},{16,17},{19,... | collective-permute-start | bytes 1572872 | tf_op jit(solution)/shard_map/ppermute | solution.py:301
  75.4 0.0 collective-permute-done.13
  75.4 0.2 add_convert_fusion.4
  75.6 0.0 collective-permute-done.15
  75.6 0.2 add_convert_fusion.3
  75.8 0.7 collective-permute-start.20
  76.5 4.1 %collective-permute-start.21 = (bf16[256,1024]{1,0:T(8,128)(2,1)S(1)}, bf16[256,1024]{1,0:T(8,128)(2,1)S(1)}, u32[]{:S(2)}, u32[]{:S(2)}) collective-permute-start(bf16[256,1024]{1,0:T(8,128)(2,1)S(1)} %project.7), channel_id=1, source_target_pairs={{0,1},{3,2},{4,5},{7,6},{8,9},{11,10},{12,13},{15,14},{16,17},{19,... | collective-permute-start | bytes 1572872 | tf_op jit(solution)/shard_map/ppermute | solution.py:301
  80.6 0.2 add_convert_fusion.2
  80.8 1.3 %collective-permute-start.19 = (bf16[256,1024]{1,0:T(8,128)(2,1)S(1)}, bf16[256,1024]{1,0:T(8,128)(2,1)S(1)}, u32[]{:S(2)}, u32[]{:S(2)}) collective-permute-start(bf16[256,1024]{1,0:T(8,128)(2,1)S(1)} %add_convert_fusion.2), channel_id=1, source_target_pairs={{1,0},{2,3},{5,4},{6,7},{9,8},{10,11},{13,12},{14,15},{17,16},{18,... | collective-permute-start | bytes 1572872 | tf_op jit(solution)/shard_map/ppermute | solution.py:307
  82.1 5.6 %collective-permute-done.18 = bf16[256,1024]{1,0:T(8,128)(2,1)S(1)} collective-permute-done((bf16[256,1024]{1,0:T(8,128)(2,1)S(1)}, bf16[256,1024]{1,0:T(8,128)(2,1)S(1)}, u32[]{:S(2)}, u32[]{:S(2)}) %collective-permute-start.18) | collective-permute-done | bytes 524320 | tf_op jit(solution)/shard_map/ppermute | solution.py:301
  87.7 0.0 collective-permute-done.17
  87.7 0.3 add_convert_fusion.1
  88.0 9.5 %collective-permute-done.21 = bf16[256,1024]{1,0:T(8,128)(2,1)S(1)} collective-permute-done((bf16[256,1024]{1,0:T(8,128)(2,1)S(1)}, bf16[256,1024]{1,0:T(8,128)(2,1)S(1)}, u32[]{:S(2)}, u32[]{:S(2)}) %collective-permute-start.21) | collective-permute-done | bytes 524320 | tf_op jit(solution)/shard_map/ppermute | solution.py:301
  97.5 0.4 add_convert_fusion
  97.9 1.1 %pad_maximum_fusion = bf16[256,2048]{1,0:T(8,128)(2,1)} fusion(bf16[256,1024]{1,0:T(8,128)(2,1)S(1)} %add_convert_fusion, bf16[256,1024]{1,0:T(8,128)(2,1)S(1)} %add_convert_fusion.1), kind=kLoop, calls=%fused_computation | loop fusion | flops 2097152 | bytes 2097152 | tf_op jit(solution)/shard_map/concatenate | solution.py:340
  (10 shorter events, 0.1 us)
Async XLA Ops:
  0.9 8.3 %collective-permute-start.1 = (bf16[1,256,256]{2,1,0:T(8,128)(2,1)S(1)}, bf16[1,256,256]{2,1,0:T(8,128)(2,1)S(1)}, u32[]{:S(2)}, u32[]{:S(2)}) collective-permute-start(bf16[1,256,256]{2,1,0:T(8,128)(2,1)S(1)} %get-tuple-element.61), channel_id=1, source_target_pairs={{0,24},{4,28},{8,16},{12,20},{16,8},{20,12},{24,0},{28,4},{1,25},{... | collective-permute-start | bytes 393224 | tf_op jit(solution)/shard_map/ppermute | solution.py:217
  4.9 6.6 %collective-permute-start.2 = (bf16[1,256,256]{2,1,0:T(8,128)(2,1)S(1)}, bf16[1,256,256]{2,1,0:T(8,128)(2,1)S(1)}, u32[]{:S(2)}, u32[]{:S(2)}) collective-permute-start(bf16[1,256,256]{2,1,0:T(8,128)(2,1)S(1)} %get-tuple-element.61), channel_id=1, source_target_pairs={{0,8},{4,12},{8,0},{12,4},{16,24},{20,28},{24,16},{28,20},{1,9},{5... | collective-permute-start | bytes 393224 | tf_op jit(solution)/shard_map/ppermute | solution.py:217
  5.4 6.0 %collective-permute-start.3 = (bf16[1,256,256]{2,1,0:T(8,128)(2,1)S(1)}, bf16[1,256,256]{2,1,0:T(8,128)(2,1)S(1)}, u32[]{:S(2)}, u32[]{:S(2)}) collective-permute-start(bf16[1,256,256]{2,1,0:T(8,128)(2,1)S(1)} %get-tuple-element.61), channel_id=1, source_target_pairs={{0,16},{4,20},{8,24},{12,28},{16,0},{20,4},{24,8},{28,12},{1,17},{... | collective-permute-start | bytes 393224 | tf_op jit(solution)/shard_map/ppermute | solution.py:217
  5.5 6.5 %collective-permute-start = (bf16[1,256,256]{2,1,0:T(8,128)(2,1)S(1)}, bf16[1,256,256]{2,1,0:T(8,128)(2,1)S(1)}, u32[]{:S(2)}, u32[]{:S(2)}) collective-permute-start(bf16[1,256,256]{2,1,0:T(8,128)(2,1)S(1)} %get-tuple-element.61), channel_id=1, source_target_pairs={{0,4},{4,0},{8,12},{12,8},{16,20},{20,16},{24,28},{28,24},{1,5},{5... | collective-permute-start | bytes 393224 | tf_op jit(solution)/shard_map/ppermute | solution.py:217
  9.2 7.4 %collective-permute-start.4 = (bf16[1,256,256]{2,1,0:T(8,128)(2,1)S(1)}, bf16[1,256,256]{2,1,0:T(8,128)(2,1)S(1)}, u32[]{:S(2)}, u32[]{:S(2)}) collective-permute-start(bf16[1,256,256]{2,1,0:T(8,128)(2,1)S(1)} %collective-permute-done.1.refs_3_), channel_id=1, source_target_pairs={{0,4},{4,0},{8,12},{12,8},{16,20},{20,16},{24,28},{28,24},{1,5},{5... | collective-permute-start | bytes 393224 | tf_op jit(solution)/shard_map/ppermute | solution.py:217
  11.4 5.2 %collective-permute-start.5 = (bf16[1,256,256]{2,1,0:T(8,128)(2,1)S(1)}, bf16[1,256,256]{2,1,0:T(8,128)(2,1)S(1)}, u32[]{:S(2)}, u32[]{:S(2)}) collective-permute-start(bf16[1,256,256]{2,1,0:T(8,128)(2,1)S(1)} %collective-permute-done.2.refs_4_), channel_id=1, source_target_pairs={{0,4},{4,0},{8,12},{12,8},{16,20},{20,16},{24,28},{28,24},{1,5},{5... | collective-permute-start | bytes 393224 | tf_op jit(solution)/shard_map/ppermute | solution.py:217
  11.4 5.2 %collective-permute-start.6 = (bf16[1,256,256]{2,1,0:T(8,128)(2,1)S(1)}, bf16[1,256,256]{2,1,0:T(8,128)(2,1)S(1)}, u32[]{:S(2)}, u32[]{:S(2)}) collective-permute-start(bf16[1,256,256]{2,1,0:T(8,128)(2,1)S(1)} %collective-permute-done.3.refs_5_), channel_id=1, source_target_pairs={{0,4},{4,0},{8,12},{12,8},{16,20},{20,16},{24,28},{28,24},{1,5},{5... | collective-permute-start | bytes 393224 | tf_op jit(solution)/shard_map/ppermute | solution.py:217
  12.0 1.0 %copy-start = (bf16[256,1024]{1,0:T(8,128)(2,1)S(1)}, bf16[256,1024]{1,0:T(8,128)(2,1)}, u32[]{:S(2)}) copy-start(bf16[256,1024]{1,0:T(8,128)(2,1)} %query_ref.1) | copy-start | bytes 1572868
  13.1 0.7 copy-start.1
  19.4 18.2 %collective-permute-start.7 = (bf16[128,1024]{1,0:T(8,128)(2,1)S(1)}, bf16[128,1024]{1,0:T(8,128)(2,1)S(1)}, u32[]{:S(2)}, u32[]{:S(2)}) collective-permute-start(bf16[128,1024]{1,0:T(8,128)(2,1)S(1)} %get-tuple-element.36), channel_id=1, source_target_pairs={{0,1},{3,2},{4,5},{7,6},{8,9},{11,10},{12,13},{15,14},{16,17},{19,... | collective-permute-start | bytes 786440 | tf_op jit(solution)/shard_map/ppermute | solution.py:301
  25.6 12.1 %collective-permute-start.8 = (bf16[128,1024]{1,0:T(8,128)(2,1)S(1)}, bf16[128,1024]{1,0:T(8,128)(2,1)S(1)}, u32[]{:S(2)}, u32[]{:S(2)}) collective-permute-start(bf16[128,1024]{1,0:T(8,128)(2,1)S(1)} %get-tuple-element.39), channel_id=1, source_target_pairs={{0,1},{3,2},{4,5},{7,6},{8,9},{11,10},{12,13},{15,14},{16,17},{19,... | collective-permute-start | bytes 786440 | tf_op jit(solution)/shard_map/ppermute | solution.py:301
  29.2 18.5 %collective-permute-start.9 = (bf16[256,1024]{1,0:T(8,128)(2,1)S(1)}, bf16[256,1024]{1,0:T(8,128)(2,1)S(1)}, u32[]{:S(2)}, u32[]{:S(2)}) collective-permute-start(bf16[256,1024]{1,0:T(8,128)(2,1)S(1)} %project.9), channel_id=1, source_target_pairs={{0,1},{3,2},{4,5},{7,6},{8,9},{11,10},{12,13},{15,14},{16,17},{19,... | collective-permute-start | bytes 1572872 | tf_op jit(solution)/shard_map/ppermute | solution.py:301
  32.7 24.9 %collective-permute-start.10 = (bf16[256,1024]{1,0:T(8,128)(2,1)S(1)}, bf16[256,1024]{1,0:T(8,128)(2,1)S(1)}, u32[]{:S(2)}, u32[]{:S(2)}) collective-permute-start(bf16[256,1024]{1,0:T(8,128)(2,1)S(1)} %project.10), channel_id=1, source_target_pairs={{0,1},{3,2},{4,5},{7,6},{8,9},{11,10},{12,13},{15,14},{16,17},{19,... | collective-permute-start | bytes 1572872 | tf_op jit(solution)/shard_map/ppermute | solution.py:301
  36.3 39.3 %collective-permute-start.15 = (bf16[256,1024]{1,0:T(8,128)(2,1)S(1)}, bf16[256,1024]{1,0:T(8,128)(2,1)S(1)}, u32[]{:S(2)}, u32[]{:S(2)}) collective-permute-start(bf16[256,1024]{1,0:T(8,128)(2,1)S(1)} %project.11), channel_id=1, source_target_pairs={{0,1},{3,2},{4,5},{7,6},{8,9},{11,10},{12,13},{15,14},{16,17},{19,... | collective-permute-start | bytes 1572872 | tf_op jit(solution)/shard_map/ppermute | solution.py:301
  37.8 20.0 %collective-permute-start.11 = (bf16[128,1024]{1,0:T(8,128)(2,1)S(1)}, bf16[128,1024]{1,0:T(8,128)(2,1)S(1)}, u32[]{:S(2)}, u32[]{:S(2)}) collective-permute-start(bf16[128,1024]{1,0:T(8,128)(2,1)S(1)} %add_convert_fusion.10), channel_id=1, source_target_pairs={{1,2},{2,1},{5,6},{6,5},{9,10},{10,9},{13,14},{14,13},{17,18},{18,... | collective-permute-start | bytes 786440 | tf_op jit(solution)/shard_map/ppermute | solution.py:304
  38.4 20.7 %collective-permute-start.12 = (bf16[128,1024]{1,0:T(8,128)(2,1)S(1)}, bf16[128,1024]{1,0:T(8,128)(2,1)S(1)}, u32[]{:S(2)}, u32[]{:S(2)}) collective-permute-start(bf16[128,1024]{1,0:T(8,128)(2,1)S(1)} %add_convert_fusion.9), channel_id=1, source_target_pairs={{1,2},{2,1},{5,6},{6,5},{9,10},{10,9},{13,14},{14,13},{17,18},{18,... | collective-permute-start | bytes 786440 | tf_op jit(solution)/shard_map/ppermute | solution.py:304
  47.9 32.7 %collective-permute-start.16 = (bf16[256,1024]{1,0:T(8,128)(2,1)S(1)}, bf16[256,1024]{1,0:T(8,128)(2,1)S(1)}, u32[]{:S(2)}, u32[]{:S(2)}) collective-permute-start(bf16[256,1024]{1,0:T(8,128)(2,1)S(1)} %add_convert_fusion.6), channel_id=1, source_target_pairs={{1,2},{2,1},{5,6},{6,5},{9,10},{10,9},{13,14},{14,13},{17,18},{18,... | collective-permute-start | bytes 1572872 | tf_op jit(solution)/shard_map/ppermute | solution.py:304
  57.9 17.5 %collective-permute-start.13 = (bf16[128,1024]{1,0:T(8,128)(2,1)S(1)}, bf16[128,1024]{1,0:T(8,128)(2,1)S(1)}, u32[]{:S(2)}, u32[]{:S(2)}) collective-permute-start(bf16[128,1024]{1,0:T(8,128)(2,1)S(1)} %add_convert_fusion.8), channel_id=1, source_target_pairs={{1,0},{2,3},{5,4},{6,7},{9,8},{10,11},{13,12},{14,15},{17,16},{18,... | collective-permute-start | bytes 786440 | tf_op jit(solution)/shard_map/ppermute | solution.py:307
  59.3 14.6 %collective-permute-start.14 = (bf16[128,1024]{1,0:T(8,128)(2,1)S(1)}, bf16[128,1024]{1,0:T(8,128)(2,1)S(1)}, u32[]{:S(2)}, u32[]{:S(2)}) collective-permute-start(bf16[128,1024]{1,0:T(8,128)(2,1)S(1)} %add_convert_fusion.7), channel_id=1, source_target_pairs={{1,0},{2,3},{5,4},{6,7},{9,8},{10,11},{13,12},{14,15},{17,16},{18,... | collective-permute-start | bytes 786440 | tf_op jit(solution)/shard_map/ppermute | solution.py:307
  60.7 27.0 %collective-permute-start.17 = (bf16[256,1024]{1,0:T(8,128)(2,1)S(1)}, bf16[256,1024]{1,0:T(8,128)(2,1)S(1)}, u32[]{:S(2)}, u32[]{:S(2)}) collective-permute-start(bf16[256,1024]{1,0:T(8,128)(2,1)S(1)} %add_convert_fusion.5), channel_id=1, source_target_pairs={{1,2},{2,1},{5,6},{6,5},{9,10},{10,9},{13,14},{14,13},{17,18},{18,... | collective-permute-start | bytes 1572872 | tf_op jit(solution)/shard_map/ppermute | solution.py:304
  73.9 13.8 %collective-permute-start.18 = (bf16[256,1024]{1,0:T(8,128)(2,1)S(1)}, bf16[256,1024]{1,0:T(8,128)(2,1)S(1)}, u32[]{:S(2)}, u32[]{:S(2)}) collective-permute-start(bf16[256,1024]{1,0:T(8,128)(2,1)S(1)} %project.6), channel_id=1, source_target_pairs={{0,1},{3,2},{4,5},{7,6},{8,9},{11,10},{12,13},{15,14},{16,17},{19,... | collective-permute-start | bytes 1572872 | tf_op jit(solution)/shard_map/ppermute | solution.py:301
  75.8 21.7 %collective-permute-start.20 = (bf16[256,1024]{1,0:T(8,128)(2,1)S(1)}, bf16[256,1024]{1,0:T(8,128)(2,1)S(1)}, u32[]{:S(2)}, u32[]{:S(2)}) collective-permute-start(bf16[256,1024]{1,0:T(8,128)(2,1)S(1)} %add_convert_fusion.3), channel_id=1, source_target_pairs={{1,2},{2,1},{5,6},{6,5},{9,10},{10,9},{13,14},{14,13},{17,18},{18,... | collective-permute-start | bytes 1572872 | tf_op jit(solution)/shard_map/ppermute | solution.py:304
  76.5 21.0 %collective-permute-start.21 = (bf16[256,1024]{1,0:T(8,128)(2,1)S(1)}, bf16[256,1024]{1,0:T(8,128)(2,1)S(1)}, u32[]{:S(2)}, u32[]{:S(2)}) collective-permute-start(bf16[256,1024]{1,0:T(8,128)(2,1)S(1)} %project.7), channel_id=1, source_target_pairs={{0,1},{3,2},{4,5},{7,6},{8,9},{11,10},{12,13},{15,14},{16,17},{19,... | collective-permute-start | bytes 1572872 | tf_op jit(solution)/shard_map/ppermute | solution.py:301
  80.8 16.7 %collective-permute-start.19 = (bf16[256,1024]{1,0:T(8,128)(2,1)S(1)}, bf16[256,1024]{1,0:T(8,128)(2,1)S(1)}, u32[]{:S(2)}, u32[]{:S(2)}) collective-permute-start(bf16[256,1024]{1,0:T(8,128)(2,1)S(1)} %add_convert_fusion.2), channel_id=1, source_target_pairs={{1,0},{2,3},{5,4},{6,7},{9,8},{10,11},{13,12},{14,15},{17,16},{18,... | collective-permute-start | bytes 1572872 | tf_op jit(solution)/shard_map/ppermute | solution.py:307
